TPU v7x, 32 devices: a whole 2x2x4 slice. The times are simulated.
32 devices in a mesh: cell: 2 (over y), seq: 4 (over z), tensor: 4 (over x, core).
Axes of the slice: x: 2, y: 2, z: 4, core: 2. Of those that a mesh axis runs over, the one named last changes fastest.
Arguments:
- tokens: bfloat16 [4, 2048, 1120], P('cell', 'seq'), may hold values from -6 to 6
- out_grad: bfloat16 [4, 2048, 1120], P('cell', 'seq'), may hold values from -6 to 6
- group_order: int32 [4, 8], P('cell'), may hold values from 0 to 7, as said below
- lengths: int32 [4], P('cell'), may hold values from 1024 to 2048, as said below
- qkv_weight: bfloat16 [2, 3, 1120, 1120], P(None, None, None, 'tensor'), may hold values from -0.1875 to 0.1875
- qv_bias: bfloat16 [2, 2, 1120], P(None, None, 'tensor'), may hold values from -0.19921875 to 0.19921875
- out_weight: bfloat16 [2, 1120, 1120], P(None, 'tensor'), may hold values from -4 to 4
- out_bias: bfloat16 [2, 1120], replicated, may hold values from -0.3984375 to 0.3984375
- up_weight: bfloat16 [2, 1120, 4480], P(None, None, 'tensor'), may hold values from -0.1875 to 0.1875
- up_bias: bfloat16 [2, 4480], P(None, 'tensor'), may hold values from -0.796875 to 0.796875
- down_weight: bfloat16 [2, 4480, 1120], P(None, 'tensor'), may hold values from -0.09375 to 0.09375
- down_bias: bfloat16 [2, 1120], replicated, may hold values from -0.3984375 to 0.3984375
- norm_gain: bfloat16 [2, 2, 1120], replicated, may hold values from 0.099609375 to 1.8984375
- norm_shift: bfloat16 [2, 2, 1120], replicated, may hold values from -0.3984375 to 0.3984375
Outputs:
- block_out: bfloat16 [4, 2048, 1120], P('cell', 'seq')
- tokens_grad: bfloat16 [4, 2048, 1120], P('cell', 'seq')
- qkv_weight_grad: float32 [2, 3, 1120, 1120], P(None, None, None, 'tensor')
- qv_bias_grad: float32 [2, 2, 1120], P(None, None, 'tensor')
- out_weight_grad: float32 [2, 1120, 1120], P(None, 'tensor')
- out_bias_grad: float32 [2, 1120], replicated
- up_weight_grad: float32 [2, 1120, 4480], P(None, None, 'tensor')
- up_bias_grad: float32 [2, 4480], P(None, 'tensor')
- down_weight_grad: float32 [2, 4480, 1120], P(None, 'tensor')
- down_bias_grad: float32 [2, 1120], replicated
- norm_gain_grad: float32 [2, 2, 1120], replicated
- norm_shift_grad: float32 [2, 2, 1120], replicated
Inputs may be any that keep to these rules, and one draw needn't show every extreme that they name: `group_order`: each row is a permutation of 0 to 7 in which entries 2s and 2s + 1 are j and 7 - j for some j. tokens at places from lengths onward are padding, which no query attends to.
All inputs are finite; a program needn't handle non-finite values.
Results may differ from a plain program's by a relative error of at most 0.024.
Values may be sent and summed in bfloat16 or wider, within the bound.
A program may use at most 384 MiB of HBM per device.

v0:
```python
import jax
import jax.numpy as jnp
from jax import lax
from jax.sharding import PartitionSpec as P

HEAD = 56


EPSILON = 1e-05
MASKED = -1e30
ROOT_TWO_PI = 0.7978845608028654
CUBIC = 0.044715


def normalize(values):
    centred = values - jnp.mean(values, axis=-1, keepdims=True)
    spread = jnp.mean(centred * centred, axis=-1, keepdims=True)
    inverse = lax.rsqrt(spread + EPSILON)
    return (centred * inverse, inverse)


def norm_back(incoming, normed, inverse, gain_row):
    scaled = incoming * gain_row
    first_mean = jnp.mean(scaled, axis=-1, keepdims=True)
    second_mean = jnp.mean(scaled * normed, axis=-1, keepdims=True)
    return inverse * (scaled - first_mean - normed * second_mean)


def gelu_value(values):
    return (
        0.5 * values * (1.0 + jnp.tanh(ROOT_TWO_PI * (values + CUBIC * values * values * values)))
    )


def gelu_slope(values):
    inner = jnp.tanh(ROOT_TWO_PI * (values + CUBIC * values * values * values))
    return 0.5 * (1.0 + inner) + 0.5 * values * (1.0 - inner * inner) * ROOT_TWO_PI * (
        1.0 + 3.0 * CUBIC * values * values
    )


def rounded(values):
    return lax.optimization_barrier(values.astype(jnp.bfloat16)).astype(jnp.float32)


def total_rows(partial_value):
    return lax.psum_scatter(partial_value, "tensor", scatter_dimension=1, tiled=True)


def widen(values):
    return lax.all_gather(values, "tensor", axis=1, tiled=True)


def own_rows(values):
    share_rows = values.shape[1] // lax.axis_size("tensor")
    return lax.dynamic_slice_in_dim(values, lax.axis_index("tensor") * share_rows, share_rows, 1)


def places_of(order_rows, first_slot, row_count, half_rows):
    slot_count = order_rows.shape[1]
    stored = jnp.arange(row_count, dtype=jnp.int32)
    slot_ids = jnp.arange(slot_count, dtype=jnp.int32)
    picked = (first_slot + stored // half_rows)[:, None] == slot_ids[None, :]
    blocks = jnp.sum(jnp.where(picked[None], order_rows[:, None, :], 0), axis=-1)
    return blocks * half_rows + stored % half_rows


def split_heads(values, head_count):
    return values.reshape(
        values.shape[0], values.shape[1], head_count, values.shape[2] // head_count
    )


def masked_scores(query_rows, key_all, allowed, head_count):
    head_size = query_rows.shape[2] // head_count
    raw_scores = jnp.einsum(
        "cqhe,ckhe->chqk",
        split_heads(query_rows, head_count),
        split_heads(key_all, head_count),
        preferred_element_type=jnp.float32,
    )
    return jnp.where(allowed, raw_scores * head_size ** (-0.5), MASKED)


def attend_back(query_rows, key_all, value_all, log_total, grad_mixed, allowed, head_count):
    head_size = query_rows.shape[2] // head_count
    score_scale = head_size ** (-0.5)
    scores = masked_scores(query_rows, key_all, allowed, head_count)
    softmax_rows = jnp.exp(scores - log_total)
    probs_low = softmax_rows.astype(jnp.bfloat16)
    grad_four = split_heads(grad_mixed, head_count)
    grad_values = jnp.einsum(
        "chqk,cqhe->ckhe", probs_low, grad_four, preferred_element_type=jnp.float32
    )
    grad_probs = jnp.einsum(
        "cqhe,ckhe->chqk",
        grad_four,
        split_heads(value_all, head_count),
        preferred_element_type=jnp.float32,
    )
    inner_sum = jnp.sum(grad_probs * softmax_rows, axis=-1, keepdims=True)
    grad_scores = (softmax_rows * (grad_probs - inner_sum)).astype(jnp.bfloat16)
    grad_queries = (
        jnp.einsum(
            "chqk,ckhe->cqhe",
            grad_scores,
            split_heads(key_all, head_count),
            preferred_element_type=jnp.float32,
        )
        * score_scale
    )
    grad_keys = (
        jnp.einsum(
            "chqk,cqhe->ckhe",
            grad_scores,
            split_heads(query_rows, head_count),
            preferred_element_type=jnp.float32,
        )
        * score_scale
    )
    flat_shape = (key_all.shape[0], key_all.shape[1], key_all.shape[2])
    query_shape = query_rows.shape
    return (
        grad_queries.reshape(query_shape),
        grad_keys.reshape(flat_shape),
        grad_values.reshape(flat_shape),
    )


def shards(
    tokens,
    out_grad,
    group_order,
    lengths,
    qkv_weight,
    qv_bias,
    out_weight,
    out_bias,
    up_weight,
    up_bias,
    down_weight,
    down_bias,
    norm_gain,
    norm_shift,
):
    cell_count, row_count, model_width = tokens.shape
    layer_count = qkv_weight.shape[0]
    local_width = qkv_weight.shape[3]
    head_count = local_width // HEAD
    seq_size = lax.axis_size("seq")
    half_rows = row_count // 2
    query_places = places_of(group_order, 2 * lax.axis_index("seq"), row_count, half_rows)
    key_places = places_of(group_order, 0, row_count * seq_size, half_rows)
    allowed = (key_places[:, None, None, :] <= query_places[:, None, :, None]) & (
        key_places[:, None, None, :] < lengths[:, None, None, None]
    )
    gains = norm_gain.astype(jnp.float32)
    stream = own_rows(tokens.astype(jnp.float32))
    kept = []
    for layer_index in range(layer_count):
        normed_one, inverse_one = normalize(stream)
        wide_one = widen(
            (normed_one * gains[layer_index, 0] + norm_shift[layer_index, 0]).astype(jnp.bfloat16)
        )
        projected = jnp.einsum(
            "ctd,jde->jcte", wide_one, qkv_weight[layer_index], preferred_element_type=jnp.float32
        )
        query_rows = (projected[0] + qv_bias[layer_index, 0]).astype(jnp.bfloat16)
        key_rows = projected[1].astype(jnp.bfloat16)
        value_rows = (projected[2] + qv_bias[layer_index, 1]).astype(jnp.bfloat16)
        key_all, value_all = (
            lax.all_gather(key_rows, "seq", axis=1, tiled=True),
            lax.all_gather(value_rows, "seq", axis=1, tiled=True),
        )
        scores = masked_scores(query_rows, key_all, allowed, head_count)
        row_max = jnp.max(scores, axis=-1, keepdims=True)
        weights = jnp.exp(scores - row_max)
        weight_sum = jnp.sum(weights, axis=-1, keepdims=True)
        log_total = row_max + jnp.log(weight_sum)
        probs_low = (weights / weight_sum).astype(jnp.bfloat16)
        mixed_rows = jnp.einsum(
            "chqk,ckhe->cqhe",
            probs_low,
            split_heads(value_all, head_count),
            preferred_element_type=jnp.float32,
        )
        mixed_rows = mixed_rows.reshape(cell_count, row_count, local_width).astype(jnp.bfloat16)
        attended = total_rows(
            jnp.einsum(
                "ctw,wd->ctd",
                mixed_rows,
                out_weight[layer_index],
                preferred_element_type=jnp.float32,
            )
        )
        stream_mid = stream + attended + out_bias[layer_index]
        normed_two, inverse_two = normalize(stream_mid)
        wide_two = widen(
            (normed_two * gains[layer_index, 1] + norm_shift[layer_index, 1]).astype(jnp.bfloat16)
        )
        pre_act = (
            jnp.einsum(
                "ctd,df->ctf", wide_two, up_weight[layer_index], preferred_element_type=jnp.float32
            )
            + up_bias[layer_index]
        )
        hidden_rows = gelu_value(pre_act).astype(jnp.bfloat16)
        lowered = total_rows(
            jnp.einsum(
                "ctf,fd->ctd",
                hidden_rows,
                down_weight[layer_index],
                preferred_element_type=jnp.float32,
            )
        )
        kept.append(
            (
                normed_one,
                inverse_one,
                wide_one,
                query_rows,
                key_all,
                value_all,
                log_total,
                mixed_rows,
                normed_two,
                inverse_two,
                wide_two,
                pre_act,
                hidden_rows,
            )
        )
        stream = stream_mid + lowered + down_bias[layer_index]
    block_out = widen(stream.astype(jnp.bfloat16))
    qkv_grads = [None] * layer_count
    qv_grads = [None] * layer_count
    out_grads = [None] * layer_count
    outb_grads = [None] * layer_count
    up_grads = [None] * layer_count
    upb_grads = [None] * layer_count
    down_grads = [None] * layer_count
    downb_grads = [None] * layer_count
    gain_grads = [None] * layer_count
    shift_grads = [None] * layer_count
    grad_stream = own_rows(out_grad.astype(jnp.float32))
    for layer_index in reversed(range(layer_count)):
        (
            normed_one,
            inverse_one,
            wide_one,
            query_rows,
            key_all,
            value_all,
            log_total,
            mixed_rows,
            normed_two,
            inverse_two,
            wide_two,
            pre_act,
            hidden_rows,
        ) = kept[layer_index]
        downb_grads[layer_index] = jnp.sum(grad_stream, axis=(0, 1))
        grad_down = widen(grad_stream.astype(jnp.bfloat16))
        down_grads[layer_index] = jnp.einsum(
            "ctf,ctd->fd", hidden_rows, grad_down, preferred_element_type=jnp.float32
        )
        grad_hidden = rounded(
            jnp.einsum(
                "ctd,fd->ctf",
                grad_down,
                down_weight[layer_index],
                preferred_element_type=jnp.float32,
            )
        )
        grad_pre = (grad_hidden * gelu_slope(pre_act)).astype(jnp.bfloat16)
        upb_grads[layer_index] = jnp.sum(grad_pre.astype(jnp.float32), axis=(0, 1))
        up_grads[layer_index] = jnp.einsum(
            "ctd,ctf->df", wide_two, grad_pre, preferred_element_type=jnp.float32
        )
        grad_normed_two = total_rows(
            jnp.einsum(
                "ctf,df->ctd", grad_pre, up_weight[layer_index], preferred_element_type=jnp.float32
            )
        )
        gain_two = jnp.sum(grad_normed_two * normed_two, axis=(0, 1))
        shift_two = jnp.sum(grad_normed_two, axis=(0, 1))
        grad_stream = grad_stream + norm_back(
            grad_normed_two, normed_two, inverse_two, gains[layer_index, 1]
        )
        outb_grads[layer_index] = jnp.sum(grad_stream, axis=(0, 1))
        grad_mid = widen(grad_stream.astype(jnp.bfloat16))
        out_grads[layer_index] = jnp.einsum(
            "ctw,ctd->wd", mixed_rows, grad_mid, preferred_element_type=jnp.float32
        )
        grad_mixed = jnp.einsum(
            "ctd,wd->ctw", grad_mid, out_weight[layer_index], preferred_element_type=jnp.float32
        ).astype(jnp.bfloat16)
        grad_queries, grad_keys_all, grad_values_all = attend_back(
            query_rows, key_all, value_all, log_total, grad_mixed, allowed, head_count
        )
        grad_keys, grad_values = (
            lax.psum_scatter(grad_keys_all, "seq", scatter_dimension=1, tiled=True),
            lax.psum_scatter(grad_values_all, "seq", scatter_dimension=1, tiled=True),
        )
        stacked = jnp.stack(
            [
                grad_queries.astype(jnp.bfloat16),
                grad_keys.astype(jnp.bfloat16),
                grad_values.astype(jnp.bfloat16),
            ]
        )
        stacked_sums = jnp.sum(stacked.astype(jnp.float32), axis=(1, 2))
        qv_grads[layer_index] = jnp.stack([stacked_sums[0], stacked_sums[2]])
        qkv_grads[layer_index] = jnp.einsum(
            "ctd,jctw->jdw", wide_one, stacked, preferred_element_type=jnp.float32
        )
        grad_normed_one = total_rows(
            jnp.einsum(
                "jctw,jdw->ctd",
                stacked,
                qkv_weight[layer_index],
                preferred_element_type=jnp.float32,
            )
        )
        gain_one = jnp.sum(grad_normed_one * normed_one, axis=(0, 1))
        shift_one = jnp.sum(grad_normed_one, axis=(0, 1))
        grad_stream = grad_stream + norm_back(
            grad_normed_one, normed_one, inverse_one, gains[layer_index, 0]
        )
        gain_grads[layer_index] = jnp.stack([gain_one, gain_two])
        shift_grads[layer_index] = jnp.stack([shift_one, shift_two])
    tokens_grad = widen(grad_stream.astype(jnp.bfloat16))
    gain_all = jnp.stack(gain_grads)
    shift_all = jnp.stack(shift_grads)
    outb_all = jnp.stack(outb_grads)
    downb_all = jnp.stack(downb_grads)
    gain_all, shift_all, outb_all, downb_all = lax.psum(
        (gain_all, shift_all, outb_all, downb_all), "tensor"
    )
    summed = lax.psum(
        (
            jnp.stack(qkv_grads),
            jnp.stack(qv_grads),
            jnp.stack(out_grads),
            outb_all,
            jnp.stack(up_grads),
            jnp.stack(upb_grads),
            jnp.stack(down_grads),
            downb_all,
            gain_all,
            shift_all,
        ),
        ("cell", "seq"),
    )
    return (
        block_out,
        tokens_grad,
        summed[0],
        summed[1],
        summed[2],
        summed[3],
        summed[4],
        summed[5],
        summed[6],
        summed[7],
        summed[8],
        summed[9],
    )


def solution(mesh):
    return jax.shard_map(
        shards,
        mesh=mesh,
        in_specs=(
            P("cell", "seq", None),
            P("cell", "seq", None),
            P("cell", None),
            P("cell"),
            P(None, None, None, "tensor"),
            P(None, None, "tensor"),
            P(None, "tensor", None),
            P(),
            P(None, None, "tensor"),
            P(None, "tensor"),
            P(None, "tensor", None),
            P(),
            P(),
            P(),
        ),
        out_specs=(
            P("cell", "seq", None),
            P("cell", "seq", None),
            P(None, None, None, "tensor"),
            P(None, None, "tensor"),
            P(None, "tensor", None),
            P(),
            P(None, None, "tensor"),
            P(None, "tensor"),
            P(None, "tensor", None),
            P(),
            P(),
            P(),
        ),
        check_vma=False,
    )
```

profile of v0, /device:TPU:0, one launch (start us, length us, event | category | flops | bytes accessed | tf_op | source)
XLA Modules:
  0.0 2396.3 jit_solution(14871324249181799074)
XLA Ops:
  14.8 26.7 %all-gather.17.cloned.1.call-done = bf16[2,512,1120]{1,2,0:T(8,128)(2,1)} async-done(((bf16[2,128,1120]{1,2,0:T(8,128)(2,1)}), bf16[2,512,1120]{1,2,0:T(8,128)(2,1)}) %all-gather.17.cloned.1.call-update) | async-done | bytes 2293776 | tf_op jit(solution)/shard_map/all_gather | solution.py:51
  55.6 42.8 %all-gather.41.cloned.1.call-done = bf16[1,2,2048,280]{2,3,0,1:T(8,128)(2,1)} async-done(((bf16[1,2,512,280]{2,3,0,1:T(8,128)(2,1)}), bf16[1,2,2048,280]{2,3,0,1:T(8,128)(2,1)}) %all-gather.41.cloned.1.call-update) | async-done | bytes 2293776 | tf_op jit(solution)/shard_map/all_gather | solution.py:172
  98.5 20.0 fusion.126
  118.5 16.7 fusion
  170.0 45.3 %reduce-scatter.13.cloned.1.call-done = f32[2,128,1120]{1,2,0:T(8,128)} async-done(((f32[2,512,1120]{1,2,0:T(8,128)}), f32[2,128,1120]{1,2,0:T(8,128)}) %reduce-scatter.13.cloned.1.call-update) | async-done | bytes 1146896 | tf_op jit(solution)/shard_map/reduce_scatter | solution.py:47
  218.6 23.9 all-gather.21.cloned.1.call-done
  257.6 46.4 %reduce-scatter.15.cloned.1.call-done = f32[2,128,1120]{1,2,0:T(8,128)} async-done(((f32[2,512,1120]{1,2,0:T(8,128)}), f32[2,128,1120]{1,2,0:T(8,128)}) %reduce-scatter.15.cloned.1.call-update) | async-done | bytes 1146896 | tf_op jit(solution)/shard_map/reduce_scatter | solution.py:47
  307.8 24.1 %all-gather.23.cloned.1.call-done = bf16[2,512,1120]{1,2,0:T(8,128)(2,1)} async-done(((bf16[2,128,1120]{1,2,0:T(8,128)(2,1)}), bf16[2,512,1120]{1,2,0:T(8,128)(2,1)}) %all-gather.23.cloned.1.call-update) | async-done | bytes 2293776 | tf_op jit(solution)/shard_map/all_gather | solution.py:51
  343.7 45.1 %all-gather.43.cloned.1.call-done = bf16[1,2,2048,280]{2,3,0,1:T(8,128)(2,1)} async-done(((bf16[1,2,512,280]{2,3,0,1:T(8,128)(2,1)}), bf16[1,2,2048,280]{2,3,0,1:T(8,128)(2,1)}) %all-gather.43.cloned.1.call-update) | async-done | bytes 2293776 | tf_op jit(solution)/shard_map/all_gather | solution.py:172
  388.8 20.0 fusion.127
  408.8 16.7 fusion.1
  439.2 15.9 fusion.72
  461.7 43.9 %reduce-scatter.17.cloned.1.call-done = f32[2,128,1120]{1,2,0:T(8,128)} async-done(((f32[2,512,1120]{1,2,0:T(8,128)}), f32[2,128,1120]{1,2,0:T(8,128)}) %reduce-scatter.17.cloned.1.call-update) | async-done | bytes 1146896 | tf_op jit(solution)/shard_map/reduce_scatter | solution.py:47
  508.9 22.8 all-gather.31.cloned.1.call-done
  538.8 19.0 all-gather.27.cloned.1.call-done
  584.8 38.0 %reduce-scatter.21.cloned.1.call-done = f32[2,128,1120]{1,2,0:T(8,128)} async-done(((f32[2,512,1120]{1,2,0:T(8,128)}), f32[2,128,1120]{1,2,0:T(8,128)}) %reduce-scatter.21.cloned.1.call-update) | async-done | bytes 1146896 | tf_op jit(solution)/shard_map/reduce_scatter | solution.py:47
  625.4 47.4 %reduce-scatter.19.cloned.1.call-done = f32[2,128,1120]{1,2,0:T(8,128)} async-done(((f32[2,512,1120]{1,2,0:T(8,128)}), f32[2,128,1120]{1,2,0:T(8,128)}) %reduce-scatter.19.cloned.1.call-update) | async-done | bytes 1146896 | tf_op jit(solution)/shard_map/reduce_scatter | solution.py:47
  677.4 24.1 %all-gather.33.cloned.1.call-done = bf16[2,512,1120]{1,2,0:T(8,128)(2,1)} async-done(((bf16[2,128,1120]{1,2,0:T(8,128)(2,1)}), bf16[2,512,1120]{1,2,0:T(8,128)(2,1)}) %all-gather.33.cloned.1.call-update) | async-done | bytes 2293776 | tf_op jit(solution)/shard_map/all_gather | solution.py:51
  704.1 18.5 fusion.6
  722.7 28.8 %multiply_reduce_fusion.1 = (f32[2,5,512]{2,1,0:T(8,128)S(1)}, f32[2,5,512,2048]{3,2,1,0:T(8,128)}) fusion(f32[2,5,512,2048]{3,2,1,0:T(8,128)} %get-tuple-element.87, f32[2,5,512]{2,1,0:T(8,128)S(1)} %log_add_fusion.1, bf16[2,512,5,56]{1,3,2,0:T(8,128)(2,1)S(1)} %bitcast.247, bf16[2,2048,5,56]{1,3,2,0:T(8,128)(2,1)} %bitcast.259), kind=kOutput, calls=%fused_computation.4 | convolution fusion | flops 1205857280 | bytes 86794240 | tf_op jit(solution)/shard_map/cqhe,ckhe->chqk/dot_general | solution.py:95
  751.5 34.2 %multiply_convert_fusion.1 = bf16[2,5,512,2048]{3,2,1,0:T(8,128)(2,1)} fusion(f32[2,5,512,2048]{3,2,1,0:T(8,128)} %get-tuple-element.90, f32[2,5,512,2048]{3,2,1,0:T(8,128)} %get-tuple-element.87, f32[2,5,512]{2,1,0:T(8,128)S(1)} %get-tuple-element.89, f32[2,5,512]{2,1,0:T(8,128)S(1)} %log_add_fusion.1), kind=kLoop, calls=%fused_computation.3 | loop fusion | flops 41943040 | bytes 104898560 | tf_op jit(solution)/shard_map/convert_element_type | solution.py:102
  813.3 79.2 %reduce-scatter.23.cloned.1.call-done = f32[2,512,280]{1,2,0:T(8,128)} async-done(((f32[2,2048,280]{1,2,0:T(8,128)}), f32[2,512,280]{1,2,0:T(8,128)}) %reduce-scatter.23.cloned.1.call-update) | async-done | bytes 1146896 | tf_op jit(solution)/shard_map/reduce_scatter | solution.py:302
  900.5 47.6 %reduce-scatter.27.cloned.1.call-done = f32[2,128,1120]{1,2,0:T(8,128)} async-done(((f32[2,512,1120]{1,2,0:T(8,128)}), f32[2,128,1120]{1,2,0:T(8,128)}) %reduce-scatter.27.cloned.1.call-update) | async-done | bytes 1146896 | tf_op jit(solution)/shard_map/reduce_scatter | solution.py:47
  952.8 24.1 %all-gather.35.cloned.1.call-done = bf16[2,512,1120]{1,2,0:T(8,128)(2,1)} async-done(((bf16[2,128,1120]{1,2,0:T(8,128)(2,1)}), bf16[2,512,1120]{1,2,0:T(8,128)(2,1)}) %all-gather.35.cloned.1.call-update) | async-done | bytes 2293776 | tf_op jit(solution)/shard_map/all_gather | solution.py:51
  996.4 46.7 %reduce-scatter.29.cloned.1.call-done = f32[2,128,1120]{1,2,0:T(8,128)} async-done(((f32[2,512,1120]{1,2,0:T(8,128)}), f32[2,128,1120]{1,2,0:T(8,128)}) %reduce-scatter.29.cloned.1.call-update) | async-done | bytes 1146896 | tf_op jit(solution)/shard_map/reduce_scatter | solution.py:47
  1048.9 24.0 %all-gather.37.cloned.1.call-done = bf16[2,512,1120]{1,2,0:T(8,128)(2,1)} async-done(((bf16[2,128,1120]{1,2,0:T(8,128)(2,1)}), bf16[2,512,1120]{1,2,0:T(8,128)(2,1)}) %all-gather.37.cloned.1.call-update) | async-done | bytes 2293776 | tf_op jit(solution)/shard_map/all_gather | solution.py:51
  1075.5 18.5 fusion.4
  1095.7 28.1 %multiply_reduce_fusion = (f32[2,5,512]{2,1,0:T(8,128)S(1)}, f32[2,5,512,2048]{3,2,1,0:T(8,128)}) fusion(f32[2,5,512,2048]{3,2,1,0:T(8,128)} %get-tuple-element.85, f32[2,5,512]{2,1,0:T(8,128)S(1)} %log_add_fusion, bf16[2,512,5,56]{1,3,2,0:T(8,128)(2,1)S(1)} %bitcast.249, bf16[2,2048,5,56]{1,3,2,0:T(8,128)(2,1)S(1)} %bitcast.257), kind=kOutput, calls=%fused_computation.1 | convolution fusion | flops 1205857280 | bytes 86794240 | tf_op jit(solution)/shard_map/cqhe,ckhe->chqk/dot_general | solution.py:95
  1123.8 34.5 %multiply_convert_fusion = bf16[2,5,512,2048]{3,2,1,0:T(8,128)(2,1)} fusion(f32[2,5,512,2048]{3,2,1,0:T(8,128)} %get-tuple-element.92, f32[2,5,512,2048]{3,2,1,0:T(8,128)} %get-tuple-element.85, f32[2,5,512]{2,1,0:T(8,128)S(1)} %get-tuple-element.91, f32[2,5,512]{2,1,0:T(8,128)S(1)} %log_add_fusion), kind=kLoop, calls=%fused_computation | loop fusion | flops 41943040 | bytes 104898560 | tf_op jit(solution)/shard_map/convert_element_type | solution.py:102
  1185.1 78.9 %reduce-scatter.31.cloned.1.call-done = f32[2,512,280]{1,2,0:T(8,128)} async-done(((f32[2,2048,280]{1,2,0:T(8,128)}), f32[2,512,280]{1,2,0:T(8,128)}) %reduce-scatter.31.cloned.1.call-update) | async-done | bytes 1146896 | tf_op jit(solution)/shard_map/reduce_scatter | solution.py:302
  1371.1 75.7 %all-reduce.6.cloned.1.call-done = (f32[2,2,280]{2,1,0:T(2,128)}, f32[2,1120]{1,0:T(2,128)}, f32[2,1120]{1,0:T(2,128)}, f32[2,1120]{1,0:T(2,128)}, f32[2,2,1120]{2,1,0:T(2,128)}, /*index=5*/f32[2,2,1120]{2,1,0:T(2,128)}) async-done(((f32[2,2,280]{2,1,0:T(2,128)}, f32[2,1120]{1,0:T(2,128)}, f32[2,1120]{1,0:T(2,128)}, f32[2,1120]{1,0:T(2,128)}, f32[2,2,1120]{2,1,0:T(2,128)}, ...) | async-done | bytes 67216 | tf_op jit(solution)/shard_map/psum | solution.py:340
  1446.8 914.0 %all-reduce.8.cloned.1.call-done = (f32[2,3,1120,280]{2,3,1,0:T(8,128)}, f32[2,280,1120]{2,1,0:T(8,128)}, f32[2,1120,1120]{2,1,0:T(8,128)}, f32[2,1120,1120]{2,1,0:T(8,128)}) async-done(((f32[2,3,1120,280]{2,3,1,0:T(8,128)}, f32[2,280,1120]{2,1,0:T(8,128)}, f32[2,1120,1120]{2,1,0:T(8,128)}, f32[2,1120,1120]{2,1,0:T(8,128)}), (f32[2,3,1120,280]{2,3,1,0:T(8,128)}, f32[2,280,1120]{2,1,0:T(8,128)}, ...) | async-done | bytes 30105616 | tf_op jit(solution)/shard_map/psum | solution.py:340
  (441 shorter events, 388.2 us)
Async XLA Ops:
  7.2 34.4 %all-gather.17.cloned.1.call-start = ((), (), s32[]{:S(2)}) async-start(), calls=%async_computation.12 | async-start | bytes 2867200 | tf_op jit(solution)/shard_map/all_gather | solution.py:51
  11.9 205.2 %copy-start.53 = (f32[1120]{0:T(1024)}, f32[1120]{0:T(1024)S(1)}, u32[]{:S(2)}) copy-start(f32[1120]{0:T(1024)S(1)} %get-tuple-element.30) | copy-start | bytes 13444
  11.9 293.8 %copy-start.55 = (f32[1120]{0:T(1024)}, f32[1120]{0:T(1024)S(1)}, u32[]{:S(2)}) copy-start(f32[1120]{0:T(1024)S(1)} %get-tuple-element.29) | copy-start | bytes 13444
  14.8 83.7 %all-gather.41.cloned.1.call-start = ((), (), s32[]{:S(2)}) async-start(), calls=%async_computation.36 | async-start | bytes 2867200 | tf_op jit(solution)/shard_map/all_gather | solution.py:172
  48.9 99.9 %all-gather.19.cloned.1.call-start = ((), (), s32[]{:S(2)}) async-start(), calls=%async_computation.13 | async-start | bytes 2867200 | tf_op jit(solution)/shard_map/all_gather | solution.py:173
  55.1 160.2 %reduce-scatter.13.cloned.1.call-start = ((), (), s32[]{:S(2)}) async-start(), calls=%async_computation.14 | async-start | bytes 5734400 | tf_op jit(solution)/shard_map/reduce_scatter | solution.py:47
  169.3 73.2 %all-gather.21.cloned.1.call-start = ((), (), s32[]{:S(2)}) async-start(), calls=%async_computation.15 | async-start | bytes 2867200 | tf_op jit(solution)/shard_map/all_gather | solution.py:51
  216.9 87.2 %copy-start = (f32[2,128,1120]{1,2,0:T(8,128)}, f32[2,128,1120]{1,2,0:T(8,128)S(1)}, u32[]{:S(2)}) copy-start(f32[2,128,1120]{1,2,0:T(8,128)S(1)} %get-tuple-element.75) | copy-start | bytes 3440644
  218.3 85.7 %reduce-scatter.15.cloned.1.call-start = ((), (), s32[]{:S(2)}) async-start(), calls=%async_computation.16 | async-start | bytes 5734400 | tf_op jit(solution)/shard_map/reduce_scatter | solution.py:47
  256.9 75.0 %all-gather.23.cloned.1.call-start = ((), (), s32[]{:S(2)}) async-start(), calls=%async_computation.17 | async-start | bytes 2867200 | tf_op jit(solution)/shard_map/all_gather | solution.py:51
  307.7 81.1 %all-gather.43.cloned.1.call-start = ((), (), s32[]{:S(2)}) async-start(), calls=%async_computation.37 | async-start | bytes 2867200 | tf_op jit(solution)/shard_map/all_gather | solution.py:172
  339.3 99.9 %all-gather.25.cloned.1.call-start = ((), (), s32[]{:S(2)}) async-start(), calls=%async_computation.18 | async-start | bytes 2867200 | tf_op jit(solution)/shard_map/all_gather | solution.py:173
  343.4 162.1 %reduce-scatter.17.cloned.1.call-start = ((), (), s32[]{:S(2)}) async-start(), calls=%async_computation.19 | async-start | bytes 5734400 | tf_op jit(solution)/shard_map/reduce_scatter | solution.py:47
  459.5 72.2 %all-gather.31.cloned.1.call-start = ((), (), s32[]{:S(2)}) async-start(), calls=%async_computation.23 | async-start | bytes 2867200 | tf_op jit(solution)/shard_map/all_gather | solution.py:51
  461.6 96.2 %all-gather.27.cloned.1.call-start = ((), (), s32[]{:S(2)}) async-start(), calls=%async_computation.20 | async-start | bytes 2867200 | tf_op jit(solution)/shard_map/all_gather | solution.py:51
  508.5 114.4 %reduce-scatter.21.cloned.1.call-start = ((), (), s32[]{:S(2)}) async-start(), calls=%async_computation.24 | async-start | bytes 5734400 | tf_op jit(solution)/shard_map/reduce_scatter | solution.py:47
  575.7 97.1 %reduce-scatter.19.cloned.1.call-start = ((), (), s32[]{:S(2)}) async-start(), calls=%async_computation.21 | async-start | bytes 5734400 | tf_op jit(solution)/shard_map/reduce_scatter | solution.py:47
  584.6 116.8 %all-gather.33.cloned.1.call-start = ((), (), s32[]{:S(2)}) async-start(), calls=%async_computation.25 | async-start | bytes 2867200 | tf_op jit(solution)/shard_map/all_gather | solution.py:51
  677.3 134.6 %reduce-scatter.25.cloned.1.call-start = ((), (), s32[]{:S(2)}) async-start(), calls=%async_computation.27 | async-start | bytes 5734400 | tf_op jit(solution)/shard_map/reduce_scatter | solution.py:303
  722.7 169.8 %reduce-scatter.23.cloned.1.call-start = ((), (), s32[]{:S(2)}) async-start(), calls=%async_computation.26 | async-start | bytes 5734400 | tf_op jit(solution)/shard_map/reduce_scatter | solution.py:302
  798.7 149.4 %reduce-scatter.27.cloned.1.call-start = ((), (), s32[]{:S(2)}) async-start(), calls=%async_computation.28 | async-start | bytes 5734400 | tf_op jit(solution)/shard_map/reduce_scatter | solution.py:47
  900.4 76.5 %all-gather.35.cloned.1.call-start = ((), (), s32[]{:S(2)}) async-start(), calls=%async_computation.29 | async-start | bytes 2867200 | tf_op jit(solution)/shard_map/all_gather | solution.py:51
  952.7 90.4 %reduce-scatter.29.cloned.1.call-start = ((), (), s32[]{:S(2)}) async-start(), calls=%async_computation.30 | async-start | bytes 5734400 | tf_op jit(solution)/shard_map/reduce_scatter | solution.py:47
  995.9 77.0 %all-gather.37.cloned.1.call-start = ((), (), s32[]{:S(2)}) async-start(), calls=%async_computation.31 | async-start | bytes 2867200 | tf_op jit(solution)/shard_map/all_gather | solution.py:51
  1048.8 134.8 %reduce-scatter.33.cloned.1.call-start = ((), (), s32[]{:S(2)}) async-start(), calls=%async_computation.33 | async-start | bytes 5734400 | tf_op jit(solution)/shard_map/reduce_scatter | solution.py:303
  1094.0 170.0 %reduce-scatter.31.cloned.1.call-start = ((), (), s32[]{:S(2)}) async-start(), calls=%async_computation.32 | async-start | bytes 5734400 | tf_op jit(solution)/shard_map/reduce_scatter | solution.py:302
  1171.2 148.4 %reduce-scatter.35.cloned.1.call-start = ((), (), s32[]{:S(2)}) async-start(), calls=%async_computation.34 | async-start | bytes 5734400 | tf_op jit(solution)/shard_map/reduce_scatter | solution.py:47
  1183.5 88.3 %copy-start.21 = (bf16[2,5,56,512]{3,2,1,0:T(8,128)(2,1)}, bf16[2,5,56,512]{3,2,1,0:T(8,128)(2,1)S(1)}, u32[]{:S(2)}) copy-start(bf16[2,5,56,512]{3,2,1,0:T(8,128)(2,1)S(1)} %fusion.75) | copy-start | bytes 1720324
  1271.9 89.9 %all-gather.29.cloned.1.call-start = ((), (), s32[]{:S(2)}) async-start(), calls=%async_computation.22 | async-start | bytes 2867200 | tf_op jit(solution)/shard_map/all_gather | solution.py:51
  1290.2 81.0 %all-gather.39.cloned.1.call-start = ((), (), s32[]{:S(2)}) async-start(), calls=%async_computation.35 | async-start | bytes 2867200 | tf_op jit(solution)/shard_map/all_gather | solution.py:51
  1324.1 122.7 %all-reduce.6.cloned.1.call-start = ((), (), s32[]{:S(2)}) async-start(), calls=%async_computation.38 | async-start | bytes 141312 | tf_op jit(solution)/shard_map/psum | solution.py:340
  1354.4 1006.3 %all-reduce.8.cloned.1.call-start = ((), (), s32[]{:S(2)}) async-start(), calls=%async_computation.39 | async-start | bytes 61931520 | tf_op jit(solution)/shard_map/psum | solution.py:340
  (109 other events, 1873.8 us)
Sparse Core Ops, SparseCore 0:
  14.9 26.6 all-gather.16
  49.1 49.3 all-gather.40
  100.6 48.2 all-gather.18
  169.4 45.8 reduce-scatter.12
  218.4 23.9 all-gather.20
  257.0 46.9 reduce-scatter.14
  307.8 23.9 all-gather.22
  339.4 49.3 all-gather.42
  390.9 48.2 all-gather.24
  459.7 45.8 reduce-scatter.16
  507.7 23.9 all-gather.30
  533.8 23.9 all-gather.26
  575.8 46.9 reduce-scatter.20
  625.8 46.9 reduce-scatter.18
  677.4 23.9 all-gather.32
  722.8 83.1 reduce-scatter.24
  808.8 83.6 reduce-scatter.22
  900.5 47.4 reduce-scatter.26
  952.8 23.9 all-gather.34
  996.1 46.9 reduce-scatter.28
  1048.9 23.9 all-gather.36
  1094.2 83.1 reduce-scatter.32
  1180.3 83.6 reduce-scatter.30
  1272.0 47.4 reduce-scatter.34
  1321.1 23.9 all-gather.28
  1347.1 23.9 all-gather.38
  1376.3 70.4 all-reduce.5
  1452.8 907.9 all-reduce.7
where the time goes:
time: 2400 us
  waiting for transfers between devices  1780 us (74%)
  matrix products  346 us (14%)
  other arithmetic  184 us (8%)
  local copies, waits for them, and re-layouts  52.6 us (2%)
    psum x2, waiting for transfers between devices, shards(): lax.psum((jnp.stack(qkv_grads), jnp.stack(qv_grads), jnp.stack(out_grads)...  990 us
    reduce_scatter x8, waiting for transfers between devices, total_rows(): lax.psum_scatter(partial_value, 'tensor', scatter_dimension=1, tiled=True)  321 us
    all_gather x10, waiting for transfers between devices, widen(): return lax.all_gather(values, 'tensor', axis=1, tiled=True)  198 us
    reduce_scatter x2, waiting for transfers between devices, shards(): lax.psum_scatter(grad_keys_all, 'seq', scatter_dimension=1, tiled=True)  158 us
    all_gather x2, waiting for transfers between devices, shards(): lax.all_gather(key_rows, 'seq', axis=1, tiled=True)  88 us
    convert_element_type x2, other arithmetic, attend_back(): grad_scores = (softmax_rows * (grad_probs - inner_sum)).astype(jnp.bfloat16)  68.7 us
    dot_general x2, matrix products, attend_back(): jnp.einsum('cqhe,ckhe->chqk', grad_four, split_heads(value_all, head_coun...  56.9 us
  transfers between devices with their start and end apart: 28, of which 25 were waited for; matrix products, arithmetic and copies ran while one was open for 15% of the time, Pallas kernels for 0%

commit v1 on v0

v1 whole, which is shorter than its diff:
```python
import functools

import jax
import jax.numpy as jnp
from jax import lax
from jax.experimental import pallas as pl
from jax.experimental.pallas import tpu as pltpu
from jax.sharding import PartitionSpec as P

HEAD = 56
EPSILON = 1e-05
MASKED = -1e30
ROOT_TWO_PI = 0.7978845608028654
CUBIC = 0.044715
LOG2E = 1.4426950408889634
F32 = jnp.float32
BF16 = jnp.bfloat16


def swap(values, axis, bit):
    size = lax.axis_size(axis)
    return lax.ppermute(values, axis, [(i, i ^ bit) for i in range(size)])


def shift_right(values, axis):
    size = lax.axis_size(axis)
    return lax.ppermute(values, axis, [(i, (i + 1) % size) for i in range(size)])


def normalize(values):
    centred = values - jnp.mean(values, axis=-1, keepdims=True)
    spread = jnp.mean(centred * centred, axis=-1, keepdims=True)
    inverse = lax.rsqrt(spread + EPSILON)
    return (centred * inverse, inverse)


def norm_back(incoming, normed, inverse, gain_row):
    scaled = incoming * gain_row
    first_mean = jnp.mean(scaled, axis=-1, keepdims=True)
    second_mean = jnp.mean(scaled * normed, axis=-1, keepdims=True)
    return inverse * (scaled - first_mean - normed * second_mean)


def gelu_both(values):
    inner = jnp.tanh(ROOT_TWO_PI * (values + CUBIC * values * values * values))
    hidden = 0.5 * values * (1.0 + inner)
    slope = 0.5 * (1.0 + inner) + 0.5 * values * (1.0 - inner * inner) * ROOT_TWO_PI * (
        1.0 + 3.0 * CUBIC * values * values
    )
    return hidden.astype(BF16), slope.astype(BF16)


def contract(left, right, left_dim, right_dim):
    return lax.dot_general(
        left, right, (((left_dim,), (right_dim,)), ((), ())), preferred_element_type=F32
    )


def score_block(info, keys, queries, key_block, query_block, masked):
    scores = contract(keys, queries, 0, 0)
    if masked:
        rows = scores.shape[0]
        key_place = key_block * rows + lax.broadcasted_iota(jnp.int32, scores.shape, 0)
        query_place = query_block * rows + lax.broadcasted_iota(jnp.int32, scores.shape, 1)
        allowed = (key_place <= query_place) & (key_place < info[2])
        scores = jnp.where(allowed, scores, MASKED)
    return scores


def for_blocks(info, ring, block_rows, work):
    def one(step, carry):
        key_half, query_half = step // 2, step % 2
        key_block, query_block = info[3 + 2 * ring + key_half], info[query_half]
        first = key_block * block_rows
        counts = (key_block <= query_block) & (first < info[2])
        partial = (key_block == query_block) | (first + block_rows > info[2])

        @pl.when(counts & partial)
        def _():
            work(key_half, query_half, key_block, query_block, True)

        @pl.when(counts & jnp.logical_not(partial))
        def _():
            work(key_half, query_half, key_block, query_block, False)

        return carry

    lax.fori_loop(0, 4, one, 0)


def attend_kernel(info, queries, *refs):
    rings = len(refs) - 5
    pairs = refs[:rings]
    mixed, log_total, top, total, sums = refs[rings:]
    heads, head_size, tokens = queries.shape
    rows = tokens // 2
    factor = head_size**-0.5 * LOG2E
    top[...] = jnp.full_like(top, MASKED)
    total[...] = jnp.zeros_like(total)
    sums[...] = jnp.zeros_like(sums)
    for ring in range(rings):
        pair = pairs[ring]

        def work(key_half, query_half, key_block, query_block, masked, pair=pair):
            key_at = pl.ds(pl.multiple_of(key_half * rows, rows), rows)
            query_at = pl.ds(pl.multiple_of(query_half * rows, rows), rows)
            for head in range(heads):
                scores = score_block(
                    info,
                    pair[0, head, :, key_at],
                    queries[head, :, query_at],
                    key_block,
                    query_block,
                    masked,
                )
                old = top[head, :, query_at]
                new = jnp.maximum(old, jnp.max(scores, axis=0, keepdims=True) * factor)
                decay = jnp.exp2(old - new)
                weights = jnp.exp2(scores * factor - new)
                top[head, :, query_at] = new
                total[head, :, query_at] = total[head, :, query_at] * decay + jnp.sum(
                    weights, axis=0, keepdims=True
                )
                sums[head, :, query_at] = sums[head, :, query_at] * decay + contract(
                    pair[1, head, :, key_at], weights.astype(BF16), 1, 0
                )

        for_blocks(info, ring, rows, work)
    for head in range(heads):
        mixed[head] = (sums[head] / total[head]).astype(BF16)
        log_total[head] = top[head] + jnp.log2(total[head])


def attend_back_kernel(info, queries, grad_mixed, mixed, log_total, *refs):
    rings = (len(refs) - 4) // 2
    pairs = refs[:rings]
    grad_queries = refs[rings]
    grad_pairs = refs[rings + 1 : 2 * rings + 1]
    inner, sums, pair_sums = refs[2 * rings + 1 :]
    heads, head_size, tokens = queries.shape
    rows = tokens // 2
    scale = head_size**-0.5
    factor = scale * LOG2E
    for head in range(heads):
        inner[head] = jnp.sum(
            grad_mixed[head].astype(F32) * mixed[head].astype(F32), axis=0, keepdims=True
        )
    sums[...] = jnp.zeros_like(sums)
    for ring in range(rings):
        pair = pairs[ring]
        pair_sums[...] = jnp.zeros_like(pair_sums)

        def work(key_half, query_half, key_block, query_block, masked, pair=pair):
            key_at = pl.ds(pl.multiple_of(key_half * rows, rows), rows)
            query_at = pl.ds(pl.multiple_of(query_half * rows, rows), rows)
            for head in range(heads):
                keys, values = pair[0, head, :, key_at], pair[1, head, :, key_at]
                query_part, grad_part = queries[head, :, query_at], grad_mixed[head, :, query_at]
                scores = score_block(info, keys, query_part, key_block, query_block, masked)
                probs = jnp.exp2(scores * factor - log_total[head, :, query_at])
                grad_probs = contract(values, grad_part, 0, 0)
                grad_scores = (probs * (grad_probs - inner[head, :, query_at])).astype(BF16)
                pair_sums[1, head, :, key_at] += contract(grad_part, probs.astype(BF16), 1, 1)
                pair_sums[0, head, :, key_at] += contract(query_part, grad_scores, 1, 1)
                sums[head, :, query_at] += contract(keys, grad_scores, 1, 0)

        for_blocks(info, ring, rows, work)
        grad_pairs[ring][0] = (pair_sums[0] * scale).astype(BF16)
        grad_pairs[ring][1] = pair_sums[1].astype(BF16)
    grad_queries[...] = (sums[...] * scale).astype(BF16)


def kernel_cost(shape, rings, matmuls):
    heads, head_size, tokens = shape
    pairs = heads * tokens * tokens * rings
    return pl.CostEstimate(
        flops=2 * pairs * 256 * matmuls // 2,
        bytes_accessed=2 * heads * head_size * tokens * (2 * rings + 2),
        transcendentals=pairs // 2,
    )


def attend(info, queries, pairs):
    heads, head_size, tokens = queries.shape
    rings = len(pairs)
    vmem = pl.BlockSpec(memory_space=pltpu.VMEM)
    return pl.pallas_call(
        attend_kernel,
        out_shape=(
            jax.ShapeDtypeStruct(queries.shape, BF16),
            jax.ShapeDtypeStruct((heads, 1, tokens), F32),
        ),
        in_specs=[pl.BlockSpec(memory_space=pltpu.SMEM)] + [vmem] * (1 + rings),
        out_specs=(vmem, vmem),
        scratch_shapes=[
            pltpu.VMEM((heads, 1, tokens), F32),
            pltpu.VMEM((heads, 1, tokens), F32),
            pltpu.VMEM((heads, head_size, tokens), F32),
        ],
        compiler_params=pltpu.CompilerParams(vmem_limit_bytes=24 << 20),
        cost_estimate=kernel_cost(queries.shape, rings, 2),
    )(info, queries, *pairs)


def attend_back(info, queries, grad_mixed, mixed, log_total, pairs):
    heads, head_size, tokens = queries.shape
    rings = len(pairs)
    vmem = pl.BlockSpec(memory_space=pltpu.VMEM)
    results = pl.pallas_call(
        attend_back_kernel,
        out_shape=(jax.ShapeDtypeStruct(queries.shape, BF16),)
        + tuple(jax.ShapeDtypeStruct(pair.shape, BF16) for pair in pairs),
        in_specs=[pl.BlockSpec(memory_space=pltpu.SMEM)] + [vmem] * (4 + rings),
        out_specs=(vmem,) * (1 + rings),
        scratch_shapes=[
            pltpu.VMEM((heads, 1, tokens), F32),
            pltpu.VMEM((heads, head_size, tokens), F32),
            pltpu.VMEM((2, heads, head_size, tokens), F32),
        ],
        compiler_params=pltpu.CompilerParams(vmem_limit_bytes=32 << 20),
        cost_estimate=kernel_cost(queries.shape, rings, 5),
    )(info, queries, grad_mixed, mixed, log_total, *pairs)
    return results[0], results[1:]


def pair_order(mine, other, bit):
    return jnp.where(
        bit == 0,
        jnp.concatenate([mine, other], axis=0),
        jnp.concatenate([other, mine], axis=0),
    )


def tensor_sum(partial):
    rows = partial.shape[0] // 2
    near = swap(partial[rows:].astype(BF16), "tensor", 1)
    half = (partial[:rows] + near.astype(F32)).astype(BF16)
    far = swap(half, "tensor", 2)
    return half.astype(F32) + far.astype(F32)


def widen(mine):
    return jnp.concatenate([mine, swap(mine, "tensor", 1)], axis=0)


def add_low(kept, got):
    return (kept.astype(F32) + got.astype(F32)).astype(BF16)


def split_sum(first, second):
    cell_size = lax.axis_size("cell")
    seq_index = lax.axis_index("seq")
    if cell_size == 2:
        cell = lax.axis_index("cell")
        kept = add_low(
            jnp.where(cell == 0, first, second),
            swap(jnp.where(cell == 0, second, first), "cell", 1),
        )
    else:
        kept = lax.psum(jnp.stack([first, second]).astype(F32), "cell").astype(BF16)
        kept = kept.reshape((-1,) + first.shape[1:])
    bits = []
    step = 1
    while step < lax.axis_size("seq"):
        bit = (seq_index // step) % 2
        half = kept.shape[0] // 2
        low, high = kept[:half], kept[half:]
        kept = add_low(
            jnp.where(bit == 0, low, high),
            swap(jnp.where(bit == 0, high, low), "seq", step),
        )
        bits.append((step, bit))
        step *= 2
    for step, bit in reversed(bits):
        kept = pair_order(kept, swap(kept, "seq", step), bit)
    if cell_size == 2:
        other = swap(kept, "cell", 1)
        return jnp.where(cell == 0, kept, other), jnp.where(cell == 0, other, kept)
    kept = kept.reshape((2,) + first.shape)
    return kept[0], kept[1]


def small_sum(values):
    values = lax.psum(values, "cell") if lax.axis_size("cell") != 2 else values + swap(values, "cell", 1)
    step = 1
    while step < lax.axis_size("seq"):
        values = values + swap(values, "seq", step)
        step *= 2
    return values


def mm(left, right):
    return jnp.einsum("ab,bc->ac", left, right, preferred_element_type=F32)


def mm_right(left, right):
    return jnp.einsum("ab,cb->ac", left, right, preferred_element_type=F32)


def mm_left(left, right):
    return jnp.einsum("ab,ac->bc", left, right, preferred_element_type=F32)


def shards(
    tokens,
    out_grad,
    group_order,
    lengths,
    qkv_weight,
    qv_bias,
    out_weight,
    out_bias,
    up_weight,
    up_bias,
    down_weight,
    down_bias,
    norm_gain,
    norm_shift,
):
    cell_count, row_count, model_width = tokens.shape
    layer_count = qkv_weight.shape[0]
    local_width = qkv_weight.shape[3]
    head_count = local_width // HEAD
    rings = lax.axis_size("seq")
    half_rows = row_count // 2
    seq_index = lax.axis_index("seq")
    core = lax.axis_index("tensor") % 2
    gains = norm_gain.astype(F32)
    shifts = norm_shift.astype(F32)

    def own_first(values):
        low, high = values[:half_rows], values[half_rows:]
        return jnp.where(core == 0, low, high), jnp.where(core == 0, high, low)

    def flat(values):
        return values.reshape(values.shape[0] * values.shape[1], values.shape[2])

    infos = []
    for cell in range(cell_count):
        slots = [
            2 * ((seq_index - ring) % rings) + (core + half) % 2
            for ring in range(rings)
            for half in range(2)
        ]
        blocks = [lax.dynamic_index_in_dim(group_order[cell], s, 0, False) for s in slots]
        infos.append(jnp.stack(blocks[:2] + [lengths[cell]] + blocks).astype(jnp.int32))

    cells = range(cell_count)
    stream, wide = [None] * cell_count, [None] * cell_count
    for cell in cells:
        mine, other = own_first(tokens[cell])
        stream[cell] = mine.astype(F32)
        both = jnp.concatenate([mine, other], axis=0).astype(F32)
        wide[cell] = (normalize(both)[0] * gains[0, 0] + shifts[0, 0]).astype(BF16)

    kept = [[None] * cell_count for _ in range(layer_count)]
    block_out = [None] * cell_count
    for layer in range(layer_count):
        flat_qkv = qkv_weight[layer]
        for cell in cells:
            normed_one, inverse_one = normalize(stream[cell])
            if layer > 0:
                wide[cell] = widen(
                    (normed_one * gains[layer, 0] + shifts[layer, 0]).astype(BF16)
                )
            wide_one = wide[cell]
            projected = jnp.einsum("td,jde->jet", wide_one, flat_qkv, preferred_element_type=F32)
            shape = (head_count, HEAD, row_count)
            queries = (projected[0] + qv_bias[layer, 0][:, None]).astype(BF16).reshape(shape)
            keys = projected[1].astype(BF16).reshape(shape)
            values = (projected[2] + qv_bias[layer, 1][:, None]).astype(BF16).reshape(shape)
            pairs = [jnp.stack([keys, values])]
            for _ in range(rings - 1):
                pairs.append(shift_right(pairs[-1], "seq"))
            mixed, log_total = attend(infos[cell], queries, pairs)
            flat_mixed = mixed.reshape(local_width, row_count)
            attended = tensor_sum(mm_left(flat_mixed, out_weight[layer]))
            stream_mid = stream[cell] + attended + out_bias[layer]
            normed_two, inverse_two = normalize(stream_mid)
            wide_two = widen((normed_two * gains[layer, 1] + shifts[layer, 1]).astype(BF16))
            hidden, slope = gelu_both(mm(wide_two, up_weight[layer]) + up_bias[layer])
            lowered = tensor_sum(mm(hidden, down_weight[layer]))
            kept[layer][cell] = (
                normed_one,
                inverse_one,
                wide_one,
                queries,
                pairs,
                mixed,
                log_total,
                normed_two,
                inverse_two,
                wide_two,
                hidden,
                slope,
            )
            stream[cell] = stream_mid + lowered + down_bias[layer]
    for cell in cells:
        low = stream[cell].astype(BF16)
        block_out[cell] = pair_order(low, swap(low, "tensor", 1), core)

    grad_stream, grad_wide = [None] * cell_count, [None] * cell_count
    for cell in cells:
        mine, other = own_first(out_grad[cell])
        grad_stream[cell] = mine.astype(F32)
        grad_wide[cell] = jnp.concatenate([mine, other], axis=0)

    per_layer = [None] * layer_count
    row_vectors = [None] * layer_count
    shard_vectors = [None] * layer_count
    for layer in reversed(range(layer_count)):
        state = [dict() for _ in cells]
        for cell in cells:
            (
                normed_one,
                inverse_one,
                wide_one,
                queries,
                pairs,
                mixed,
                log_total,
                normed_two,
                inverse_two,
                wide_two,
                hidden,
                slope,
            ) = kept[layer][cell]
            now = state[cell]
            if grad_wide[cell] is None:
                grad_wide[cell] = widen(grad_stream[cell].astype(BF16))
            grad_down = grad_wide[cell]
            grad_wide[cell] = None
            now["downb"] = jnp.sum(grad_stream[cell], axis=0)
            now["down"] = mm_left(hidden, grad_down)
            grad_hidden = mm_right(grad_down, down_weight[layer]).astype(BF16)
            grad_pre = (grad_hidden.astype(F32) * slope.astype(F32)).astype(BF16)
            now["upb"] = jnp.sum(grad_pre.astype(F32), axis=0)
            now["up"] = mm_left(wide_two, grad_pre)
            grad_two = tensor_sum(mm_right(grad_pre, up_weight[layer]))
            now["gain_two"] = jnp.sum(grad_two * normed_two, axis=0)
            now["shift_two"] = jnp.sum(grad_two, axis=0)
            grad_mid = grad_stream[cell] + norm_back(
                grad_two, normed_two, inverse_two, gains[layer, 1]
            )
            now["outb"] = jnp.sum(grad_mid, axis=0)
            wide_mid = widen(grad_mid.astype(BF16))
            flat_mixed = mixed.reshape(local_width, row_count)
            now["out"] = mm_left(wide_mid, flat_mixed.T)
            grad_mixed = mm_right(out_weight[layer], wide_mid).astype(BF16)
            grad_queries, grad_pairs = attend_back(
                infos[cell], queries, grad_mixed.reshape(mixed.shape), mixed, log_total, pairs
            )
            moving = grad_pairs[1]
            for ring in range(2, rings):
                moving = add_low(grad_pairs[ring], shift_right(moving, "seq"))
            moving = add_low(grad_pairs[0], shift_right(moving, "seq"))
            grads = jnp.concatenate([grad_queries[None], moving], axis=0)
            grads = grads.reshape(3, local_width, row_count)
            sums = jnp.sum(grads.astype(F32), axis=2)
            now["qv"] = jnp.stack([sums[0], sums[2]])
            now["qkv"] = jnp.einsum("td,jet->jde", wide_one, grads, preferred_element_type=F32)
            grad_one = tensor_sum(
                jnp.einsum("jet,jde->td", grads, qkv_weight[layer], preferred_element_type=F32)
            )
            now["gain_one"] = jnp.sum(grad_one * normed_one, axis=0)
            now["shift_one"] = jnp.sum(grad_one, axis=0)
            grad_stream[cell] = grad_mid + norm_back(
                grad_one, normed_one, inverse_one, gains[layer, 0]
            )

        def over_cells(name, state=state):
            return functools.reduce(jnp.add, [now[name] for now in state])

        up, down = split_sum(over_cells("up").astype(BF16), over_cells("down").astype(BF16))
        qkv = over_cells("qkv").astype(BF16)
        out = over_cells("out").astype(BF16)
        first, second = split_sum(
            jnp.concatenate([qkv[0], qkv[1]], axis=0), jnp.concatenate([qkv[2], out], axis=0)
        )
        per_layer[layer] = (
            jnp.stack([first[:model_width], first[model_width:], second[:model_width]]),
            second[model_width:].T,
            up,
            down,
        )
        row_vectors[layer] = jnp.stack(
            [
                over_cells(name)
                for name in ("gain_one", "gain_two", "shift_one", "shift_two", "outb", "downb")
            ]
        )
        shard_vectors[layer] = jnp.concatenate(
            [over_cells("qv").reshape(-1), over_cells("upb")]
        )
    tokens_grad = [None] * cell_count
    for cell in cells:
        low = grad_stream[cell].astype(BF16)
        tokens_grad[cell] = pair_order(low, swap(low, "tensor", 1), core)

    rows = jnp.stack(row_vectors)
    rows = rows + swap(rows, "tensor", 1)
    shards_low = jnp.stack(shard_vectors)
    vector = small_sum(jnp.concatenate([rows.reshape(-1), shards_low.reshape(-1)]))
    rows = vector[: rows.size].reshape(rows.shape)
    shards_low = vector[rows.size :].reshape(shards_low.shape)
    qkv_grad, out_grad_weight, up_grad, down_grad = (
        jnp.stack([per_layer[layer][part] for layer in range(layer_count)]).astype(F32)
        for part in range(4)
    )
    return (
        jnp.stack(block_out),
        jnp.stack(tokens_grad),
        qkv_grad,
        shards_low[:, : 2 * local_width].reshape(layer_count, 2, local_width),
        out_grad_weight,
        rows[:, 4],
        up_grad,
        shards_low[:, 2 * local_width :],
        down_grad,
        rows[:, 5],
        rows[:, 0:2],
        rows[:, 2:4],
    )


def solution(mesh):
    return jax.shard_map(
        shards,
        mesh=mesh,
        in_specs=(
            P("cell", "seq", None),
            P("cell", "seq", None),
            P("cell", None),
            P("cell"),
            P(None, None, None, "tensor"),
            P(None, None, "tensor"),
            P(None, "tensor", None),
            P(),
            P(None, None, "tensor"),
            P(None, "tensor"),
            P(None, "tensor", None),
            P(),
            P(),
            P(),
        ),
        out_specs=(
            P("cell", "seq", None),
            P("cell", "seq", None),
            P(None, None, None, "tensor"),
            P(None, None, "tensor"),
            P(None, "tensor", None),
            P(),
            P(None, None, "tensor"),
            P(None, "tensor"),
            P(None, "tensor", None),
            P(),
            P(),
            P(),
        ),
        check_vma=False,
    )
```

time: 2400 us -> 1080 us (0.45)
  waiting for transfers between devices: 1780 us -> 625 us
  matrix products: 346 us -> 93.3 us
  Pallas kernels: 0 us -> 119 us
  other arithmetic: 184 us -> 110 us
  starting transfers between devices: 3.91 us -> 69.6 us
    psum x2 -> x0, waiting for transfers between devices: 990 us -> none  [shards(): lax.psum((jnp.stack(qkv_grads), jnp.stack(qv_grads), jnp.stack(out_grads)...]
    ppermute x0 -> x100, waiting for transfers between devices: none -> 625 us  [the longest x76 393 us: swap(): return lax.ppermute(values, axis, [(i, i ^ bit) for i in range(size)])]
    reduce_scatter x12 -> x0, waiting for transfers between devices: 479 us -> none  [the longest x8 321 us: total_rows(): lax.psum_scatter(partial_value, 'tensor', scatter_dimension=1, tiled=True)]
    all_gather x14 -> x0, waiting for transfers between devices: 313 us -> none  [the longest x10 198 us: widen(): return lax.all_gather(values, 'tensor', axis=1, tiled=True)]
    dot_general x36 -> x48, matrix products: 346 us -> 93.3 us  [the longest x16 32.9 us: mm_left(): return jnp.einsum('ab,ac->bc', left, right, preferred_element_type=F32)]
    pallas_call x0 -> x8, Pallas kernels: none -> 119 us  [the longest x4 59.5 us: attend_back(): pl.pallas_call(attend_back_kernel, out_shape=(jax.ShapeDtypeStruct(querie...]
    ppermute x0 -> x100, starting transfers between devices: none -> 69.6 us  [the longest x76 52.8 us: swap(): return lax.ppermute(values, axis, [(i, i ^ bit) for i in range(size)])]
    reduce_sum x14 -> x16, other arithmetic: 55.5 us -> 13.4 us  [the longest x4 4.5 us: shards(): now['outb'] = jnp.sum(grad_mid, axis=0)]
  transfers between devices with their start and end apart: 28 -> 100, of which waited for: 25 -> 47; matrix products, arithmetic and copies ran while one was open for 15% -> 20% of each run, Pallas kernels for 0% -> 11%
where the time goes in v1:
time: 1080 us; the launch traced here: 1070 us
  waiting for transfers between devices  625 us (58%)
  Pallas kernels  119 us (11%)
  other arithmetic  110 us (10%)
  matrix products  93.3 us (9%)
  starting transfers between devices  69.6 us (6%)
  local copies, waits for them, and re-layouts  50.5 us (5%)
    ppermute x76, waiting for transfers between devices, swap(): return lax.ppermute(values, axis, [(i, i ^ bit) for i in range(size)])  393 us
    ppermute x24, waiting for transfers between devices, shift_right(): lax.ppermute(values, axis, [(i, (i + 1) % size) for i in range(size)])  231 us
    pallas_call x4, Pallas kernels, attend_back(): pl.pallas_call(attend_back_kernel, out_shape=(jax.ShapeDtypeStruct(querie...  59.5 us
    pallas_call x4, Pallas kernels, attend(): pl.pallas_call(attend_kernel, out_shape=(jax.ShapeDtypeStruct(queries.sha...  59 us
    ppermute x76, starting transfers between devices, swap(): return lax.ppermute(values, axis, [(i, i ^ bit) for i in range(size)])  52.8 us
    dot_general x16, matrix products, mm_left(): return jnp.einsum('ab,ac->bc', left, right, preferred_element_type=F32)  32.9 us
    dot_general x12, matrix products, mm_right(): return jnp.einsum('ab,cb->ac', left, right, preferred_element_type=F32)  23.9 us
  transfers between devices with their start and end apart: 100, of which 47 were waited for; matrix products, arithmetic and copies ran while one was open for 20% of the time, Pallas kernels for 11%

profile of v1, /device:TPU:0, one launch (start us, length us, event | category | flops | bytes accessed | tf_op | source)
XLA Modules:
  0.0 1071.1 jit_solution(12002031803181163368)
XLA Ops:
  19.0 13.0 %collective-permute-done.18.refs_1_ = bf16[2,5,56,512]{3,2,1,0:T(8,128)(2,1)S(1)} collective-permute-done((bf16[2,5,56,512]{3,2,1,0:T(8,128)(2,1)S(1)}, bf16[2,5,56,512]{3,2,1,0:T(8,128)(2,1)S(1)}, u32[]{:S(2)}, u32[]{:S(2)}) %collective-permute-start.18) | collective-permute-done | bytes 573472 | tf_op jit(solution)/shard_map/ppermute | solution.py:27
  32.1 12.3 %collective-permute-done.refs_1_ = bf16[2,5,56,512]{3,2,1,0:T(8,128)(2,1)S(1)} collective-permute-done((bf16[2,5,56,512]{3,2,1,0:T(8,128)(2,1)S(1)}, bf16[2,5,56,512]{3,2,1,0:T(8,128)(2,1)S(1)}, u32[]{:S(2)}, u32[]{:S(2)}) %collective-permute-start) | collective-permute-done | bytes 573472 | tf_op jit(solution)/shard_map/ppermute | solution.py:27
  44.5 12.3 %collective-permute-done.19.refs_2_ = bf16[2,5,56,512]{3,2,1,0:T(8,128)(2,1)} collective-permute-done((bf16[2,5,56,512]{3,2,1,0:T(8,128)(2,1)S(1)}, bf16[2,5,56,512]{3,2,1,0:T(8,128)(2,1)}, u32[]{:S(2)}, u32[]{:S(2)}) %collective-permute-start.19) | collective-permute-done | bytes 573472 | tf_op jit(solution)/shard_map/ppermute | solution.py:27
  84.4 14.7 %shard_map.231 = (bf16[5,56,512]{2,1,0:T(8,128)(2,1)S(1)}, f32[5,1,512]{2,1,0:T(1,128)S(1)}) custom-call(s32[11]{0:T(128)S(1)} %stack.159.info, bf16[5,56,512]{2,1,0:T(8,128)(2,1)S(1)} %get-tuple-element.237.queries, bf16[2,5,56,512]{3,2,1,0:T(8,128)(2,1)S(1)} %pad_maximum_fusion.50.refs_0_, bf16[2,5,56,512]{3,2,1,0:T(8,128)(2,1)S(1)} %collective-permute-done.18.refs_1_, ...), custom_call_target="tpu_custom_call" | custom-call | flops 2684354560 | bytes 2867200 | tf_op jit(solution)/shard_map/pallas_call | solution.py:187
  100.2 14.9 %shard_map.229 = (bf16[5,56,512]{2,1,0:T(8,128)(2,1)S(1)}, f32[5,1,512]{2,1,0:T(1,128)S(1)}) custom-call(s32[11]{0:T(128)S(1)} %stack.156.info, bf16[5,56,512]{2,1,0:T(8,128)(2,1)S(1)} %get-tuple-element.236.queries, bf16[2,5,56,512]{3,2,1,0:T(8,128)(2,1)S(1)} %pad_maximum_fusion.48.refs_0_, bf16[2,5,56,512]{3,2,1,0:T(8,128)(2,1)S(1)} %collective-permute-done.refs_1_, ...), custom_call_target="tpu_custom_call" | custom-call | flops 2684354560 | bytes 2867200 | tf_op jit(solution)/shard_map/pallas_call | solution.py:187
  120.2 12.5 %collective-permute-done.22 = bf16[256,1120]{0,1:T(8,128)(2,1)S(1)} collective-permute-done((bf16[256,1120]{0,1:T(8,128)(2,1)S(1)}, bf16[256,1120]{0,1:T(8,128)(2,1)S(1)}, u32[]{:S(2)}, u32[]{:S(2)}) %collective-permute-start.22) | collective-permute-done | bytes 573472 | tf_op jit(solution)/shard_map/ppermute | solution.py:22
  160.4 12.4 %collective-permute-done.7 = bf16[256,1120]{0,1:T(8,128)(2,1)S(1)} collective-permute-done((bf16[256,1120]{0,1:T(8,128)(2,1)S(1)}, bf16[256,1120]{0,1:T(8,128)(2,1)S(1)}, u32[]{:S(2)}, u32[]{:S(2)}) %collective-permute-start.7) | collective-permute-done | bytes 573472 | tf_op jit(solution)/shard_map/ppermute | solution.py:22
  172.8 11.5 %collective-permute-done.25 = bf16[256,1120]{0,1:T(8,128)(2,1)S(1)} collective-permute-done((bf16[256,1120]{0,1:T(8,128)(2,1)S(1)}, bf16[256,1120]{0,1:T(8,128)(2,1)S(1)}, u32[]{:S(2)}, u32[]{:S(2)}) %collective-permute-start.25) | collective-permute-done | bytes 573472 | tf_op jit(solution)/shard_map/ppermute | solution.py:22
  198.9 14.3 %collective-permute-done.9.refs_1_ = bf16[2,5,56,512]{3,2,1,0:T(8,128)(2,1)S(1)} collective-permute-done((bf16[2,5,56,512]{3,2,1,0:T(8,128)(2,1)S(1)}, bf16[2,5,56,512]{3,2,1,0:T(8,128)(2,1)S(1)}, u32[]{:S(2)}, u32[]{:S(2)}) %collective-permute-start.9) | collective-permute-done | bytes 573472 | tf_op jit(solution)/shard_map/ppermute | solution.py:27
  214.0 11.5 %collective-permute-done.27.refs_1_ = bf16[2,5,56,512]{3,2,1,0:T(8,128)(2,1)S(1)} collective-permute-done((bf16[2,5,56,512]{3,2,1,0:T(8,128)(2,1)S(1)}, bf16[2,5,56,512]{3,2,1,0:T(8,128)(2,1)S(1)}, u32[]{:S(2)}, u32[]{:S(2)}) %collective-permute-start.27) | collective-permute-done | bytes 573472 | tf_op jit(solution)/shard_map/ppermute | solution.py:27
  226.3 11.6 %collective-permute-done.10.refs_2_ = bf16[2,5,56,512]{3,2,1,0:T(8,128)(2,1)} collective-permute-done((bf16[2,5,56,512]{3,2,1,0:T(8,128)(2,1)S(1)}, bf16[2,5,56,512]{3,2,1,0:T(8,128)(2,1)}, u32[]{:S(2)}, u32[]{:S(2)}) %collective-permute-start.10) | collective-permute-done | bytes 573472 | tf_op jit(solution)/shard_map/ppermute | solution.py:27
  238.0 12.2 %collective-permute-done.28.refs_2_ = bf16[2,5,56,512]{3,2,1,0:T(8,128)(2,1)} collective-permute-done((bf16[2,5,56,512]{3,2,1,0:T(8,128)(2,1)S(1)}, bf16[2,5,56,512]{3,2,1,0:T(8,128)(2,1)}, u32[]{:S(2)}, u32[]{:S(2)}) %collective-permute-start.28) | collective-permute-done | bytes 573472 | tf_op jit(solution)/shard_map/ppermute | solution.py:27
  264.2 14.5 %shard_map.230 = (bf16[5,56,512]{2,1,0:T(8,128)(2,1)S(1)}, f32[5,1,512]{2,1,0:T(1,128)S(1)}) custom-call(s32[11]{0:T(128)S(1)} %stack.156.info, bf16[5,56,512]{2,1,0:T(8,128)(2,1)S(1)} %get-tuple-element.232.queries, bf16[2,5,56,512]{3,2,1,0:T(8,128)(2,1)S(1)} %pad_maximum_fusion.49.refs_0_, bf16[2,5,56,512]{3,2,1,0:T(8,128)(2,1)S(1)} %copy-done.18, ...), custom_call_target="tpu_custom_call" | custom-call | flops 2684354560 | bytes 2867200 | tf_op jit(solution)/shard_map/pallas_call | solution.py:187
  279.8 15.0 %shard_map.232 = (bf16[5,56,512]{2,1,0:T(8,128)(2,1)S(1)}, f32[5,1,512]{2,1,0:T(1,128)S(1)}) custom-call(s32[11]{0:T(128)S(1)} %stack.159.info, bf16[5,56,512]{2,1,0:T(8,128)(2,1)S(1)} %get-tuple-element.233.queries, bf16[2,5,56,512]{3,2,1,0:T(8,128)(2,1)S(1)} %pad_maximum_fusion.51.refs_0_, bf16[2,5,56,512]{3,2,1,0:T(8,128)(2,1)S(1)} %copy-done.15, ...), custom_call_target="tpu_custom_call" | custom-call | flops 2684354560 | bytes 2867200 | tf_op jit(solution)/shard_map/pallas_call | solution.py:187
  384.0 11.5 %collective-permute-done.16 = bf16[256,1120]{0,1:T(8,128)(2,1)S(1)} collective-permute-done((bf16[256,1120]{0,1:T(8,128)(2,1)S(1)}, bf16[256,1120]{0,1:T(8,128)(2,1)S(1)}, u32[]{:S(2)}, u32[]{:S(2)}) %collective-permute-start.16) | collective-permute-done | bytes 573472 | tf_op jit(solution)/shard_map/ppermute | solution.py:22
  395.5 12.3 %collective-permute-done.55 = bf16[256,1120]{0,1:T(8,128)(2,1)S(1)} collective-permute-done((bf16[256,1120]{0,1:T(8,128)(2,1)S(1)}, bf16[256,1120]{0,1:T(8,128)(2,1)S(1)}, u32[]{:S(2)}, u32[]{:S(2)}) %collective-permute-start.55) | collective-permute-done | bytes 573472 | tf_op jit(solution)/shard_map/ppermute | solution.py:22
  423.3 14.9 %shard_map.233 = (bf16[5,56,512]{2,1,0:T(8,128)(2,1)S(1)}, bf16[2,5,56,512]{3,2,1,0:T(8,128)(2,1)S(1)}, bf16[2,5,56,512]{3,2,1,0:T(8,128)(2,1)S(1)}, bf16[2,5,56...) custom-call(s32[11]{0:T(128)S(1)} %stack.156.info, bf16[5,56,512]{2,1,0:T(8,128)(2,1)S(1)} %get-tuple-element.232.queries, ...), custom_call_target="tpu_custom_call" | custom-call | flops 6710886400 | bytes 2867200 | tf_op jit(solution)/shard_map/pallas_call | solution.py:209
  439.5 14.8 %shard_map.235 = (bf16[5,56,512]{2,1,0:T(8,128)(2,1)S(1)}, bf16[2,5,56,512]{3,2,1,0:T(8,128)(2,1)S(1)}, bf16[2,5,56,512]{3,2,1,0:T(8,128)(2,1)S(1)}, bf16[2,5,56...) custom-call(s32[11]{0:T(128)S(1)} %stack.159.info, bf16[5,56,512]{2,1,0:T(8,128)(2,1)S(1)} %get-tuple-element.233.queries, ...), custom_call_target="tpu_custom_call" | custom-call | flops 6710886400 | bytes 2867200 | tf_op jit(solution)/shard_map/pallas_call | solution.py:209
  497.2 11.6 %collective-permute-done.41 = bf16[2,5,56,512]{3,2,1,0:T(8,128)(2,1)S(1)} collective-permute-done((bf16[2,5,56,512]{3,2,1,0:T(8,128)(2,1)S(1)}, bf16[2,5,56,512]{3,2,1,0:T(8,128)(2,1)S(1)}, u32[]{:S(2)}, u32[]{:S(2)}) %collective-permute-start.41) | collective-permute-done | bytes 573472 | tf_op jit(solution)/shard_map/ppermute | solution.py:27
  511.3 36.9 %collective-permute-done.59 = bf16[2,5,56,512]{3,2,1,0:T(8,128)(2,1)S(1)} collective-permute-done((bf16[2,5,56,512]{3,2,1,0:T(8,128)(2,1)S(1)}, bf16[2,5,56,512]{3,2,1,0:T(8,128)(2,1)S(1)}, u32[]{:S(2)}, u32[]{:S(2)}) %collective-permute-start.59) | collective-permute-done | bytes 573472 | tf_op jit(solution)/shard_map/ppermute | solution.py:27
  565.0 24.5 %collective-permute-done.96 = bf16[280,1120]{1,0:T(8,128)(2,1)S(1)} collective-permute-done((bf16[280,1120]{1,0:T(8,128)(2,1)S(1)}, bf16[280,1120]{1,0:T(8,128)(2,1)S(1)}, u32[]{:S(2)}, u32[]{:S(2)}) %collective-permute-start.96) | collective-permute-done | bytes 627232 | tf_op jit(solution)/shard_map/ppermute | solution.py:22
  604.0 18.1 %collective-permute-done.97 = bf16[280,1120]{1,0:T(8,128)(2,1)} collective-permute-done((bf16[280,1120]{1,0:T(8,128)(2,1)}, bf16[280,1120]{1,0:T(8,128)(2,1)}, u32[]{:S(2)}, u32[]{:S(2)}) %collective-permute-start.97) | collective-permute-done | bytes 627232 | tf_op jit(solution)/shard_map/ppermute | solution.py:22
  670.2 14.7 %collective-permute-done.81 = bf16[560,280]{0,1:T(8,128)(2,1)S(1)} collective-permute-done((bf16[560,280]{0,1:T(8,128)(2,1)S(1)}, bf16[560,280]{0,1:T(8,128)(2,1)S(1)}, u32[]{:S(2)}, u32[]{:S(2)}) %collective-permute-start.81) | collective-permute-done | bytes 313632 | tf_op jit(solution)/shard_map/ppermute | solution.py:22
  705.0 14.9 %shard_map.236 = (bf16[5,56,512]{2,1,0:T(8,128)(2,1)S(1)}, bf16[2,5,56,512]{3,2,1,0:T(8,128)(2,1)S(1)}, bf16[2,5,56,512]{3,2,1,0:T(8,128)(2,1)S(1)}, bf16[2,5,56...) custom-call(s32[11]{0:T(128)S(1)} %stack.159.info, bf16[5,56,512]{2,1,0:T(8,128)(2,1)S(1)} %copy-done.3, ...), custom_call_target="tpu_custom_call" | custom-call | flops 6710886400 | bytes 2867200 | tf_op jit(solution)/shard_map/pallas_call | solution.py:209
  721.3 14.9 %shard_map.234 = (bf16[5,56,512]{2,1,0:T(8,128)(2,1)S(1)}, bf16[2,5,56,512]{3,2,1,0:T(8,128)(2,1)S(1)}, bf16[2,5,56,512]{3,2,1,0:T(8,128)(2,1)S(1)}, bf16[2,5,56...) custom-call(s32[11]{0:T(128)S(1)} %stack.156.info, bf16[5,56,512]{2,1,0:T(8,128)(2,1)S(1)} %copy-done.1, ...), custom_call_target="tpu_custom_call" | custom-call | flops 6710886400 | bytes 2867200 | tf_op jit(solution)/shard_map/pallas_call | solution.py:209
  740.0 14.0 %collective-permute-done.48 = bf16[2,5,56,512]{3,2,1,0:T(8,128)(2,1)S(1)} collective-permute-done((bf16[2,5,56,512]{3,2,1,0:T(8,128)(2,1)S(1)}, bf16[2,5,56,512]{3,2,1,0:T(8,128)(2,1)S(1)}, u32[]{:S(2)}, u32[]{:S(2)}) %collective-permute-start.48) | collective-permute-done | bytes 573472 | tf_op jit(solution)/shard_map/ppermute | solution.py:27
  757.0 37.6 %collective-permute-done.83 = bf16[2240,280]{0,1:T(8,128)(2,1)S(1)} collective-permute-done((bf16[2240,280]{0,1:T(8,128)(2,1)S(1)}, bf16[2240,280]{0,1:T(8,128)(2,1)S(1)}, u32[]{:S(2)}, u32[]{:S(2)}) %collective-permute-start.83) | collective-permute-done | bytes 1254432 | tf_op jit(solution)/shard_map/ppermute | solution.py:22
  800.4 18.1 %collective-permute-done.68 = bf16[2,5,56,512]{3,2,1,0:T(8,128)(2,1)S(1)} collective-permute-done((bf16[2,5,56,512]{3,2,1,0:T(8,128)(2,1)S(1)}, bf16[2,5,56,512]{3,2,1,0:T(8,128)(2,1)S(1)}, u32[]{:S(2)}, u32[]{:S(2)}) %collective-permute-start.68) | collective-permute-done | bytes 573472 | tf_op jit(solution)/shard_map/ppermute | solution.py:27
  894.1 24.5 %collective-permute-done.86 = f32[16800]{0:T(1024)S(1)} collective-permute-done((f32[16800]{0:T(1024)S(1)}, f32[16800]{0:T(1024)S(1)}, u32[]{:S(2)}, u32[]{:S(2)}) %collective-permute-start.86) | collective-permute-done | bytes 67232 | tf_op jit(solution)/shard_map/ppermute | solution.py:22
  940.0 16.6 %collective-permute-done.75 = bf16[560,280]{0,1:T(8,128)(2,1)S(1)} collective-permute-done((bf16[560,280]{0,1:T(8,128)(2,1)S(1)}, bf16[560,280]{0,1:T(8,128)(2,1)S(1)}, u32[]{:S(2)}, u32[]{:S(2)}) %collective-permute-start.75) | collective-permute-done | bytes 313632 | tf_op jit(solution)/shard_map/ppermute | solution.py:22
  978.9 22.2 %collective-permute-done.92 = bf16[560,1120]{1,0:T(8,128)(2,1)S(1)} collective-permute-done((bf16[560,1120]{1,0:T(8,128)(2,1)S(1)}, bf16[560,1120]{1,0:T(8,128)(2,1)S(1)}, u32[]{:S(2)}, u32[]{:S(2)}) %collective-permute-start.92) | collective-permute-done | bytes 1254432 | tf_op jit(solution)/shard_map/ppermute | solution.py:22
  1012.1 47.3 %collective-permute-done.93 = bf16[1120,1120]{1,0:T(8,128)(2,1)S(1)} collective-permute-done((bf16[1120,1120]{1,0:T(8,128)(2,1)S(1)}, bf16[1120,1120]{1,0:T(8,128)(2,1)S(1)}, u32[]{:S(2)}, u32[]{:S(2)}) %collective-permute-start.93) | collective-permute-done | bytes 2508832 | tf_op jit(solution)/shard_map/ppermute | solution.py:22
  (874 shorter events, 514.4 us)
Async XLA Ops:
  69.0 31.2 %collective-permute-start.2 = (bf16[2,5,56,512]{3,2,1,0:T(8,128)(2,1)S(1)}, bf16[2,5,56,512]{3,2,1,0:T(8,128)(2,1)}, u32[]{:S(2)}, u32[]{:S(2)}) collective-permute-start(bf16[2,5,56,512]{3,2,1,0:T(8,128)(2,1)S(1)} %collective-permute-done.1.refs_2_), channel_id=1, source_target_pairs={{0,4},{4,8},{8,12},{12,0},{1,5},{5,9},{9,13},{13,1},{2,6},{6,10},{... | collective-permute-start | bytes 1720328 | tf_op jit(solution)/shard_map/ppermute | solution.py:27
  367.0 105.1 %collective-permute-start.94 = (bf16[1120,1120]{1,0:T(8,128)(2,1)S(1)}, bf16[1120,1120]{1,0:T(8,128)(2,1)S(1)}, u32[]{:S(2)}, u32[]{:S(2)}) collective-permute-start(bf16[1120,1120]{1,0:T(8,128)(2,1)S(1)} %get-tuple-element.266), channel_id=1, source_target_pairs={{0,16},{16,0},{1,17},{17,1},{2,18},{18,2},{3,19},{19,3},{4,20},{20... | collective-permute-start | bytes 7526408 | tf_op jit(solution)/shard_map/ppermute | solution.py:22
  369.9 37.9 %collective-permute-start.55 = (bf16[256,1120]{0,1:T(8,128)(2,1)S(1)}, bf16[256,1120]{0,1:T(8,128)(2,1)S(1)}, u32[]{:S(2)}, u32[]{:S(2)}) collective-permute-start(bf16[256,1120]{0,1:T(8,128)(2,1)S(1)} %fusion.161), channel_id=1, source_target_pairs={{0,2},{1,3},{2,0},{3,1},{4,6},{5,7},{6,4},{7,5},{8,10},{9,11},{10,... | collective-permute-start | bytes 1720328 | tf_op jit(solution)/shard_map/ppermute | solution.py:22
  372.0 47.2 %collective-permute-start.34 = (bf16[256,1120]{0,1:T(8,128)(2,1)S(1)}, bf16[256,1120]{0,1:T(8,128)(2,1)S(1)}, u32[]{:S(2)}, u32[]{:S(2)}) collective-permute-start(bf16[256,1120]{0,1:T(8,128)(2,1)S(1)} %fusion.166), channel_id=1, source_target_pairs={{0,2},{1,3},{2,0},{3,1},{4,6},{5,7},{6,4},{7,5},{8,10},{9,11},{10,... | collective-permute-start | bytes 1720328 | tf_op jit(solution)/shard_map/ppermute | solution.py:22
  420.1 35.5 %collective-permute-start.35 = (bf16[256,1120]{0,1:T(8,128)(2,1)S(1)}, bf16[256,1120]{0,1:T(8,128)(2,1)S(1)}, u32[]{:S(2)}, u32[]{:S(2)}) collective-permute-start(bf16[256,1120]{0,1:T(8,128)(2,1)S(1)} %get-tuple-element.189), channel_id=1, source_target_pairs={{0,1},{1,0},{2,3},{3,2},{4,5},{5,4},{6,7},{7,6},{8,9},{9,8},{10,11... | collective-permute-start | bytes 1720328 | tf_op jit(solution)/shard_map/ppermute | solution.py:22
  420.2 36.4 %collective-permute-start.17 = (bf16[256,1120]{0,1:T(8,128)(2,1)S(1)}, bf16[256,1120]{0,1:T(8,128)(2,1)S(1)}, u32[]{:S(2)}, u32[]{:S(2)}) collective-permute-start(bf16[256,1120]{0,1:T(8,128)(2,1)S(1)} %get-tuple-element.188), channel_id=1, source_target_pairs={{0,1},{1,0},{2,3},{3,2},{4,5},{5,4},{6,7},{7,6},{8,9},{9,8},{10,11... | collective-permute-start | bytes 1720328 | tf_op jit(solution)/shard_map/ppermute | solution.py:22
  485.6 71.6 %collective-permute-start.95 = (bf16[560,1120]{1,0:T(8,128)(2,1)}, bf16[560,1120]{1,0:T(8,128)(2,1)}, u32[]{:S(2)}, u32[]{:S(2)}) collective-permute-start(bf16[560,1120]{1,0:T(8,128)(2,1)} %broadcast_select_fusion.2), channel_id=1, source_target_pairs={{0,4},{4,0},{8,12},{12,8},{1,5},{5,1},{9,13},{13,9},{2,6},{6,2},{1... | collective-permute-start | bytes 3763208 | tf_op jit(solution)/shard_map/ppermute | solution.py:22
  496.7 51.5 %collective-permute-start.59 = (bf16[2,5,56,512]{3,2,1,0:T(8,128)(2,1)S(1)}, bf16[2,5,56,512]{3,2,1,0:T(8,128)(2,1)S(1)}, u32[]{:S(2)}, u32[]{:S(2)}) collective-permute-start(bf16[2,5,56,512]{3,2,1,0:T(8,128)(2,1)S(1)} %add_convert_fusion.14), channel_id=1, source_target_pairs={{0,4},{4,8},{8,12},{12,0},{1,5},{5,9},{9,13},{13,1},{2,6},{6,10},{... | collective-permute-start | bytes 1720328 | tf_op jit(solution)/shard_map/ppermute | solution.py:27
  511.3 48.8 %collective-permute-start.42 = (bf16[256,1120]{0,1:T(8,128)(2,1)}, bf16[256,1120]{0,1:T(8,128)(2,1)}, u32[]{:S(2)}, u32[]{:S(2)}) collective-permute-start(bf16[256,1120]{0,1:T(8,128)(2,1)} %slice.1005), channel_id=1, source_target_pairs={{0,1},{1,0},{2,3},{3,2},{4,5},{5,4},{6,7},{7,6},{8,9},{9,8},{10,11... | collective-permute-start | bytes 1720328 | tf_op jit(solution)/shard_map/ppermute | solution.py:22
  556.2 41.8 %collective-permute-start.78 = (bf16[2240,280]{0,1:T(8,128)(2,1)}, bf16[2240,280]{0,1:T(8,128)(2,1)}, u32[]{:S(2)}, u32[]{:S(2)}) collective-permute-start(bf16[2240,280]{0,1:T(8,128)(2,1)} %broadcast_select_fusion.6), channel_id=1, source_target_pairs={{0,16},{16,0},{1,17},{17,1},{2,18},{18,2},{3,19},{19,3},{4,20},{20... | collective-permute-start | bytes 3763208 | tf_op jit(solution)/shard_map/ppermute | solution.py:22
  590.5 31.6 %collective-permute-start.97 = (bf16[280,1120]{1,0:T(8,128)(2,1)}, bf16[280,1120]{1,0:T(8,128)(2,1)}, u32[]{:S(2)}, u32[]{:S(2)}) collective-permute-start(bf16[280,1120]{1,0:T(8,128)(2,1)} %add_convert_fusion.6), channel_id=1, source_target_pairs={{0,8},{4,12},{8,0},{12,4},{1,9},{5,13},{9,1},{13,5},{2,10},{6,14},... | collective-permute-start | bytes 1881608 | tf_op jit(solution)/shard_map/ppermute | solution.py:22
  594.3 30.0 %collective-permute-start.44 = (bf16[256,1120]{0,1:T(8,128)(2,1)}, bf16[256,1120]{0,1:T(8,128)(2,1)}, u32[]{:S(2)}, u32[]{:S(2)}) collective-permute-start(bf16[256,1120]{0,1:T(8,128)(2,1)} %convert_element_type.928), channel_id=1, source_target_pairs={{0,1},{1,0},{2,3},{3,2},{4,5},{5,4},{6,7},{7,6},{8,9},{9,8},{10,11... | collective-permute-start | bytes 1720328 | tf_op jit(solution)/shard_map/ppermute | solution.py:22
  597.8 33.5 %collective-permute-start.62 = (bf16[256,1120]{0,1:T(8,128)(2,1)}, bf16[256,1120]{0,1:T(8,128)(2,1)}, u32[]{:S(2)}, u32[]{:S(2)}) collective-permute-start(bf16[256,1120]{0,1:T(8,128)(2,1)} %convert_element_type.981), channel_id=1, source_target_pairs={{0,1},{1,0},{2,3},{3,2},{4,5},{5,4},{6,7},{7,6},{8,9},{9,8},{10,11... | collective-permute-start | bytes 1720328 | tf_op jit(solution)/shard_map/ppermute | solution.py:22
  601.5 45.8 %collective-permute-start.79 = (bf16[1120,280]{0,1:T(8,128)(2,1)S(1)}, bf16[1120,280]{0,1:T(8,128)(2,1)S(1)}, u32[]{:S(2)}, u32[]{:S(2)}) collective-permute-start(bf16[1120,280]{0,1:T(8,128)(2,1)S(1)} %broadcast_select_fusion.12), channel_id=1, source_target_pairs={{0,4},{4,0},{8,12},{12,8},{1,5},{5,1},{9,13},{13,9},{2,6},{6,2},{1... | collective-permute-start | bytes 1881608 | tf_op jit(solution)/shard_map/ppermute | solution.py:22
  624.3 72.1 %collective-permute-start.98 = (bf16[560,1120]{1,0:T(8,128)(2,1)S(1)}, bf16[560,1120]{1,0:T(8,128)(2,1)S(1)}, u32[]{:S(2)}, u32[]{:S(2)}) collective-permute-start(bf16[560,1120]{1,0:T(8,128)(2,1)S(1)} %maximum_select_fusion.5), channel_id=1, source_target_pairs={{0,4},{4,0},{8,12},{12,8},{1,5},{5,1},{9,13},{13,9},{2,6},{6,2},{1... | collective-permute-start | bytes 3763208 | tf_op jit(solution)/shard_map/ppermute | solution.py:22
  631.2 36.3 %collective-permute-start.45 = (bf16[256,1120]{0,1:T(8,128)(2,1)S(1)}, bf16[256,1120]{0,1:T(8,128)(2,1)S(1)}, u32[]{:S(2)}, u32[]{:S(2)}) collective-permute-start(bf16[256,1120]{0,1:T(8,128)(2,1)S(1)} %slice.1004), channel_id=1, source_target_pairs={{0,1},{1,0},{2,3},{3,2},{4,5},{5,4},{6,7},{7,6},{8,9},{9,8},{10,11... | collective-permute-start | bytes 1720328 | tf_op jit(solution)/shard_map/ppermute | solution.py:22
  637.3 32.3 %collective-permute-start.63 = (bf16[256,1120]{0,1:T(8,128)(2,1)S(1)}, bf16[256,1120]{0,1:T(8,128)(2,1)S(1)}, u32[]{:S(2)}, u32[]{:S(2)}) collective-permute-start(bf16[256,1120]{0,1:T(8,128)(2,1)S(1)} %slice.1000), channel_id=1, source_target_pairs={{0,1},{1,0},{2,3},{3,2},{4,5},{5,4},{6,7},{7,6},{8,9},{9,8},{10,11... | collective-permute-start | bytes 1720328 | tf_op jit(solution)/shard_map/ppermute | solution.py:22
  653.9 100.3 %collective-permute-start.88 = (bf16[1120,1120]{1,0:T(8,128)(2,1)S(1)}, bf16[1120,1120]{1,0:T(8,128)(2,1)S(1)}, u32[]{:S(2)}, u32[]{:S(2)}) collective-permute-start(bf16[1120,1120]{1,0:T(8,128)(2,1)S(1)} %get-tuple-element.268), channel_id=1, source_target_pairs={{0,16},{16,0},{1,17},{17,1},{2,18},{18,2},{3,19},{19,3},{4,20},{20... | collective-permute-start | bytes 7526408 | tf_op jit(solution)/shard_map/ppermute | solution.py:22
  699.0 140.6 %collective-permute-start.99 = (bf16[1120,1120]{1,0:T(8,128)(2,1)}, bf16[1120,1120]{1,0:T(8,128)(2,1)}, u32[]{:S(2)}, u32[]{:S(2)}) collective-permute-start(bf16[1120,1120]{1,0:T(8,128)(2,1)} %maximum_select_fusion.1), channel_id=1, source_target_pairs={{0,16},{16,0},{1,17},{17,1},{2,18},{18,2},{3,19},{19,3},{4,20},{20... | collective-permute-start | bytes 7526408 | tf_op jit(solution)/shard_map/ppermute | solution.py:22
  702.6 92.0 %collective-permute-start.83 = (bf16[2240,280]{0,1:T(8,128)(2,1)S(1)}, bf16[2240,280]{0,1:T(8,128)(2,1)S(1)}, u32[]{:S(2)}, u32[]{:S(2)}) collective-permute-start(bf16[2240,280]{0,1:T(8,128)(2,1)S(1)} %maximum_select_fusion.3), channel_id=1, source_target_pairs={{0,16},{16,0},{1,17},{17,1},{2,18},{18,2},{3,19},{19,3},{4,20},{20... | collective-permute-start | bytes 3763208 | tf_op jit(solution)/shard_map/ppermute | solution.py:22
  738.5 57.9 %collective-permute-start.67 = (bf16[2,5,56,512]{3,2,1,0:T(8,128)(2,1)S(1)}, bf16[2,5,56,512]{3,2,1,0:T(8,128)(2,1)S(1)}, u32[]{:S(2)}, u32[]{:S(2)}) collective-permute-start(bf16[2,5,56,512]{3,2,1,0:T(8,128)(2,1)S(1)} %add_convert_fusion.12), channel_id=1, source_target_pairs={{0,4},{4,8},{8,12},{12,0},{1,5},{5,9},{9,13},{13,1},{2,6},{6,10},{... | collective-permute-start | bytes 1720328 | tf_op jit(solution)/shard_map/ppermute | solution.py:27
  754.2 44.5 %collective-permute-start.49 = (bf16[2,5,56,512]{3,2,1,0:T(8,128)(2,1)S(1)}, bf16[2,5,56,512]{3,2,1,0:T(8,128)(2,1)S(1)}, u32[]{:S(2)}, u32[]{:S(2)}) collective-permute-start(bf16[2,5,56,512]{3,2,1,0:T(8,128)(2,1)S(1)} %add_convert_fusion.18), channel_id=1, source_target_pairs={{0,4},{4,8},{8,12},{12,0},{1,5},{5,9},{9,13},{13,1},{2,6},{6,10},{... | collective-permute-start | bytes 1720328 | tf_op jit(solution)/shard_map/ppermute | solution.py:27
  756.5 88.5 %collective-permute-start.89 = (bf16[560,1120]{1,0:T(8,128)(2,1)}, bf16[560,1120]{1,0:T(8,128)(2,1)}, u32[]{:S(2)}, u32[]{:S(2)}) collective-permute-start(bf16[560,1120]{1,0:T(8,128)(2,1)} %broadcast_select_fusion.3), channel_id=1, source_target_pairs={{0,4},{4,0},{8,12},{12,8},{1,5},{5,1},{9,13},{13,9},{2,6},{6,2},{1... | collective-permute-start | bytes 3763208 | tf_op jit(solution)/shard_map/ppermute | solution.py:22
  798.8 30.7 %collective-permute-start.50 = (bf16[2,5,56,512]{3,2,1,0:T(8,128)(2,1)S(1)}, bf16[2,5,56,512]{3,2,1,0:T(8,128)(2,1)S(1)}, u32[]{:S(2)}, u32[]{:S(2)}) collective-permute-start(bf16[2,5,56,512]{3,2,1,0:T(8,128)(2,1)S(1)} %add_convert_fusion.17), channel_id=1, source_target_pairs={{0,4},{4,8},{8,12},{12,0},{1,5},{5,9},{9,13},{13,1},{2,6},{6,10},{... | collective-permute-start | bytes 1720328 | tf_op jit(solution)/shard_map/ppermute | solution.py:27
  838.8 44.7 %collective-permute-start.72 = (bf16[2240,280]{0,1:T(8,128)(2,1)}, bf16[2240,280]{0,1:T(8,128)(2,1)}, u32[]{:S(2)}, u32[]{:S(2)}) collective-permute-start(bf16[2240,280]{0,1:T(8,128)(2,1)} %broadcast_select_fusion.9), channel_id=1, source_target_pairs={{0,16},{16,0},{1,17},{17,1},{2,18},{18,2},{3,19},{19,3},{4,20},{20... | collective-permute-start | bytes 3763208 | tf_op jit(solution)/shard_map/ppermute | solution.py:22
  851.4 29.8 %collective-permute-start.90 = (bf16[280,1120]{1,0:T(8,128)(2,1)}, bf16[280,1120]{1,0:T(8,128)(2,1)}, u32[]{:S(2)}, u32[]{:S(2)}) collective-permute-start(bf16[280,1120]{1,0:T(8,128)(2,1)} %broadcast_select_fusion.11), channel_id=1, source_target_pairs={{0,8},{4,12},{8,0},{12,4},{1,9},{5,13},{9,1},{13,5},{2,10},{6,14},... | collective-permute-start | bytes 1881608 | tf_op jit(solution)/shard_map/ppermute | solution.py:22
  883.4 76.4 %collective-permute-start.91 = (bf16[280,1120]{1,0:T(8,128)(2,1)}, bf16[280,1120]{1,0:T(8,128)(2,1)}, u32[]{:S(2)}, u32[]{:S(2)}) collective-permute-start(bf16[280,1120]{1,0:T(8,128)(2,1)} %add_convert_fusion.7), channel_id=1, source_target_pairs={{0,8},{4,12},{8,0},{12,4},{1,9},{5,13},{9,1},{13,5},{2,10},{6,14},... | collective-permute-start | bytes 1881608 | tf_op jit(solution)/shard_map/ppermute | solution.py:22
  886.9 31.8 %collective-permute-start.73 = (bf16[1120,280]{0,1:T(8,128)(2,1)S(1)}, bf16[1120,280]{0,1:T(8,128)(2,1)S(1)}, u32[]{:S(2)}, u32[]{:S(2)}) collective-permute-start(bf16[1120,280]{0,1:T(8,128)(2,1)S(1)} %broadcast_select_fusion.13), channel_id=1, source_target_pairs={{0,4},{4,0},{8,12},{12,8},{1,5},{5,1},{9,13},{13,9},{2,6},{6,2},{1... | collective-permute-start | bytes 1881608 | tf_op jit(solution)/shard_map/ppermute | solution.py:22
  924.4 39.5 %collective-permute-start.71 = (bf16[256,1120]{0,1:T(8,128)(2,1)}, bf16[256,1120]{0,1:T(8,128)(2,1)}, u32[]{:S(2)}, u32[]{:S(2)}) collective-permute-start(bf16[256,1120]{0,1:T(8,128)(2,1)} %fusion.144), channel_id=1, source_target_pairs={{0,1},{1,0},{2,3},{3,2},{4,5},{5,4},{6,7},{7,6},{8,9},{9,8},{10,11... | collective-permute-start | bytes 1720328 | tf_op jit(solution)/shard_map/ppermute | solution.py:22
  924.4 52.6 %collective-permute-start.53 = (bf16[256,1120]{0,1:T(8,128)(2,1)S(1)}, bf16[256,1120]{0,1:T(8,128)(2,1)S(1)}, u32[]{:S(2)}, u32[]{:S(2)}) collective-permute-start(bf16[256,1120]{0,1:T(8,128)(2,1)S(1)} %copy-done.88), channel_id=1, source_target_pairs={{0,1},{1,0},{2,3},{3,2},{4,5},{5,4},{6,7},{7,6},{8,9},{9,8},{10,11... | collective-permute-start | bytes 1720328 | tf_op jit(solution)/shard_map/ppermute | solution.py:22
  961.8 39.3 %collective-permute-start.92 = (bf16[560,1120]{1,0:T(8,128)(2,1)S(1)}, bf16[560,1120]{1,0:T(8,128)(2,1)S(1)}, u32[]{:S(2)}, u32[]{:S(2)}) collective-permute-start(bf16[560,1120]{1,0:T(8,128)(2,1)S(1)} %maximum_select_fusion.4), channel_id=1, source_target_pairs={{0,4},{4,0},{8,12},{12,8},{1,5},{5,1},{9,13},{13,9},{2,6},{6,2},{1... | collective-permute-start | bytes 3763208 | tf_op jit(solution)/shard_map/ppermute | solution.py:22
  1002.3 57.1 %collective-permute-start.93 = (bf16[1120,1120]{1,0:T(8,128)(2,1)S(1)}, bf16[1120,1120]{1,0:T(8,128)(2,1)S(1)}, u32[]{:S(2)}, u32[]{:S(2)}) collective-permute-start(bf16[1120,1120]{1,0:T(8,128)(2,1)S(1)} %maximum_select_fusion), channel_id=1, source_target_pairs={{0,16},{16,0},{1,17},{17,1},{2,18},{18,2},{3,19},{19,3},{4,20},{20... | collective-permute-start | bytes 7526408 | tf_op jit(solution)/shard_map/ppermute | solution.py:22
  (257 other events, 3191.7 us)

commit v2 on v0

v2 whole, which is shorter than its diff:
```python
import functools
import types

import jax
import jax.numpy as jnp
from jax import lax
from jax.experimental import pallas as pl
from jax.experimental.pallas import tpu as pltpu
from jax.sharding import PartitionSpec as P

HEAD = 56
EPSILON = 1e-05
MASKED = -1e30
ROOT_TWO_PI = 0.7978845608028654
CUBIC = 0.044715
LOG2E = 1.4426950408889634
F32 = jnp.float32
BF16 = jnp.bfloat16
MESH = pl.DeviceIdType.MESH
CELL, SEQ, TENSOR = "cell", "seq", "tensor"
COPIES = 28


def swap(values, axis, bit):
    size = lax.axis_size(axis)
    return lax.ppermute(values, axis, [(i, i ^ bit) for i in range(size)])


def normalize(values):
    centred = values - jnp.mean(values, axis=-1, keepdims=True)
    spread = jnp.mean(centred * centred, axis=-1, keepdims=True)
    inverse = lax.rsqrt(spread + EPSILON)
    return (centred * inverse, inverse)


def norm_back(incoming, normed, inverse, gain_row):
    scaled = incoming * gain_row
    first_mean = jnp.mean(scaled, axis=-1, keepdims=True)
    second_mean = jnp.mean(scaled * normed, axis=-1, keepdims=True)
    return inverse * (scaled - first_mean - normed * second_mean)


def gelu_both(values):
    inner = jnp.tanh(ROOT_TWO_PI * (values + CUBIC * values * values * values))
    hidden = 0.5 * values * (1.0 + inner)
    slope = 0.5 * (1.0 + inner) + 0.5 * values * (1.0 - inner * inner) * ROOT_TWO_PI * (
        1.0 + 3.0 * CUBIC * values * values
    )
    return hidden.astype(BF16), slope.astype(BF16)


def contract(left, right, left_dim, right_dim):
    return lax.dot_general(
        left, right, (((left_dim,), (right_dim,)), ((), ())), preferred_element_type=F32
    )


def mm(left, right):
    return contract(left, right, 1, 0)


def mm_left(left, right):
    return contract(left, right, 0, 0)


def score_block(info, keys, queries, key_block, query_block, masked):
    scores = contract(keys, queries, 0, 0)
    if masked:
        rows = scores.shape[0]
        key_place = key_block * rows + lax.broadcasted_iota(jnp.int32, scores.shape, 0)
        query_place = query_block * rows + lax.broadcasted_iota(jnp.int32, scores.shape, 1)
        allowed = (key_place <= query_place) & (key_place < info[0])
        scores = jnp.where(allowed, scores, MASKED)
    return scores


def for_blocks(info, stream, chunk, block_rows, work):
    def one(step, carry):
        key_half, query_half = step // 2, step % 2
        key_block, query_block = info[5 + 2 * chunk + key_half], info[1 + 2 * stream + query_half]
        key_at = pl.ds(pl.multiple_of(key_half * block_rows, block_rows), block_rows)
        query_at = pl.ds(pl.multiple_of(query_half * block_rows, block_rows), block_rows)
        first = key_block * block_rows
        counts = (key_block <= query_block) & (first < info[0])
        partial = (key_block == query_block) | (first + block_rows > info[0])

        @pl.when(counts & partial)
        def _():
            work(key_at, query_at, key_block, query_block, True)

        @pl.when(counts & jnp.logical_not(partial))
        def _():
            work(key_at, query_at, key_block, query_block, False)

        return carry

    lax.fori_loop(0, 4, one, 0)


def attend_kernel(first_chunk, chunks, streams, resumed, last, info, *refs):
    per_stream = 4 if resumed else 1
    given = [refs[per_stream * i : per_stream * (i + 1)] for i in range(streams)]
    refs = refs[per_stream * streams :]
    pairs, refs = refs[:chunks], refs[chunks:]
    per_output = 2 if last else 3
    results = [refs[per_output * i : per_output * (i + 1)] for i in range(streams)]
    scratch = refs[per_output * streams :]
    heads, head_size, tokens = given[0][0].shape
    rows = tokens // 2
    factor = head_size**-0.5 * LOG2E
    for stream in range(streams):
        queries = given[stream][0]
        top, total, sums = (
            scratch[3 * stream : 3 * stream + 3] if last else results[stream]
        )
        if resumed:
            for kept, start in zip((top, total, sums), given[stream][1:]):
                kept[...] = start[...]
        else:
            top[...] = jnp.full_like(top, MASKED)
            total[...] = jnp.zeros_like(total)
            sums[...] = jnp.zeros_like(sums)
        for chunk in range(chunks):
            pair = pairs[chunk]

            def work(
                key_at,
                query_at,
                key_block,
                query_block,
                masked,
                pair=pair,
                queries=queries,
                top=top,
                total=total,
                sums=sums,
            ):
                for head in range(heads):
                    scores = score_block(
                        info,
                        pair[0, head, :, key_at],
                        queries[head, :, query_at],
                        key_block,
                        query_block,
                        masked,
                    )
                    old = top[head, :, query_at]
                    new = jnp.maximum(old, jnp.max(scores, axis=0, keepdims=True) * factor)
                    decay = jnp.exp2(old - new)
                    weights = jnp.exp2(scores * factor - new)
                    top[head, :, query_at] = new
                    total[head, :, query_at] = total[head, :, query_at] * decay + jnp.sum(
                        weights, axis=0, keepdims=True
                    )
                    sums[head, :, query_at] = sums[head, :, query_at] * decay + contract(
                        pair[1, head, :, key_at], weights.astype(BF16), 1, 0
                    )

            for_blocks(info, stream, first_chunk + chunk, rows, work)
        if last:
            mixed, log_total = results[stream]
            for head in range(heads):
                mixed[head] = (sums[head] / total[head]).astype(BF16)
                log_total[head] = top[head] + jnp.log2(total[head])


def attend_back_kernel(first_chunk, chunks, resumed, info, *refs):
    per_stream = 5 if resumed else 4
    streams = (len(refs) - 2 * chunks - 2) // (per_stream + 1)
    given = [refs[per_stream * i : per_stream * (i + 1)] for i in range(streams)]
    refs = refs[per_stream * streams :]
    pairs, refs = refs[:chunks], refs[chunks:]
    query_sums, refs = refs[:streams], refs[streams:]
    grad_pairs, refs = refs[:chunks], refs[chunks:]
    inner, pair_sums = refs
    heads, head_size, tokens = given[0][0].shape
    rows = tokens // 2
    scale = head_size**-0.5
    factor = scale * LOG2E
    for stream in range(streams):
        _, grad_mixed, mixed = given[stream][:3]
        for head in range(heads):
            inner[stream, head] = jnp.sum(
                grad_mixed[head].astype(F32) * mixed[head].astype(F32), axis=0, keepdims=True
            )
        query_sums[stream][...] = (
            given[stream][4][...] if resumed else jnp.zeros_like(query_sums[stream])
        )
    for chunk in range(chunks):
        pair = pairs[chunk]
        pair_sums[...] = jnp.zeros_like(pair_sums)
        for stream in range(streams):
            queries, grad_mixed, _, log_total = given[stream][:4]

            def work(
                key_at,
                query_at,
                key_block,
                query_block,
                masked,
                pair=pair,
                stream=stream,
                queries=queries,
                grad_mixed=grad_mixed,
                log_total=log_total,
            ):
                for head in range(heads):
                    keys, values = pair[0, head, :, key_at], pair[1, head, :, key_at]
                    query_part = queries[head, :, query_at]
                    grad_part = grad_mixed[head, :, query_at]
                    scores = score_block(info, keys, query_part, key_block, query_block, masked)
                    probs = jnp.exp2(scores * factor - log_total[head, :, query_at])
                    grad_probs = contract(values, grad_part, 0, 0)
                    grad_scores = (
                        probs * (grad_probs - inner[stream, head, :, query_at])
                    ).astype(BF16)
                    pair_sums[1, head, :, key_at] += contract(grad_part, probs.astype(BF16), 1, 1)
                    pair_sums[0, head, :, key_at] += contract(query_part, grad_scores, 1, 1)
                    query_sums[stream][head, :, query_at] += contract(keys, grad_scores, 1, 0)

            for_blocks(info, stream, first_chunk + chunk, rows, work)
        grad_pairs[chunk][0] = (pair_sums[0] * scale).astype(grad_pairs[chunk].dtype)
        grad_pairs[chunk][1] = pair_sums[1].astype(grad_pairs[chunk].dtype)


SMALL_COST = pl.CostEstimate(flops=1 << 20, bytes_accessed=1 << 20, transcendentals=0)


def attend(info, queries, pairs, first_chunk, states, last):
    heads, head_size, tokens = queries[0].shape
    vmem = pl.BlockSpec(memory_space=pltpu.VMEM)
    state = [(heads, 1, tokens), (heads, 1, tokens), (heads, head_size, tokens)]
    operands = []
    for stream, member in enumerate(queries):
        operands.append(member)
        if states is not None:
            operands.extend(states[stream])
    operands.extend(pairs)
    if last:
        shapes = [
            jax.ShapeDtypeStruct((heads, head_size, tokens), BF16),
            jax.ShapeDtypeStruct((heads, 1, tokens), F32),
        ]
    else:
        shapes = [jax.ShapeDtypeStruct(shape, F32) for shape in state]
    results = pl.pallas_call(
        functools.partial(
            attend_kernel, first_chunk, len(pairs), len(queries), states is not None, last
        ),
        out_shape=tuple(shapes * len(queries)),
        in_specs=[pl.BlockSpec(memory_space=pltpu.SMEM)] + [vmem] * len(operands),
        out_specs=(vmem,) * (len(shapes) * len(queries)),
        scratch_shapes=[pltpu.VMEM(shape, F32) for shape in state] * len(queries) if last else [],
        compiler_params=pltpu.CompilerParams(vmem_limit_bytes=24 << 20),
        cost_estimate=SMALL_COST,
    )(info, *operands)
    return [results[len(shapes) * i : len(shapes) * (i + 1)] for i in range(len(queries))]


def attend_back(info, given, pairs, first_chunk, resumed, pair_type):
    heads, head_size, tokens = given[0][0].shape
    vmem = pl.BlockSpec(memory_space=pltpu.VMEM)
    operands = [member for stream in given for member in stream] + list(pairs)
    results = pl.pallas_call(
        functools.partial(attend_back_kernel, first_chunk, len(pairs), resumed),
        out_shape=tuple(
            jax.ShapeDtypeStruct((heads, head_size, tokens), F32) for _ in given
        )
        + tuple(jax.ShapeDtypeStruct(pair.shape, pair_type) for pair in pairs),
        in_specs=[pl.BlockSpec(memory_space=pltpu.SMEM)] + [vmem] * len(operands),
        out_specs=(vmem,) * (len(given) + len(pairs)),
        scratch_shapes=[
            pltpu.VMEM((len(given), heads, 1, tokens), F32),
            pltpu.VMEM((2, heads, head_size, tokens), F32),
        ],
        compiler_params=pltpu.CompilerParams(vmem_limit_bytes=32 << 20),
        cost_estimate=SMALL_COST,
    )(info, *operands)
    return results[: len(given)], results[len(given) :]


def near():
    tensor = lax.axis_index(TENSOR)
    return {TENSOR: tensor + 1 - 2 * lax.rem(tensor, 2)}


def far():
    tensor = lax.axis_index(TENSOR)
    return {TENSOR: tensor + 2 - 4 * lax.rem(tensor // 2, 2)}


def pair():
    seq = lax.axis_index(SEQ)
    return {SEQ: seq + 1 - 2 * lax.rem(seq, 2)}


def pair_far():
    seq = lax.axis_index(SEQ)
    return {SEQ: seq + 2 - 4 * lax.rem(seq // 2, 2)}


def across():
    return {CELL: 1 - lax.axis_index(CELL)}


class Wires:
    def __init__(self, r, partners):
        self.send, self.recv, self.local = r.send, r.recv, r.local
        self.started, self.open = 0, []
        barrier = pltpu.get_barrier_semaphore()
        for partner in partners:
            pl.semaphore_signal(barrier, inc=1, device_id=partner(), device_id_type=MESH)
        pl.semaphore_wait(barrier, len(partners))

    def start(self, source, target, partner):
        at = self.started
        copy = pltpu.make_async_remote_copy(
            src_ref=source,
            dst_ref=target,
            send_sem=self.send.at[at],
            recv_sem=self.recv.at[at],
            device_id=partner(),
            device_id_type=MESH,
        )
        copy.start()
        self.started += 1
        self.open.append(copy)
        return copy

    def sent(self, copy):
        copy.wait_send()
        self.open = [member for member in self.open if member is not copy]

    def finish(self):
        for copy in self.open:
            copy.wait_send()


class Local:
    def __init__(self, r, at, source, target):
        self.copy = pltpu.make_async_copy(source, target, r.local.at[at])
        self.copy.start()
        self.target, self.waited = target, False

    def get(self):
        if not self.waited:
            self.copy.wait()
            self.waited = True
        return self.target


def call_kernel(body, given, in_hbm, results, out_hbm, scratch, collective_id):
    scratch = dict(
        scratch,
        send=pltpu.SemaphoreType.DMA((COPIES,)),
        recv=pltpu.SemaphoreType.DMA((COPIES,)),
        local=pltpu.SemaphoreType.DMA((12,)),
    )
    vmem, hbm = pl.BlockSpec(memory_space=pltpu.VMEM), pl.BlockSpec(memory_space=pl.ANY)
    trees = (given, in_hbm, results, out_hbm, scratch)
    flat = [jax.tree.flatten(tree) for tree in trees]

    def kernel(*refs):
        found, at = {}, 0
        for leaves, tree in flat:
            found.update(jax.tree.unflatten(tree, refs[at : at + len(leaves)]))
            at += len(leaves)
        body(types.SimpleNamespace(**found))

    outs = pl.pallas_call(
        kernel,
        out_shape=tuple(flat[2][0] + flat[3][0]),
        in_specs=[vmem] * len(flat[0][0]) + [hbm] * len(flat[1][0]),
        out_specs=tuple([vmem] * len(flat[2][0]) + [hbm] * len(flat[3][0])),
        scratch_shapes=flat[4][0],
        compiler_params=pltpu.CompilerParams(
            collective_id=collective_id, has_side_effects=True, vmem_limit_bytes=62 << 20
        ),
        cost_estimate=SMALL_COST,
    )(*flat[0][0], *flat[1][0])
    count = len(flat[2][0])
    found = jax.tree.unflatten(flat[2][1], outs[:count])
    found.update(jax.tree.unflatten(flat[3][1], outs[count:]))
    return found


def shape_of(shape, dtype):
    return jax.ShapeDtypeStruct(shape, dtype)


def twice(value):
    return [value, value]


def by_rows(count, work, step=32):
    def one(index, carry):
        work(pl.ds(pl.multiple_of(index * step, step), step))
        return carry

    lax.fori_loop(0, count // step, one, 0)


def by_columns(width, work, step=128):
    def one(index, carry):
        work(pl.ds(pl.multiple_of(index * step, step), step))
        return carry

    lax.fori_loop(0, width // step, one, 0)
    if width % step:
        work(pl.ds(width // step * step, width % step))


def head_rows(source, rows):
    parts = [source[head, :, rows].astype(F32) for head in range(source.shape[0])]
    return jnp.concatenate(parts, axis=0).T


def put_heads(target, rows, values):
    head_size = target.shape[1]
    for head in range(target.shape[0]):
        target[head, :, rows] = values[head * head_size : (head + 1) * head_size].astype(
            target.dtype
        )


class Exchange:
    def __init__(self, wires, part, sent, got):
        self.wires, self.part, self.sent, self.got = wires, part, sent, got
        self.rows = part.shape[0]

    def give(self, values):
        self.sent[0] = values.astype(BF16)
        self.to_near = self.wires.start(self.sent.at[0], self.got.at[0], near)

    def keep(self, values):
        self.part[...] = values

    def join(self):
        self.to_near.wait_recv()

        def work(rows):
            self.sent[1, rows] = (self.part[rows] + self.got[0, rows].astype(F32)).astype(BF16)

        by_rows(self.rows, work)

    def cross(self):
        self.to_far = self.wires.start(self.sent.at[1], self.got.at[1], far)

    def wait(self):
        self.to_far.wait_recv()

    def total(self, rows):
        return self.sent[1, rows].astype(F32) + self.got[1, rows].astype(F32)


class Sum:
    def __init__(self, wires, whole, out, near_sum, got, got_far):
        self.wires, self.whole, self.out = wires, whole, out
        self.near_sum, self.got, self.got_far = near_sum, got, got_far
        self.bit = lax.rem(lax.axis_index(SEQ), 2)
        self.copy = None

    def wait(self):
        if self.copy is not None:
            self.copy.wait_recv()
            self.copy = None

    def add(self, target, left, right):
        def work(columns):
            target[:, columns] = (
                left[:, columns].astype(F32) + right[:, columns].astype(F32)
            ).astype(BF16)

        by_columns(target.shape[1], work)

    def one(self):
        self.copy = self.wires.start(self.whole.at[1 - self.bit], self.got, pair)

    def two(self):
        self.wait()
        self.add(self.near_sum, self.whole.at[self.bit], self.got)
        self.copy = self.wires.start(self.near_sum, self.got_far, pair_far)

    def three(self):
        self.wait()
        mine = self.out.at[self.bit]
        self.add(mine, self.near_sum, self.got_far)
        self.copy = self.wires.start(mine, mine, pair)

    def five(self, everything, rows):
        self.wait()
        target = everything.at[lax.axis_index(CELL), :, rows]
        self.copy = self.wires.start(self.out, target, across)
        return self.out, target


def sum_scratch(rows, width):
    return [pltpu.VMEM((rows, width), BF16)] * 3


def exchange_scratch(half, width, exchanges):
    return dict(
        part=pltpu.VMEM((2, half, width), F32),
        sent=pltpu.VMEM((2 * exchanges, 2, half, width), BF16),
        got=pltpu.VMEM((2 * exchanges, 2, half, width), BF16),
    )


def exchanges_of(r, wires, count):
    return [
        [Exchange(wires, r.part.at[i], r.sent.at[2 * k + i], r.got.at[2 * k + i]) for i in (0, 1)]
        for k in range(count)
    ]


def project(r, i, to_near, weight):
    half = r.wide_one[i].shape[0] // 2
    for part in (0, 1):
        at = pl.ds(part * half, half)
        if part and to_near is not None:
            to_near.wait_recv()
        wide = r.wide_one[i][at]
        for j in range(3):
            values = contract(wide, weight[j], 1, 1) + r.qkv_b[j : j + 1]
            target = r.queries[i] if j == 0 else r.pair[i].at[j - 1]
            put_heads(target, at, values.T)


def side_and_core():
    return lax.axis_index(SEQ) // 2, lax.rem(lax.axis_index(TENSOR), 2)


def core_columns(half, core):
    return pl.ds(pl.multiple_of(core * half, half), half)


def start_kernel(r):
    side, core = side_and_core()
    half = r.stream[0].shape[0]
    own = Local(r, 0, r.tokens.at[side], r.own_tokens)
    weight = Local(r, 1, r.qkv_w.at[0], r.own_qkv)
    wires = Wires(r, (near, pair, pair_far))
    arriving = wires.start(
        r.tokens.at[1 - side, :, core_columns(half, core)], r.got_tokens, pair_far
    )

    def norm(i, part, values):
        r.rows[...] = values.astype(F32).T

        def work(rows):
            stream = r.rows[rows]
            normed, inverse = normalize(stream)
            if part == 0:
                r.stream[i][rows] = stream
                r.normed_one[i][rows] = normed.astype(BF16)
                r.inverse_one[i][rows] = inverse
            to = pl.ds(part * half + rows.start, rows.size)
            r.wide_one[i][to] = (normed * r.gain[...] + r.shift[...]).astype(BF16)

        by_rows(half, work)

    tokens = own.get()
    for part in (0, 1):
        norm(0, part, tokens[:, core_columns(half, lax.rem(core + part, 2))])
    project(r, 0, None, weight.get())
    paired = wires.start(r.pair[0], r.got_pair, pair)
    arriving.wait_recv()
    norm(1, 0, r.got_tokens[...])
    wide = r.wide_one[1]
    to_near = wires.start(wide.at[pl.ds(0, half)], wide.at[pl.ds(half, half)], near)
    project(r, 1, to_near, weight.get())
    paired.wait_recv()
    wires.finish()


def next_shapes(half, width, head_shape):
    return dict(
        stream=twice(shape_of((half, width), F32)),
        wide_one=twice(shape_of((2 * half, width), BF16)),
        normed_one=twice(shape_of((half, width), BF16)),
        inverse_one=twice(shape_of((half, 1), F32)),
        queries=twice(shape_of(head_shape, BF16)),
        pair=twice(shape_of((2,) + head_shape, BF16)),
        got_pair=shape_of((2,) + head_shape, BF16),
    )


def start_call(tokens, qkv_w, qkv_b, gain, shift, head_shape, collective_id):
    _, width, row_count = tokens.shape
    half = row_count // 2
    return call_kernel(
        start_kernel,
        dict(qkv_b=qkv_b, gain=gain, shift=shift),
        dict(tokens=tokens, qkv_w=qkv_w),
        next_shapes(half, width, head_shape),
        {},
        dict(
            own_tokens=pltpu.VMEM((width, row_count), BF16),
            got_tokens=pltpu.VMEM((width, half), BF16),
            own_qkv=pltpu.VMEM(qkv_w.shape[1:], BF16),
            rows=pltpu.VMEM((half, width), F32),
        ),
        collective_id,
    )


def forward_kernel(layer, last, r):
    side, core = side_and_core()
    half = r.base[0].shape[0]
    halves = (pl.ds(0, half), pl.ds(half, half))
    out_w = Local(r, 0, r.out_w.at[layer], r.own_out)
    up_w = Local(r, 1, r.up_w.at[layer], r.own_up)
    down_w = Local(r, 2, r.down_w.at[layer], r.own_down)
    if not last:
        qkv_w = Local(r, 3, r.qkv_w.at[layer + 1], r.own_qkv)
    wires = Wires(r, (near, far) + (() if last else (pair, pair_far)))
    first, second = exchanges_of(r, wires, 2)
    to_near = {}

    def row(index):
        return r.vectors[index : index + 1]

    def norm(i, exchange, base, at, kept, normed_to, inverse_to, wide):
        def work(rows):
            stream = base[rows] + exchange.total(rows) + row(at)
            normed, inverse = normalize(stream)
            kept[rows] = stream
            normed_to[rows] = normed.astype(BF16)
            inverse_to[rows] = inverse
            wide[rows] = (normed * row(at + 1) + row(at + 2)).astype(BF16)

        by_rows(half, work)
        to_near[i] = wires.start(wide.at[halves[0]], wide.at[halves[1]], near)

    def attended(i):
        for part in (1, 0):
            values = mm(head_rows(r.mixed[i], halves[part]).astype(BF16), out_w.get()[...])
            (first[i].give if part else first[i].keep)(values)

    def mid_norm(i):
        norm(
            i, first[i], r.base[i], 0, r.mid.at[i], r.normed_two[i], r.inverse_two[i], r.wide_two[i]
        )

    def feed(i):
        for part in (0, 1):
            if part:
                to_near[i].wait_recv()
            r.wide_part[...] = mm(r.wide_two[i][halves[part]], up_w.get()[...])

            def work(rows, part=part):
                hidden, slope = gelu_both(r.wide_part[rows] + r.up_b[...])
                to = pl.ds(part * half + rows.start, rows.size)
                r.hidden[i][to] = hidden
                r.slope[i][to] = slope

            by_rows(half, work)
        for part in (1, 0):
            values = mm(r.hidden[i][halves[part]], down_w.get()[...])
            (second[i].give if part else second[i].keep)(values)

    def leave(i):
        if last:

            def work(rows):
                r.part[i, rows] = r.mid[i, rows] + second[i].total(rows) + row(3)

            by_rows(half, work)
            r.low[i][...] = r.part[i].T.astype(BF16)
        else:
            norm(
                i, second[i], r.mid.at[i], 3, r.stream[i], r.normed_one[i], r.inverse_one[i],
                r.wide_one[i],
            )
            project(r, i, to_near[i], qkv_w.get())

    for i in (0, 1):
        attended(i)
    first[0].join()
    first[0].cross()
    first[1].join()
    first[0].wait()
    first[1].cross()
    if not last:
        given = wires.start(
            r.out_grad.at[1 - side, :, core_columns(half, core)], r.got_grad, pair_far
        )
    mid_norm(0)
    feed(0)
    second[0].join()
    first[1].wait()
    second[0].cross()
    mid_norm(1)
    feed(1)
    second[1].join()
    second[0].wait()
    second[1].cross()
    leave(0)
    if not last:
        paired = wires.start(r.pair[0], r.got_pair, pair)
    second[1].wait()
    leave(1)
    if not last:
        given.wait_recv()
        paired.wait_recv()
    wires.finish()


def forward_call(given, in_hbm, layer, last, collective_id):
    half, width = given["base"][0].shape
    hidden_width = in_hbm["up_w"].shape[2]
    head_shape = given["mixed"][0].shape
    wide_hidden = shape_of((2 * half, hidden_width), BF16)
    results = dict(
        wide_two=twice(shape_of((2 * half, width), BF16)),
        normed_two=twice(shape_of((half, width), BF16)),
        inverse_two=twice(shape_of((half, 1), F32)),
        hidden=twice(wide_hidden),
        slope=twice(wide_hidden),
    )
    out_hbm = {}
    scratch = dict(
        exchange_scratch(half, width, 2),
        mid=pltpu.VMEM((2, half, width), F32),
        wide_part=pltpu.VMEM((half, hidden_width), F32),
        own_out=pltpu.VMEM(in_hbm["out_w"].shape[1:], BF16),
        own_up=pltpu.VMEM(in_hbm["up_w"].shape[1:], BF16),
        own_down=pltpu.VMEM(in_hbm["down_w"].shape[1:], BF16),
    )
    if last:
        results.update(low=twice(shape_of((width, half), BF16)))
    else:
        results.update(next_shapes(half, width, head_shape))
        out_hbm.update(got_grad=shape_of((width, half), BF16))
        scratch.update(own_qkv=pltpu.VMEM(in_hbm["qkv_w"].shape[1:], BF16))
    return call_kernel(
        functools.partial(forward_kernel, layer, last),
        given,
        in_hbm,
        results,
        out_hbm,
        scratch,
        collective_id,
    )


def backward_kernel(attention, feed, riding, r):
    begin, end = attention is None, feed is None
    side, core = side_and_core()
    half = r.grad_out[0].shape[0]
    halves = (pl.ds(0, half), pl.ds(half, half))
    if begin:
        own = Local(r, 0, r.out_grad.at[side], r.own_grad)
    else:
        qkv_w = Local(r, 1, r.qkv_w.at[attention], r.own_qkv)
    if not end:
        down_w = Local(r, 2, r.down_w.at[feed], r.own_down)
        up_w = Local(r, 3, r.up_w.at[feed], r.own_up)
        out_w = Local(r, 4, r.out_w.at[feed], r.own_out)
    partners = [near, far]
    if begin or riding:
        partners.append(pair_far)
    if riding:
        partners.append(pair)
    wires = Wires(r, partners)
    exchanges = exchanges_of(r, wires, int(not begin) + int(not end))
    to_near = {}
    r.sums[...] = jnp.zeros_like(r.sums)
    if riding:
        rider = Sum(wires, r.whole, r.summed if riding == 2 else None, r.near_sum, r.got_sum, r.got_far)

    def note(index, values):
        r.sums[index : index + 1, : values.shape[1]] += jnp.sum(values, axis=0, keepdims=True)

    def gather(i, exchange):
        scale = HEAD**-0.5
        for part in (1, 0):
            at = halves[part]
            values = None
            for j in range(3):
                target = r.grads[i].at[j]
                for head in range(target.shape[0]):
                    if j == 0:
                        found = r.query_sum[i][head, :, at] * scale
                    else:
                        found = r.pair_sum[i][j - 1, head, :, at] + r.pair_got[i][
                            j - 1, head, :, at
                        ].astype(F32)
                    target[head, :, at] = found.astype(BF16)
                rows = head_rows(target, at)
                if j != 1:
                    index = 7 + j // 2
                    r.sums[index : index + 1, : rows.shape[1]] += jnp.sum(
                        rows, axis=0, keepdims=True
                    )
                product = mm(rows.astype(BF16), qkv_w.get()[j])
                values = product if values is None else values + product
            (exchange.give if part else exchange.keep)(values)

    def norm(i, exchange, base, normed_of, inverse_of, gain, at, wide):
        def work(rows):
            incoming = exchange.total(rows)
            normed = normed_of[rows].astype(F32)
            grad = base[rows] + norm_back(
                incoming, normed, inverse_of[rows], r.gains[gain : gain + 1]
            )
            r.grad_out[i][rows] = grad
            note(at, incoming * normed)
            note(at + 1, incoming)
            note(at + 2, grad)
            if wide is not None:
                wide[rows] = grad.astype(BF16)

        by_rows(half, work)
        if wide is not None:
            to_near[i] = wires.start(wide.at[halves[0]], wide.at[halves[1]], near)

    def first_norm(i):
        norm(
            i, exchanges[0][i], r.grad[i], r.normed_one[i], r.inverse_one[i], 0, 0,
            None if end else r.wide[i],
        )
        if end:
            r.low[i][...] = r.grad_out[i][...].T.astype(BF16)

    def second_norm(i):
        norm(
            i, exchanges[-1][i], r.grad_out[i], r.normed_two[i], r.inverse_two[i], 1, 3,
            r.wide_mid[i],
        )
        for part in (0, 1):
            if part:
                to_near[i].wait_recv()
            values = contract(out_w.get()[...], r.wide_mid[i][halves[part]], 1, 1)
            put_heads(r.mixed_grad[i], halves[part], values)

    def first_rows(i):
        if i == 0:
            given = own.get()
            for part in (0, 1):
                values = given[:, core_columns(half, lax.rem(core + part, 2))].astype(F32).T
                if part == 0:
                    r.grad_out[0][...] = values
                r.wide[0][halves[part]] = values.astype(BF16)
        else:
            r.grad_out[1][...] = r.got_grad[...].astype(F32).T
            wide = r.wide[1]
            wide[halves[0]] = r.grad_out[1][...].astype(BF16)
            to_near[1] = wires.start(wide.at[halves[0]], wide.at[halves[1]], near)
        by_rows(half, lambda rows: note(2, r.grad_out[i][rows]))

    def slide(i, exchange):
        wide = r.wide[i]
        for part in (0, 1):
            if part and i in to_near:
                to_near[i].wait_recv()
            r.wide_part[...] = contract(wide[halves[part]], down_w.get()[...], 1, 1)

            def work(rows, part=part):
                to = pl.ds(part * half + rows.start, rows.size)
                hidden = r.wide_part[rows].astype(BF16).astype(F32)
                pre = (hidden * r.slope[i][to].astype(F32)).astype(BF16)
                r.pre[i][to] = pre
                note(6, pre.astype(F32))

            by_rows(half, work)
        for part in (1, 0):
            values = contract(r.pre[i][halves[part]], up_w.get()[...], 1, 1)
            (exchange.give if part else exchange.keep)(values)

    def ride(step):
        if riding and step == 0:
            rider.one()
        elif riding and step == 1:
            rider.two()
        elif riding and step == 5:
            rider.wait()
        elif riding == 2 and step == 3:
            rider.three()

    ride(0)
    if begin:
        (after,) = exchanges
        placed = place_cells(r, wires, r.block, r.block_low)
        for i in (0, 1):
            first_rows(i)
            slide(i, after[i])
            after[i].join()
            if i == 1:
                after[0].wait()
            after[i].cross()
        second_norm(0)
        placed.forward()
        after[1].wait()
        second_norm(1)
        placed.finish()
    else:
        before, after = exchanges[0], exchanges[-1]
        a, b = (1, 0) if end else (0, 1)
        gather(a, before[a])
        gather(b, before[b])
        before[a].join()
        before[a].cross()
        before[b].join()
        before[a].wait()
        before[b].cross()
        ride(1)
        first_norm(a)
        if end:
            before[b].wait()
            first_norm(b)
        else:
            slide(a, after[a])
            after[a].join()
            before[b].wait()
            after[a].cross()
            first_norm(b)
            slide(b, after[b])
            after[b].join()
            after[a].wait()
            after[b].cross()
            ride(3)
            second_norm(a)
            after[b].wait()
            second_norm(b)
    ride(5)
    wires.finish()


class place_cells:
    def __init__(self, r, wires, target, low):
        side, core = side_and_core()
        half = low[0].shape[1]
        self.wires = wires
        columns = core_columns(half, core)
        self.own = target.at[side, :, columns]
        self.arrived = target.at[1 - side, :, columns]
        self.local = Local(r, 11, low[0], self.own)
        self.to_far = wires.start(low[1], self.own, pair_far)
        self.to_near = wires.start(low[0], self.own, near)

    def forward(self):
        self.to_far.wait_recv()
        self.second = self.wires.start(self.arrived, self.arrived, near)

    def finish(self):
        self.local.get()
        self.to_near.wait_recv()
        self.second.wait_recv()


def backward_call(given, in_hbm, attention, feed, riding, collective_id):
    begin, end = attention is None, feed is None
    some = given["block_low"][0] if begin else given["grad"][0]
    width = given["gains"].shape[1]
    half = some.shape[1] if begin else some.shape[0]
    results = dict(sums=shape_of((16, width), F32), grad_out=twice(shape_of((half, width), F32)))
    wide = twice(shape_of((2 * half, width), BF16))
    out_hbm = {}
    scratch = exchange_scratch(half, width, int(not begin) + int(not end))
    if begin:
        out_hbm.update(block=shape_of((2, width, 2 * half), BF16))
        scratch.update(own_grad=pltpu.VMEM((width, 2 * half), BF16))
    else:
        head_shape = given["query_sum"][0].shape
        results.update(grads=twice(shape_of((3,) + head_shape, BF16)))
        scratch.update(own_qkv=pltpu.VMEM(in_hbm["qkv_w"].shape[1:], BF16))
    if end:
        results.update(low=twice(shape_of((width, half), BF16)))
    else:
        hidden_width = in_hbm["up_w"].shape[2]
        head_count = in_hbm["out_w"].shape[1] // HEAD
        results.update(
            wide=wide,
            wide_mid=wide,
            pre=twice(shape_of((2 * half, hidden_width), BF16)),
            mixed_grad=twice(shape_of((head_count, HEAD, 2 * half), BF16)),
        )
        scratch.update(
            wide_part=pltpu.VMEM((half, hidden_width), F32),
            own_out=pltpu.VMEM(in_hbm["out_w"].shape[1:], BF16),
            own_up=pltpu.VMEM(in_hbm["up_w"].shape[1:], BF16),
            own_down=pltpu.VMEM(in_hbm["down_w"].shape[1:], BF16),
        )
    if riding:
        whole = given["whole"]
        one = pltpu.VMEM(whole.shape[1:], BF16)
        if riding == 2:
            results.update(summed=shape_of(whole.shape, BF16))
            scratch.update(near_sum=one, got_far=one)
        else:
            part = shape_of(whole.shape[1:], BF16)
            results.update(near_sum=part, got_far=part)
        scratch.update(got_sum=one)
    return call_kernel(
        functools.partial(backward_kernel, attention, feed, riding),
        given,
        in_hbm,
        results,
        out_hbm,
        scratch,
        collective_id,
    )


def closing_kernel(sums_too, r):
    wires = Wires(r, [near, pair, pair_far] + ([across] if sums_too else []))
    cell = lax.axis_index(CELL)
    kernels = r.vectors.shape[0]
    r.total[...] = r.vectors[...]

    def vectors(at, partner, own_rows=16):
        copy = wires.start(r.total, r.around.at[at], partner)

        def add():
            copy.wait_recv()
            wires.sent(copy)
            for kernel in range(kernels):
                r.total[kernel, :own_rows] += r.around[at, kernel, :own_rows]

        return add

    if sums_too:
        span = r.sum_feed[0].shape[1]
        spans = [pl.ds(0, span), pl.ds(span, r.all_feed.shape[2] - span)]
        whole = pl.ds(0, r.all_last.shape[2])
        arriving = wires.start(r.sent_last, r.got_last, across)
        feed = [
            Sum(wires, r.whole_feed[k], r.sum_feed[k], *r.riding_feed[k]) for k in (0, 1)
        ]
        last = Sum(wires, r.whole_last, r.sum_last, *r.riding_last)
        late = Sum(wires, r.whole_late, r.sum_late, *r.riding_late)
        prior = Sum(wires, None, r.sum_prior, r.near_prior, None, r.far_prior)
        local = []

        def fold(target, kept, got, rows):
            def work(columns):
                target[:, :, columns] = (
                    kept[:, rows, columns].astype(F32) + got[:, rows, columns].astype(F32)
                ).astype(BF16)

            by_columns(kept.shape[2], work)

        def five(member, everything, rows):
            own, target = member.five(everything, rows)
            local.append(Local(r, len(local), own, target))

        fold(r.whole_feed[0], r.kept_feed, r.got_feed, spans[0])
        feed[0].one()
        prior.three()
        late.one()
        placed = place_cells(r, wires, r.tokens_grad, r.low)
        add = vectors(0, near, 6)
        local.append(Local(r, 0, r.early, r.all_late.at[cell, :, spans[0]]))
        local.append(Local(r, 1, r.got_early, r.all_late.at[1 - cell, :, spans[0]]))
        fold(r.whole_feed[1], r.kept_feed, r.got_feed, spans[1])
        feed[0].two()
        feed[1].one()
        add()
        add = vectors(1, across)
        late.two()
        five(prior, r.all_prior, whole)
        arriving.wait_recv()
        fold(r.whole_last, r.kept_last, r.got_last, whole)
        last.one()
        add()
        add = vectors(2, pair)
        feed[1].two()
        feed[0].three()
        placed.forward()
        add()
        add = vectors(3, pair_far)
        last.two()
        late.three()
        feed[1].three()
        add()
        five(feed[0], r.all_feed, spans[0])
        five(late, r.all_late, spans[1])
        last.three()
        five(feed[1], r.all_feed, spans[1])
        five(last, r.all_last, whole)
        for member in feed + [late, prior, last]:
            member.wait()
        for copy in local:
            copy.get()
    else:
        placed = place_cells(r, wires, r.tokens_grad, r.low)
        vectors(0, near, 6)()
        placed.forward()
        vectors(1, pair)()
        vectors(2, pair_far)()
    r.totals[...] = r.total[...]
    placed.finish()
    wires.finish()


def closing_call(given, in_hbm, sums_too, collective_id):
    width, half = given["low"][0].shape
    vectors = given["vectors"].shape
    results = dict(totals=shape_of(vectors, F32))
    out_hbm = dict(tokens_grad=shape_of((2, width, 2 * half), BF16))
    scratch = dict(total=pltpu.VMEM(vectors, F32), around=pltpu.VMEM((4,) + vectors, F32))
    if sums_too:
        feed, last = given["kept_feed"].shape, given["kept_last"].shape
        late = given["whole_late"].shape
        early = (feed[0], feed[1] - late[1]) + feed[2:]
        spans = [pltpu.VMEM(early, BF16), pltpu.VMEM(late, BF16)]
        out_hbm.update(
            all_feed=shape_of((2,) + feed, BF16),
            all_late=shape_of((2,) + feed, BF16),
            all_last=shape_of((2,) + last, BF16),
            all_prior=shape_of((2,) + last, BF16),
        )
        scratch.update(
            whole_feed=spans,
            sum_feed=spans,
            riding_feed=[sum_scratch(*early[1:]), sum_scratch(*late[1:])],
            sum_late=spans[1],
            riding_late=sum_scratch(*late[1:]),
            whole_last=pltpu.VMEM(last, BF16),
            sum_last=pltpu.VMEM(last, BF16),
            got_last=pltpu.VMEM(last, BF16),
            riding_last=sum_scratch(*last[1:]),
            sum_prior=pltpu.VMEM(last, BF16),
        )
    return call_kernel(
        functools.partial(closing_kernel, sums_too),
        given,
        in_hbm,
        results,
        out_hbm,
        scratch,
        collective_id,
    )


class Line:
    def __init__(self):
        self.last = None

    def run(self, step, *operands):
        if self.last is not None:
            operands, _ = lax.optimization_barrier((operands, self.last))
        results = step(*operands)
        self.last = jax.tree.leaves(results)[0]
        return types.SimpleNamespace(**results) if isinstance(results, dict) else results


def add_low(kept, got):
    return (kept.astype(F32) + got.astype(F32)).astype(BF16)


def pick(cell, low, high):
    first, second = jnp.stack(low), jnp.stack(high)
    return jnp.where(cell == 0, first, second), jnp.where(cell == 0, second, first)


def two_sum(product, left, right):
    return (product(left[0], right[0]) + product(left[1], right[1])).astype(BF16)


def feed_sums(hidden, grad_down, wide_two, pre_grad):
    up, down = two_sum(mm_left, wide_two, pre_grad), two_sum(mm_left, hidden, grad_down)
    return [part for whole in (up, down) for part in jnp.split(whole, 2, axis=0)]


def attention_sums(wide_mid, mixed, wide_one, grads):
    def product(left, right):
        return mm(left.reshape(left.shape[0] * left.shape[1], left.shape[2]), right)

    return [two_sum(product, [grad[j] for grad in grads], wide_one) for j in range(3)] + [
        two_sum(product, mixed, wide_mid)
    ]


def shards(
    tokens,
    out_grad,
    group_order,
    lengths,
    qkv_weight,
    qv_bias,
    out_weight,
    out_bias,
    up_weight,
    up_bias,
    down_weight,
    down_bias,
    norm_gain,
    norm_shift,
):
    layer_count = qkv_weight.shape[0]
    local_width = qkv_weight.shape[3]
    seq_index = lax.axis_index(SEQ)
    cell = lax.axis_index(CELL)
    core = lax.axis_index(TENSOR) % 2
    side = seq_index // 2
    paired_cells = lax.axis_size(CELL) == 2
    gains, shifts = norm_gain.astype(F32), norm_shift.astype(F32)
    row_count = tokens.shape[1]
    head_shape = (local_width // HEAD, HEAD, row_count)
    tokens, out_grad = jnp.swapaxes(tokens, 1, 2), jnp.swapaxes(out_grad, 1, 2)
    qkv_weight = jnp.swapaxes(qkv_weight, 2, 3)
    biases = qv_bias.astype(F32)
    qkv_bias = jnp.stack([biases[:, 0], jnp.zeros_like(biases[:, 0]), biases[:, 1]], axis=1)
    line = Line()

    order = jnp.where(side == 0, group_order[0], group_order[1])
    length = jnp.where(side == 0, lengths[0], lengths[1])
    offsets = jnp.array([0, 2, 0, 2, 1, 3], jnp.int32)
    slots = 2 * (seq_index ^ offsets)[:, None] + (core + jnp.arange(2)[None]) % 2
    wanted = slots.reshape(-1, 1) == jnp.arange(order.shape[0])[None]
    blocks = jnp.sum(jnp.where(wanted, order[None], 0), axis=1)
    info = jnp.concatenate([length[None], blocks]).astype(jnp.int32)

    weights = dict(out_w=out_weight, up_w=up_weight, down_w=down_weight)
    now = line.run(
        lambda *given: start_call(*given, head_shape, 0),
        tokens,
        qkv_weight,
        qkv_bias[0],
        gains[0, :1],
        shifts[0, :1],
    )
    saved = []
    for layer in range(layer_count):
        last = layer == layer_count - 1
        got_pair = swap(now.pair[1], SEQ, 1)
        states = line.run(
            lambda queries, *pairs: attend(info, queries, pairs, 0, None, False),
            now.queries,
            *now.pair,
            now.got_pair,
        )
        mixed = line.run(
            lambda queries, states, pair: attend(info, queries, [pair], 3, states, True),
            now.queries,
            states,
            got_pair,
        )
        rows = [out_bias[layer], gains[layer, 1], shifts[layer, 1], down_bias[layer]]
        given = dict(
            base=now.stream,
            mixed=[mixed[0][0], mixed[1][0]],
            up_b=up_bias[layer].astype(F32)[None],
        )
        in_hbm = dict(weights)
        if not last:
            rows += [gains[layer + 1, 0], shifts[layer + 1, 0]]
            in_hbm.update(qkv_w=qkv_weight, out_grad=out_grad)
            given.update(qkv_b=qkv_bias[layer + 1])
        given.update(vectors=jnp.stack([row.astype(F32) for row in rows]))
        found = line.run(
            lambda given, in_hbm, layer=layer, last=last: forward_call(
                given, in_hbm, layer, last, 1 + layer
            ),
            given,
            in_hbm,
        )
        saved.append(
            types.SimpleNamespace(
                queries=now.queries,
                near_pairs=now.pair,
                far_pairs=[now.got_pair, got_pair],
                wide_one=now.wide_one,
                normed_one=now.normed_one,
                inverse_one=now.inverse_one,
                mixed=[mixed[0][0], mixed[1][0]],
                log_total=[mixed[0][1], mixed[1][1]],
                wide_two=found.wide_two,
                normed_two=found.normed_two,
                inverse_two=found.inverse_two,
                hidden=found.hidden,
                slope=found.slope,
            )
        )
        if not last:
            got_grad = found.got_grad
            now = found

    identity = layer_count + 1
    block_low = found.low
    vectors = []
    halves = {}
    for layer in reversed(range(layer_count + 1)):
        begin, end = layer == layer_count, layer == 0
        given, in_hbm = dict(), dict()
        gain_rows = [gains[0, 0], gains[0, 0]]
        riding = 0
        if begin:
            given.update(got_grad=got_grad, block_low=block_low)
            in_hbm.update(out_grad=out_grad)
        else:
            above = saved[layer]
            given.update(
                grad=found.grad_out,
                query_sum=query_sums,
                pair_sum=near_sums,
                pair_got=far_got,
                normed_one=above.normed_one,
                inverse_one=above.inverse_one,
            )
            in_hbm.update(qkv_w=qkv_weight)
            gain_rows[0] = gains[layer, 0]
            if paired_cells:
                given.update(whole=line.run(add_low, *pending))
                riding = 1 if end else 2
        if not end:
            below = saved[layer - 1]
            given.update(
                slope=below.slope, normed_two=below.normed_two, inverse_two=below.inverse_two
            )
            in_hbm.update(weights)
            gain_rows[1] = gains[layer - 1, 1]
        given.update(gains=jnp.stack(gain_rows))
        found = line.run(
            lambda given, in_hbm, layer=layer, riding=riding: backward_call(
                given,
                in_hbm,
                layer if layer < layer_count else None,
                layer - 1 if layer > 0 else None,
                riding,
                identity + layer,
            ),
            given,
            in_hbm,
        )
        vectors.append(found.sums)
        if begin:
            block_out = found.block
        else:
            if riding == 2:
                early = found.summed
                got_early = swap(early, CELL, 1)
                late = line.run(add_low, *late)
            sums = line.run(attention_sums, wide_mid, above.mixed, above.wide_one, found.grads)
            if paired_cells:
                kept, sent = line.run(functools.partial(pick, cell), sums[:2], sums[2:])
                if not end:
                    pending = [kept, swap(sent, CELL, 1)]
            else:
                halves[layer, 1] = sums
        if end:
            break
        wide_mid = found.wide_mid
        sums = line.run(feed_sums, below.hidden, found.wide, below.wide_two, found.pre)
        if paired_cells:
            kept_feed, sent_feed = line.run(functools.partial(pick, cell), sums[:2], sums[2:])
            if begin:
                cut = kept_feed.shape[1] // 32 * 16 + 16
                pending = [kept_feed[:, :cut], swap(sent_feed[:, :cut], CELL, 1)]
                late = [kept_feed[:, cut:], swap(sent_feed[:, cut:], CELL, 1)]
            else:
                got_feed = swap(sent_feed, CELL, 1)
        else:
            halves[layer - 1, 0] = sums
        streams = [
            list(members)
            for members in zip(below.queries, found.mixed_grad, below.mixed, below.log_total)
        ]
        query_sums, far_sums = line.run(
            lambda given, pairs: attend_back(info, given, pairs, 2, False, BF16),
            streams,
            below.far_pairs,
        )
        far_got = [swap(far_sum, SEQ, 1) for far_sum in far_sums]
        streams = [members + [start] for members, start in zip(streams, query_sums)]
        query_sums, near_sums = line.run(
            lambda given, pairs: attend_back(info, given, pairs, 0, True, F32),
            streams,
            below.near_pairs,
        )

    vectors = jnp.stack(vectors)
    if not paired_cells:
        vectors = lax.psum(vectors, CELL)
    given, in_hbm = dict(low=found.low, vectors=vectors), dict()
    if paired_cells:
        given.update(
            kept_feed=kept_feed,
            got_feed=got_feed,
            kept_last=kept,
            sent_last=sent,
            whole_late=late,
            near_prior=found.near_sum,
            far_prior=found.got_far,
        )
        in_hbm.update(early=early, got_early=got_early)
    closing = line.run(
        lambda given, in_hbm: closing_call(given, in_hbm, paired_cells, identity + layer_count + 1),
        given,
        in_hbm,
    )
    if paired_cells:
        feeds = [closing.all_feed, closing.all_late]
        attentions = [closing.all_last, closing.all_prior]
    else:

        def whole(part):
            found = []
            for layer in range(layer_count):
                total = lax.psum(jnp.stack(halves[layer, part]).astype(F32), (CELL, SEQ))
                found.append(total.reshape((2, 2) + total.shape[1:]))
            return found

        feeds, attentions = whole(0), whole(1)

    def final(pieces):
        return jnp.stack([piece.astype(F32) for piece in pieces])

    def square(member):
        return member.reshape(member.shape[0] * member.shape[1], member.shape[2])

    totals = closing.totals
    attention_rows = [totals[layer_count - layer] for layer in range(layer_count)]
    feed_rows = [totals[layer_count - 1 - layer] for layer in range(layer_count)]

    def rows_of(members, *indices):
        return jnp.stack([member[index] for member in members for index in indices])

    gain_grad = jnp.stack([rows_of(attention_rows, 0), rows_of(feed_rows, 3)], axis=1)
    shift_grad = jnp.stack([rows_of(attention_rows, 1), rows_of(feed_rows, 4)], axis=1)
    qv_grad = rows_of(attention_rows, 7, 8)[:, :local_width]
    return (
        jnp.swapaxes(block_out, 1, 2),
        jnp.swapaxes(closing.tokens_grad, 1, 2),
        jnp.swapaxes(
            final([jnp.stack([*member[0], member[1, 0]]) for member in attentions]), 2, 3
        ),
        qv_grad.reshape(layer_count, 2, local_width),
        final([member[1, 1] for member in attentions]),
        rows_of(feed_rows, 5),
        final([square(member[0]) for member in feeds]),
        rows_of(feed_rows, 6),
        final([square(member[1]) for member in feeds]),
        rows_of(feed_rows, 2),
        gain_grad,
        shift_grad,
    )


def solution(mesh):
    shared, by_tensor = P(), P(None, TENSOR)
    rows, last = P(CELL, SEQ, None), P(None, None, TENSOR)
    middle = P(None, TENSOR, None)
    weights = (P(None, None, None, TENSOR), last, middle, shared, last, by_tensor, middle)
    norms = (shared, shared, shared)
    return jax.shard_map(
        shards,
        mesh=mesh,
        in_specs=(rows, rows, P(CELL, None), P(CELL)) + weights + norms,
        out_specs=(rows, rows) + weights + norms,
        check_vma=False,
    )
```

time: 2400 us -> 896 us (0.37)
  waiting for transfers between devices: 1780 us -> 13.1 us
  Pallas kernels: 0 us -> 750 us
  matrix products: 346 us -> 24.4 us
  other arithmetic: 184 us -> 34 us
    psum x2 -> x0, waiting for transfers between devices: 990 us -> none  [shards(): lax.psum((jnp.stack(qkv_grads), jnp.stack(qv_grads), jnp.stack(out_grads)...]
    pallas_call x0 -> x15, Pallas kernels: none -> 750 us  [the longest x7 636 us: call_kernel(): pl.pallas_call(kernel, out_shape=tuple(flat[2][0] + flat[3][0]), in_specs...]
    reduce_scatter x12 -> x0, waiting for transfers between devices: 479 us -> none  [the longest x8 321 us: total_rows(): lax.psum_scatter(partial_value, 'tensor', scatter_dimension=1, tiled=True)]
    dot_general x36 -> x24, matrix products: 346 us -> 24.4 us  [contract(): lax.dot_general(left, right, (((left_dim,), (right_dim,)), ((), ())), pre...]
    all_gather x14 -> x0, waiting for transfers between devices: 313 us -> none  [the longest x10 198 us: widen(): return lax.all_gather(values, 'tensor', axis=1, tiled=True)]
    convert_element_type x17 -> x7, other arithmetic: 87.6 us -> 8.36 us  [the longest x3 6.33 us: add_low(): return (kept.astype(F32) + got.astype(F32)).astype(BF16)]
    reduce_sum x22 -> x1, other arithmetic: 63 us -> 0.09 us  [shards(): blocks = jnp.sum(jnp.where(wanted, order[None], 0), axis=1)]
  transfers between devices with their start and end apart: 28 -> 11, of which waited for: 25 -> 2; matrix products, arithmetic and copies ran while one was open for 15% -> 3% of each run, Pallas kernels for 0% -> 26%
where the time goes in v2:
time: 896 us; the launch traced here: 887 us
  Pallas kernels  750 us (84%)
  local copies, waits for them, and re-layouts  51.9 us (6%)
  other arithmetic  34 us (4%)
  matrix products  24.4 us (3%)
  waiting for transfers between devices  13.1 us (1%)
  starting transfers between devices  10.9 us (1%)
    pallas_call x7, Pallas kernels, call_kernel(): pl.pallas_call(kernel, out_shape=tuple(flat[2][0] + flat[3][0]), in_specs...  636 us
    pallas_call x4, Pallas kernels, attend_back(): pl.pallas_call(functools.partial(attend_back_kernel, first_chunk, len(pai...  57.2 us
    pallas_call x4, Pallas kernels, attend(): pl.pallas_call(functools.partial(attend_kernel, first_chunk, len(pairs),...  56.4 us
    unnamed x188, local copies, waits for them, and re-layouts  34.6 us
    dot_general x24, matrix products, contract(): lax.dot_general(left, right, (((left_dim,), (right_dim,)), ((), ())), pre...  24.4 us
  transfers between devices with their start and end apart: 11, of which 2 were waited for; matrix products, arithmetic and copies ran while one was open for 3% of the time, Pallas kernels for 26%

profile of v2, /device:TPU:0, one launch (start us, length us, event | category | flops | bytes accessed | tf_op | source)
XLA Modules:
  0.0 887.2 jit_solution(1768652942478518630)
XLA Ops:
  4.2 41.0 %shard_map.238 = (bf16[2,5,56,512]{3,2,1,0:T(8,128)(2,1)}, f32[256,1]{1,0:T(8,128)}, f32[256,1]{1,0:T(8,128)}, bf16[256,1120]{1,0:T(8,128)(2,1)}, bf16[256,1120]...) custom-call(f32[1,1120]{1,0:T(1,128)} %get-tuple-element.784.refs_0_, ...), custom_call_target="tpu_custom_call" | custom-call | flops 1048576 | bytes 1048576 | tf_op jit(solution)/shard_map/pallas_call | solution.py:370
  53.4 21.5 %shard_map.239 = (f32[5,1,512]{2,1,0:T(1,128)S(1)}, f32[5,1,512]{2,1,0:T(1,128)S(1)}, f32[5,56,512]{2,1,0:T(8,128)S(1)}, f32[5,1,512]{2,1,0:T(1,128)S(1)}, f32[5...) custom-call(s32[13]{0:T(128)S(1)} %pad_add_fusion.info, bf16[5,56,512]{2,1,0:T(8,128)(2,1)S(1)} %copy-done.4, ...), custom_call_target="tpu_custom_call" | custom-call | flops 1048576 | bytes 1048576 | tf_op jit(solution)/shard_map/pallas_call | solution.py:246
  75.5 6.7 shard_map.240
  83.7 74.6 %shard_map.241 = (bf16[2,5,56,512]{3,2,1,0:T(8,128)(2,1)}, bf16[512,1120]{1,0:T(8,128)(2,1)}, bf16[512,1120]{1,0:T(8,128)(2,1)}, f32[256,1]{1,0:T(8,128)}, f32[2...) custom-call(f32[256,1120]{1,0:T(8,128)} %get-tuple-element.377.refs_, ...), custom_call_target="tpu_custom_call" | custom-call | flops 1048576 | bytes 1048576 | tf_op jit(solution)/shard_map/pallas_call | solution.py:370
  165.7 21.4 %shard_map.242 = (f32[5,1,512]{2,1,0:T(1,128)S(1)}, f32[5,1,512]{2,1,0:T(1,128)S(1)}, f32[5,56,512]{2,1,0:T(8,128)S(1)}, f32[5,1,512]{2,1,0:T(1,128)S(1)}, f32[5...) custom-call(s32[13]{0:T(128)S(1)} %pad_add_fusion.info, bf16[5,56,512]{2,1,0:T(8,128)(2,1)S(1)} %copy-done.8, ...), custom_call_target="tpu_custom_call" | custom-call | flops 1048576 | bytes 1048576 | tf_op jit(solution)/shard_map/pallas_call | solution.py:246
  187.2 6.7 shard_map.243
  195.4 66.9 %shard_map.244 = (bf16[512,1120]{1,0:T(8,128)(2,1)}, bf16[512,1120]{1,0:T(8,128)(2,1)}, f32[256,1]{1,0:T(8,128)}, f32[256,1]{1,0:T(8,128)}, bf16[1120,256]{1,0:T...) custom-call(f32[256,1120]{1,0:T(8,128)} %get-tuple-element.419.refs_, ...), custom_call_target="tpu_custom_call" | custom-call | flops 1048576 | bytes 1048576 | tf_op jit(solution)/shard_map/pallas_call | solution.py:370
  262.3 47.7 %shard_map.245 = (f32[256,1120]{1,0:T(8,128)}, f32[256,1120]{1,0:T(8,128)}, bf16[5,56,512]{2,1,0:T(8,128)(2,1)}, bf16[5,56,512]{2,1,0:T(8,128)(2,1)}, bf16[512,1...) custom-call(bf16[1120,256]{1,0:T(8,128)(2,1)} %get-tuple-element.437, ...), custom_call_target="tpu_custom_call" | custom-call | flops 1048576 | bytes 1048576 | tf_op jit(solution)/shard_map/pallas_call | solution.py:370
  310.0 3.5 fusion.26
  313.5 1.8 fusion
  317.0 1.7 fusion.27
  318.7 1.8 fusion.1
  321.7 2.7 collective-permute-start.4
  328.9 12.7 %shard_map.246 = (f32[5,56,512]{2,1,0:T(8,128)S(1)}, f32[5,56,512]{2,1,0:T(8,128)S(1)}, bf16[2,5,56,512]{3,2,1,0:T(8,128)(2,1)S(1)}, bf16[2,5,56,512]{3,2,1,0:T(8,128)(2,1)S(1)}) custom-call(s32[13]{0:T(128)S(1)} %pad_add_fusion.info, bf16[5,56,512]{2,1,0:T(8,128)(2,1)S(1)} %copy-done.9, bf16[5,56,512]{2,1,0:T(8,128)(2,1)S(1)} %copy-done.36, ...), custom_call_target="tpu_custom_call" | custom-call | flops 1048576 | bytes 1048576 | tf_op jit(solution)/shard_map/pallas_call | solution.py:264
  343.7 16.0 %shard_map.247 = (f32[5,56,512]{2,1,0:T(8,128)S(1)}, f32[5,56,512]{2,1,0:T(8,128)S(1)}, f32[2,5,56,512]{3,2,1,0:T(8,128)S(1)}, f32[2,5,56,512]{3,2,1,0:T(8,128)S(1)}) custom-call(s32[13]{0:T(128)S(1)} %pad_add_fusion.info, bf16[5,56,512]{2,1,0:T(8,128)(2,1)S(1)} %copy-done.9, bf16[5,56,512]{2,1,0:T(8,128)(2,1)S(1)} %copy-done.36, ...), custom_call_target="tpu_custom_call" | custom-call | flops 1048576 | bytes 1048576 | tf_op jit(solution)/shard_map/pallas_call | solution.py:264
  361.9 7.4 collective-permute-done.3.refs_12_
  370.1 75.3 %shard_map.248 = (f32[256,1120]{1,0:T(8,128)}, f32[256,1120]{1,0:T(8,128)}, bf16[3,5,56,512]{3,2,1,0:T(8,128)(2,1)}, bf16[3,5,56,512]{3,2,1,0:T(8,128)(2,1)}, bf...) custom-call(f32[2,1120]{1,0:T(2,128)} %pad_maximum_fusion.15.refs_0_, ...), custom_call_target="tpu_custom_call" | custom-call | flops 1048576 | bytes 1048576 | tf_op jit(solution)/shard_map/pallas_call | solution.py:370
  445.5 3.1 add_convert_fusion.2.refs_9_
  461.8 1.8 fusion.2
  466.9 1.8 fusion.3
  469.0 3.0 broadcast_select_fusion
  472.0 12.5 %shard_map.249 = (f32[5,56,512]{2,1,0:T(8,128)S(1)}, f32[5,56,512]{2,1,0:T(8,128)S(1)}, bf16[2,5,56,512]{3,2,1,0:T(8,128)(2,1)S(1)}, bf16[2,5,56,512]{3,2,1,0:T(8,128)(2,1)S(1)}) custom-call(s32[13]{0:T(128)S(1)} %pad_add_fusion.info, bf16[5,56,512]{2,1,0:T(8,128)(2,1)S(1)} %copy-done.5, bf16[5,56,512]{2,1,0:T(8,128)(2,1)S(1)} %copy-done.34, ...), custom_call_target="tpu_custom_call" | custom-call | flops 1048576 | bytes 1048576 | tf_op jit(solution)/shard_map/pallas_call | solution.py:264
  484.6 2.7 collective-permute-start.6
  487.3 16.0 %shard_map.250 = (f32[5,56,512]{2,1,0:T(8,128)S(1)}, f32[5,56,512]{2,1,0:T(8,128)S(1)}, f32[2,5,56,512]{3,2,1,0:T(8,128)S(1)}, f32[2,5,56,512]{3,2,1,0:T(8,128)S(1)}) custom-call(s32[13]{0:T(128)S(1)} %pad_add_fusion.info, bf16[5,56,512]{2,1,0:T(8,128)(2,1)S(1)} %copy-done.5, bf16[5,56,512]{2,1,0:T(8,128)(2,1)S(1)} %copy-done.34, ...), custom_call_target="tpu_custom_call" | custom-call | flops 1048576 | bytes 1048576 | tf_op jit(solution)/shard_map/pallas_call | solution.py:264
  505.5 5.6 collective-permute-done.7.refs_8_
  512.0 57.0 %shard_map.251 = (bf16[280,1120]{1,0:T(8,128)(2,1)}, f32[256,1120]{1,0:T(8,128)}, f32[256,1120]{1,0:T(8,128)}, bf16[3,5,56,512]{3,2,1,0:T(8,128)(2,1)}, bf16[3,5...) custom-call(f32[2,1120]{1,0:T(2,128)} %get-tuple-element.625.refs_0_, ...), custom_call_target="tpu_custom_call" | custom-call | flops 1048576 | bytes 1048576 | tf_op jit(solution)/shard_map/pallas_call | solution.py:370
  578.9 1.9 broadcast_select_fusion.4
  580.8 273.7 %shard_map.252 = (f32[3,16,1120]{2,1,0:T(8,128)}, bf16[2,2,560,1120]{3,2,1,0:T(8,128)(2,1)}, bf16[2,2,280,1120]{3,2,1,0:T(8,128)(2,1)}, bf16[2,2,560,1120]{3,2,1...) custom-call(bf16[280,1120]{1,0:T(8,128)(2,1)} %get-tuple-element.666.refs_0_, ...), custom_call_target="tpu_custom_call" | custom-call | flops 1048576 | bytes 1048576 | tf_op jit(solution)/shard_map/pallas_call | solution.py:370
  863.2 3.0 fusion.14
  870.1 4.8 maximum_convert_fusion
  874.9 4.8 maximum_convert_fusion.1
  879.6 3.5 convert_bitcast_fusion
  (281 shorter events, 79.4 us)
Async XLA Ops:
  4.2 41.1 %copy-start.89 = (s32[6]{0:T(128)S(1)}, s32[6]{0:T(128)}, u32[]{:S(2)}) copy-start(s32[6]{0:T(128)} %constant.51.clone) | copy-start | bytes 76
  4.2 41.3 %copy-start.80 = (s32[2,8]{1,0:T(2,128)S(1)}, s32[2,8]{1,0:T(2,128)}, u32[]{:S(2)}) copy-start(s32[2,8]{1,0:T(2,128)} %param.17) | copy-start | bytes 196
  4.2 41.4 %copy-start.77 = (bf16[2,1120]{1,0:T(2,128)(2,1)S(1)}, bf16[2,1120]{1,0:T(2,128)(2,1)}, u32[]{:S(2)}) copy-start(bf16[2,1120]{1,0:T(2,128)(2,1)} %param.26) | copy-start | bytes 13444
  4.2 41.4 %copy-start.78 = (bf16[2,1120]{1,0:T(2,128)(2,1)S(1)}, bf16[2,1120]{1,0:T(2,128)(2,1)}, u32[]{:S(2)}) copy-start(bf16[2,1120]{1,0:T(2,128)(2,1)} %param.22) | copy-start | bytes 13444
  4.2 41.4 %copy-start.79 = (s32[2]{0:T(128)S(1)}, s32[2]{0:T(128)}, u32[]{:S(2)}) copy-start(s32[2]{0:T(128)} %param.18) | copy-start | bytes 28
  45.2 29.6 %copy-start.76 = (bf16[2,1120]{1,0:T(2,128)(2,1)S(1)}, bf16[2,1120]{1,0:T(2,128)(2,1)}, u32[]{:S(2)}) copy-start(bf16[2,1120]{1,0:T(2,128)(2,1)} %param.24) | copy-start | bytes 13444
  45.2 30.2 %collective-permute-start = (bf16[2,5,56,512]{3,2,1,0:T(8,128)(2,1)}, bf16[2,5,56,512]{3,2,1,0:T(8,128)(2,1)S(1)}, u32[]{:S(2)}, u32[]{:S(2)}) collective-permute-start(bf16[2,5,56,512]{3,2,1,0:T(8,128)(2,1)} %get-tuple-element.618.refs_3_.refs_11_), channel_id=1, source_target_pairs={{0,4},{4,0},{8,12},{12,8},{1,5},{5,1},{9,13},{13,9},{2,6},{6,2},{1... | collective-permute-start | bytes 1720328 | tf_op jit(solution)/shard_map/ppermute | solution.py:26
  53.4 22.1 %copy-start.5 = (bf16[5,56,512]{2,1,0:T(8,128)(2,1)S(1)}, bf16[5,56,512]{2,1,0:T(8,128)(2,1)}, u32[]{:S(2)}) copy-start(bf16[5,56,512]{2,1,0:T(8,128)(2,1)} %get-tuple-element.607.refs_0_) | copy-start | bytes 860164
  53.4 22.1 %copy-start.7 = (bf16[5,56,512]{2,1,0:T(8,128)(2,1)S(1)}, bf16[5,56,512]{2,1,0:T(8,128)(2,1)}, u32[]{:S(2)}) copy-start(bf16[5,56,512]{2,1,0:T(8,128)(2,1)} %get-tuple-element.612.refs_1_.refs_4_.refs_5_) | copy-start | bytes 860164
  75.5 6.8 copy-start.26
  83.7 75.7 %copy-start.75 = (f32[1,1120]{1,0:T(1,128)S(1)}, f32[1,1120]{1,0:T(1,128)}, u32[]{:S(2)}) copy-start(f32[1,1120]{1,0:T(1,128)} %get-tuple-element.784.refs_0_) | copy-start | bytes 13444
  158.3 28.9 %collective-permute-start.1 = (bf16[2,5,56,512]{3,2,1,0:T(8,128)(2,1)}, bf16[2,5,56,512]{3,2,1,0:T(8,128)(2,1)S(1)}, u32[]{:S(2)}, u32[]{:S(2)}) collective-permute-start(bf16[2,5,56,512]{3,2,1,0:T(8,128)(2,1)} %get-tuple-element.510.refs_3_.refs_11_), channel_id=1, source_target_pairs={{0,4},{4,0},{8,12},{12,8},{1,5},{5,1},{9,13},{13,9},{2,6},{6,2},{1... | collective-permute-start | bytes 1720328 | tf_op jit(solution)/shard_map/ppermute | solution.py:26
  165.7 21.5 %copy-start.9 = (bf16[5,56,512]{2,1,0:T(8,128)(2,1)S(1)}, bf16[5,56,512]{2,1,0:T(8,128)(2,1)}, u32[]{:S(2)}) copy-start(bf16[5,56,512]{2,1,0:T(8,128)(2,1)} %get-tuple-element.499.refs_0_) | copy-start | bytes 860164
  165.7 21.5 %copy-start.11 = (bf16[5,56,512]{2,1,0:T(8,128)(2,1)S(1)}, bf16[5,56,512]{2,1,0:T(8,128)(2,1)}, u32[]{:S(2)}) copy-start(bf16[5,56,512]{2,1,0:T(8,128)(2,1)} %get-tuple-element.504.refs_1_.refs_4_.refs_5_) | copy-start | bytes 860164
  187.2 6.8 copy-start.30
  321.7 38.1 %collective-permute-start.4 = (bf16[2,288,1120]{2,1,0:T(8,128)(2,1)S(1)}, bf16[2,288,1120]{2,1,0:T(8,128)(2,1)S(1)}, u32[]{:S(2)}, u32[]{:S(2)}) collective-permute-start(bf16[2,288,1120]{2,1,0:T(8,128)(2,1)S(1)} %slice.385), channel_id=1, source_target_pairs={{0,16},{16,0},{1,17},{17,1},{2,18},{18,2},{3,19},{19,3},{4,20},{20... | collective-permute-start | bytes 3870728 | tf_op jit(solution)/shard_map/ppermute | solution.py:26
  325.5 119.9 %collective-permute-start.5 = (bf16[2,272,1120]{2,1,0:T(8,128)(2,1)}, bf16[2,272,1120]{2,1,0:T(8,128)(2,1)}, u32[]{:S(2)}, u32[]{:S(2)}) collective-permute-start(bf16[2,272,1120]{2,1,0:T(8,128)(2,1)} %slice.387), channel_id=1, source_target_pairs={{0,16},{16,0},{1,17},{17,1},{2,18},{18,2},{3,19},{19,3},{4,20},{20... | collective-permute-start | bytes 3655688 | tf_op jit(solution)/shard_map/ppermute | solution.py:26
  328.9 14.8 %copy-start.21 = (bf16[2,5,56,512]{3,2,1,0:T(8,128)(2,1)S(1)}, bf16[2,5,56,512]{3,2,1,0:T(8,128)(2,1)}, u32[]{:S(2)}) copy-start(bf16[2,5,56,512]{3,2,1,0:T(8,128)(2,1)} %get-tuple-element.509.refs_2_.refs_10_) | copy-start | bytes 1720324
  328.9 14.8 %copy-start.23 = (bf16[2,5,56,512]{3,2,1,0:T(8,128)(2,1)S(1)}, bf16[2,5,56,512]{3,2,1,0:T(8,128)(2,1)}, u32[]{:S(2)}) copy-start(bf16[2,5,56,512]{3,2,1,0:T(8,128)(2,1)} %get-tuple-element.510.refs_3_.refs_11_) | copy-start | bytes 1720324
  341.6 20.3 %collective-permute-start.2 = (bf16[2,5,56,512]{3,2,1,0:T(8,128)(2,1)S(1)}, bf16[2,5,56,512]{3,2,1,0:T(8,128)(2,1)S(1)}, u32[]{:S(2)}, u32[]{:S(2)}) collective-permute-start(bf16[2,5,56,512]{3,2,1,0:T(8,128)(2,1)S(1)} %get-tuple-element.495), channel_id=1, source_target_pairs={{0,4},{4,0},{8,12},{12,8},{1,5},{5,1},{9,13},{13,9},{2,6},{6,2},{1... | collective-permute-start | bytes 1720328 | tf_op jit(solution)/shard_map/ppermute | solution.py:26
  342.2 27.1 %collective-permute-start.3 = (bf16[2,5,56,512]{3,2,1,0:T(8,128)(2,1)S(1)}, bf16[2,5,56,512]{3,2,1,0:T(8,128)(2,1)S(1)}, u32[]{:S(2)}, u32[]{:S(2)}) collective-permute-start(bf16[2,5,56,512]{3,2,1,0:T(8,128)(2,1)S(1)} %get-tuple-element.496), channel_id=1, source_target_pairs={{0,4},{4,0},{8,12},{12,8},{1,5},{5,1},{9,13},{13,9},{2,6},{6,2},{1... | collective-permute-start | bytes 1720328 | tf_op jit(solution)/shard_map/ppermute | solution.py:26
  361.9 7.4 copy-start.68
  457.9 45.4 %collective-permute-start.8 = (bf16[2,280,1120]{2,1,0:T(8,128)(2,1)S(1)}, bf16[2,280,1120]{2,1,0:T(8,128)(2,1)S(1)}, u32[]{:S(2)}, u32[]{:S(2)}) collective-permute-start(bf16[2,280,1120]{2,1,0:T(8,128)(2,1)S(1)} %get-tuple-element.722), channel_id=1, source_target_pairs={{0,16},{16,0},{1,17},{17,1},{2,18},{18,2},{3,19},{19,3},{4,20},{20... | collective-permute-start | bytes 3763208 | tf_op jit(solution)/shard_map/ppermute | solution.py:26
  458.9 121.9 %collective-permute-start.10 = (bf16[2,288,1120]{2,1,0:T(8,128)(2,1)}, bf16[2,288,1120]{2,1,0:T(8,128)(2,1)}, u32[]{:S(2)}, u32[]{:S(2)}) collective-permute-start(bf16[2,288,1120]{2,1,0:T(8,128)(2,1)} %get-tuple-element.676.refs_10_), channel_id=1, source_target_pairs={{0,16},{16,0},{1,17},{17,1},{2,18},{18,2},{3,19},{19,3},{4,20},{20... | collective-permute-start | bytes 3870728 | tf_op jit(solution)/shard_map/ppermute | solution.py:26
  472.0 15.3 %copy-start.17 = (bf16[2,5,56,512]{3,2,1,0:T(8,128)(2,1)S(1)}, bf16[2,5,56,512]{3,2,1,0:T(8,128)(2,1)}, u32[]{:S(2)}) copy-start(bf16[2,5,56,512]{3,2,1,0:T(8,128)(2,1)} %get-tuple-element.617.refs_2_.refs_10_) | copy-start | bytes 1720324
  472.0 15.3 %copy-start.19 = (bf16[2,5,56,512]{3,2,1,0:T(8,128)(2,1)S(1)}, bf16[2,5,56,512]{3,2,1,0:T(8,128)(2,1)}, u32[]{:S(2)}) copy-start(bf16[2,5,56,512]{3,2,1,0:T(8,128)(2,1)} %get-tuple-element.618.refs_3_.refs_11_) | copy-start | bytes 1720324
  484.6 20.9 %collective-permute-start.6 = (bf16[2,5,56,512]{3,2,1,0:T(8,128)(2,1)S(1)}, bf16[2,5,56,512]{3,2,1,0:T(8,128)(2,1)S(1)}, u32[]{:S(2)}, u32[]{:S(2)}) collective-permute-start(bf16[2,5,56,512]{3,2,1,0:T(8,128)(2,1)S(1)} %get-tuple-element.603), channel_id=1, source_target_pairs={{0,4},{4,0},{8,12},{12,8},{1,5},{5,1},{9,13},{13,9},{2,6},{6,2},{1... | collective-permute-start | bytes 1720328 | tf_op jit(solution)/shard_map/ppermute | solution.py:26
  487.2 23.9 %collective-permute-start.7 = (bf16[2,5,56,512]{3,2,1,0:T(8,128)(2,1)S(1)}, bf16[2,5,56,512]{3,2,1,0:T(8,128)(2,1)S(1)}, u32[]{:S(2)}, u32[]{:S(2)}) collective-permute-start(bf16[2,5,56,512]{3,2,1,0:T(8,128)(2,1)S(1)} %get-tuple-element.604), channel_id=1, source_target_pairs={{0,4},{4,0},{8,12},{12,8},{1,5},{5,1},{9,13},{13,9},{2,6},{6,2},{1... | collective-permute-start | bytes 1720328 | tf_op jit(solution)/shard_map/ppermute | solution.py:26
  487.3 93.4 %collective-permute-start.9 = (bf16[2,560,1120]{2,1,0:T(8,128)(2,1)}, bf16[2,560,1120]{2,1,0:T(8,128)(2,1)}, u32[]{:S(2)}, u32[]{:S(2)}) collective-permute-start(bf16[2,560,1120]{2,1,0:T(8,128)(2,1)} %get-tuple-element.712), channel_id=1, source_target_pairs={{0,16},{16,0},{1,17},{17,1},{2,18},{18,2},{3,19},{19,3},{4,20},{20... | collective-permute-start | bytes 7526408 | tf_op jit(solution)/shard_map/ppermute | solution.py:26
  505.5 6.5 copy-start.70
  861.8 4.3 slice-start
  874.9 4.8 copy-start.48
  (71 other events, 122.4 us)

commit v3 on v2

--- a/solution.py
+++ b/solution.py
@@ -135,8 +135,8 @@
                 total=total,
                 sums=sums,
             ):
-                for head in range(heads):
-                    scores = score_block(
+                scores = [
+                    score_block(
                         info,
                         pair[0, head, :, key_at],
                         queries[head, :, query_at],
@@ -144,17 +144,25 @@
                         query_block,
                         masked,
                     )
-                    old = top[head, :, query_at]
-                    new = jnp.maximum(old, jnp.max(scores, axis=0, keepdims=True) * factor)
-                    decay = jnp.exp2(old - new)
-                    weights = jnp.exp2(scores * factor - new)
-                    top[head, :, query_at] = new
+                    for head in range(heads)
+                ]
+                olds = [top[head, :, query_at] for head in range(heads)]
+                news = [
+                    jnp.maximum(old, jnp.max(score, axis=0, keepdims=True) * factor)
+                    for old, score in zip(olds, scores)
+                ]
+                weights = [jnp.exp2(score * factor - new) for score, new in zip(scores, news)]
+                products = [
+                    contract(pair[1, head, :, key_at], weights[head].astype(BF16), 1, 0)
+                    for head in range(heads)
+                ]
+                for head in range(heads):
+                    decay = jnp.exp2(olds[head] - news[head])
+                    top[head, :, query_at] = news[head]
                     total[head, :, query_at] = total[head, :, query_at] * decay + jnp.sum(
-                        weights, axis=0, keepdims=True
+                        weights[head], axis=0, keepdims=True
                     )
-                    sums[head, :, query_at] = sums[head, :, query_at] * decay + contract(
-                        pair[1, head, :, key_at], weights.astype(BF16), 1, 0
-                    )
+                    sums[head, :, query_at] = sums[head, :, query_at] * decay + products[head]
 
             for_blocks(info, stream, first_chunk + chunk, rows, work)
         if last:
@@ -204,19 +212,31 @@
                 grad_mixed=grad_mixed,
                 log_total=log_total,
             ):
-                for head in range(heads):
-                    keys, values = pair[0, head, :, key_at], pair[1, head, :, key_at]
-                    query_part = queries[head, :, query_at]
-                    grad_part = grad_mixed[head, :, query_at]
-                    scores = score_block(info, keys, query_part, key_block, query_block, masked)
-                    probs = jnp.exp2(scores * factor - log_total[head, :, query_at])
-                    grad_probs = contract(values, grad_part, 0, 0)
-                    grad_scores = (
-                        probs * (grad_probs - inner[stream, head, :, query_at])
-                    ).astype(BF16)
-                    pair_sums[1, head, :, key_at] += contract(grad_part, probs.astype(BF16), 1, 1)
-                    pair_sums[0, head, :, key_at] += contract(query_part, grad_scores, 1, 1)
-                    query_sums[stream][head, :, query_at] += contract(keys, grad_scores, 1, 0)
+                every = range(heads)
+                keys = [pair[0, head, :, key_at] for head in every]
+                values = [pair[1, head, :, key_at] for head in every]
+                query_parts = [queries[head, :, query_at] for head in every]
+                grad_parts = [grad_mixed[head, :, query_at] for head in every]
+                scores = [
+                    score_block(info, keys[h], query_parts[h], key_block, query_block, masked)
+                    for h in every
+                ]
+                grad_probs = [contract(values[h], grad_parts[h], 0, 0) for h in every]
+                probs = [
+                    jnp.exp2(scores[h] * factor - log_total[h, :, query_at]) for h in every
+                ]
+                grad_scores = [
+                    (probs[h] * (grad_probs[h] - inner[stream, h, :, query_at])).astype(BF16)
+                    for h in every
+                ]
+                low_probs = [member.astype(BF16) for member in probs]
+                for_values = [contract(grad_parts[h], low_probs[h], 1, 1) for h in every]
+                for_keys = [contract(query_parts[h], grad_scores[h], 1, 1) for h in every]
+                for_queries = [contract(keys[h], grad_scores[h], 1, 0) for h in every]
+                for h in every:
+                    pair_sums[0, h, :, key_at] += for_keys[h]
+                    pair_sums[1, h, :, key_at] += for_values[h]
+                    query_sums[stream][h, :, query_at] += for_queries[h]
 
             for_blocks(info, stream, first_chunk + chunk, rows, work)
         grad_pairs[chunk][0] = (pair_sums[0] * scale).astype(grad_pairs[chunk].dtype)
@@ -435,19 +455,34 @@
     def keep(self, values):
         self.part[...] = values
 
-    def join(self):
+    def part_rows(self, part):
+        return pl.ds(part * (self.rows // 2), self.rows // 2)
+
+    def join(self, cross):
         self.to_near.wait_recv()
-
-        def work(rows):
-            self.sent[1, rows] = (self.part[rows] + self.got[0, rows].astype(F32)).astype(BF16)
-
-        by_rows(self.rows, work)
-
-    def cross(self):
-        self.to_far = self.wires.start(self.sent.at[1], self.got.at[1], far)
-
-    def wait(self):
-        self.to_far.wait_recv()
+        self.to_far = [None, None]
+        for part in (0, 1):
+            start = part * (self.rows // 2)
+
+            def work(rows, start=start):
+                at = pl.ds(start + rows.start, rows.size)
+                self.sent[1, at] = (self.part[at] + self.got[0, at].astype(F32)).astype(BF16)
+
+            by_rows(self.rows // 2, work)
+            if cross:
+                self.cross(part)
+
+    def cross(self, part):
+        rows = self.part_rows(part)
+        self.to_far[part] = self.wires.start(
+            self.sent.at[1, rows], self.got.at[1, rows], far
+        )
+
+    def wait(self, then=None):
+        for part in (0, 1):
+            self.to_far[part].wait_recv()
+            if then is not None:
+                then.cross(part)
 
     def total(self, rows):
         return self.sent[1, rows].astype(F32) + self.got[1, rows].astype(F32)
@@ -676,25 +711,21 @@
 
     for i in (0, 1):
         attended(i)
-    first[0].join()
-    first[0].cross()
-    first[1].join()
-    first[0].wait()
-    first[1].cross()
+    first[0].join(True)
+    first[1].join(False)
+    first[0].wait(first[1])
     if not last:
         given = wires.start(
             r.out_grad.at[1 - side, :, core_columns(half, core)], r.got_grad, pair_far
         )
     mid_norm(0)
     feed(0)
-    second[0].join()
-    first[1].wait()
-    second[0].cross()
+    second[0].join(False)
+    first[1].wait(second[0])
     mid_norm(1)
     feed(1)
-    second[1].join()
-    second[0].wait()
-    second[1].cross()
+    second[1].join(False)
+    second[0].wait(second[1])
     leave(0)
     if not last:
         paired = wires.start(r.pair[0], r.got_pair, pair)
@@ -789,8 +820,8 @@
                     target[head, :, at] = found.astype(BF16)
                 rows = head_rows(target, at)
                 if j != 1:
-                    index = 7 + j // 2
-                    r.sums[index : index + 1, : rows.shape[1]] += jnp.sum(
+                    start = j // 2 * (r.sums.shape[1] // 256 * 128)
+                    r.sums[7:8, start : start + rows.shape[1]] += jnp.sum(
                         rows, axis=0, keepdims=True
                     )
                 product = mm(rows.astype(BF16), qkv_w.get()[j])
@@ -871,10 +902,14 @@
     def ride(step):
         if riding and step == 0:
             rider.one()
+            if riding == 1:
+                r.late = wires.start(r.near_late, r.far_late, pair_far)
         elif riding and step == 1:
             rider.two()
         elif riding and step == 5:
             rider.wait()
+            if riding == 1:
+                r.late.wait_recv()
         elif riding == 2 and step == 3:
             rider.three()
 
@@ -885,10 +920,8 @@
         for i in (0, 1):
             first_rows(i)
             slide(i, after[i])
-            after[i].join()
-            if i == 1:
-                after[0].wait()
-            after[i].cross()
+            after[i].join(i == 0)
+        after[0].wait(after[1])
         second_norm(0)
         placed.forward()
         after[1].wait()
@@ -899,26 +932,22 @@
         a, b = (1, 0) if end else (0, 1)
         gather(a, before[a])
         gather(b, before[b])
-        before[a].join()
-        before[a].cross()
-        before[b].join()
-        before[a].wait()
-        before[b].cross()
+        before[a].join(True)
+        before[b].join(False)
         ride(1)
+        before[a].wait(before[b])
         first_norm(a)
         if end:
             before[b].wait()
             first_norm(b)
         else:
             slide(a, after[a])
-            after[a].join()
-            before[b].wait()
-            after[a].cross()
+            after[a].join(False)
+            before[b].wait(after[a])
             first_norm(b)
             slide(b, after[b])
-            after[b].join()
-            after[a].wait()
-            after[b].cross()
+            after[b].join(False)
+            after[a].wait(after[b])
             ride(3)
             second_norm(a)
             after[b].wait()
@@ -954,7 +983,7 @@
     some = given["block_low"][0] if begin else given["grad"][0]
     width = given["gains"].shape[1]
     half = some.shape[1] if begin else some.shape[0]
-    results = dict(sums=shape_of((16, width), F32), grad_out=twice(shape_of((half, width), F32)))
+    results = dict(sums=shape_of((8, width), F32), grad_out=twice(shape_of((half, width), F32)))
     wide = twice(shape_of((2 * half, width), BF16))
     out_hbm = {}
     scratch = exchange_scratch(half, width, int(not begin) + int(not end))
@@ -991,6 +1020,7 @@
         else:
             part = shape_of(whole.shape[1:], BF16)
             results.update(near_sum=part, got_far=part)
+            results.update(far_late=shape_of(given["near_late"].shape, BF16))
         scratch.update(got_sum=one)
     return call_kernel(
         functools.partial(backward_kernel, attention, feed, riding),
@@ -1009,7 +1039,7 @@
     kernels = r.vectors.shape[0]
     r.total[...] = r.vectors[...]
 
-    def vectors(at, partner, own_rows=16):
+    def vectors(at, partner, own_rows=8):
         copy = wires.start(r.total, r.around.at[at], partner)
 
         def add():
@@ -1029,7 +1059,7 @@
             Sum(wires, r.whole_feed[k], r.sum_feed[k], *r.riding_feed[k]) for k in (0, 1)
         ]
         last = Sum(wires, r.whole_last, r.sum_last, *r.riding_last)
-        late = Sum(wires, r.whole_late, r.sum_late, *r.riding_late)
+        late = Sum(wires, None, r.sum_late, r.near_late, None, r.far_late)
         prior = Sum(wires, None, r.sum_prior, r.near_prior, None, r.far_prior)
         local = []
 
@@ -1045,40 +1075,38 @@
             own, target = member.five(everything, rows)
             local.append(Local(r, len(local), own, target))
 
+        late.three()
         fold(r.whole_feed[0], r.kept_feed, r.got_feed, spans[0])
         feed[0].one()
-        prior.three()
-        late.one()
-        placed = place_cells(r, wires, r.tokens_grad, r.low)
-        add = vectors(0, near, 6)
         local.append(Local(r, 0, r.early, r.all_late.at[cell, :, spans[0]]))
         local.append(Local(r, 1, r.got_early, r.all_late.at[1 - cell, :, spans[0]]))
-        fold(r.whole_feed[1], r.kept_feed, r.got_feed, spans[1])
+        add = vectors(0, near, 6)
         feed[0].two()
-        feed[1].one()
-        add()
-        add = vectors(1, across)
-        late.two()
-        five(prior, r.all_prior, whole)
         arriving.wait_recv()
         fold(r.whole_last, r.kept_last, r.got_last, whole)
         last.one()
+        prior.three()
+        five(late, r.all_late, spans[1])
+        fold(r.whole_feed[1], r.kept_feed, r.got_feed, spans[1])
+        feed[0].three()
+        five(prior, r.all_prior, whole)
+        last.two()
+        feed[1].one()
+        last.three()
+        feed[1].two()
+        five(feed[0], r.all_feed, spans[0])
+        add()
+        add = vectors(1, across)
+        five(last, r.all_last, whole)
+        feed[1].three()
         add()
         add = vectors(2, pair)
-        feed[1].two()
-        feed[0].three()
+        five(feed[1], r.all_feed, spans[1])
+        add()
+        placed = place_cells(r, wires, r.tokens_grad, r.low)
+        add = vectors(3, pair_far)
         placed.forward()
         add()
-        add = vectors(3, pair_far)
-        last.two()
-        late.three()
-        feed[1].three()
-        add()
-        five(feed[0], r.all_feed, spans[0])
-        five(late, r.all_late, spans[1])
-        last.three()
-        five(feed[1], r.all_feed, spans[1])
-        five(last, r.all_last, whole)
         for member in feed + [late, prior, last]:
             member.wait()
         for copy in local:
@@ -1102,7 +1130,7 @@
     scratch = dict(total=pltpu.VMEM(vectors, F32), around=pltpu.VMEM((4,) + vectors, F32))
     if sums_too:
         feed, last = given["kept_feed"].shape, given["kept_last"].shape
-        late = given["whole_late"].shape
+        late = (2,) + given["near_late"].shape
         early = (feed[0], feed[1] - late[1]) + feed[2:]
         spans = [pltpu.VMEM(early, BF16), pltpu.VMEM(late, BF16)]
         out_hbm.update(
@@ -1116,7 +1144,6 @@
             sum_feed=spans,
             riding_feed=[sum_scratch(*early[1:]), sum_scratch(*late[1:])],
             sum_late=spans[1],
-            riding_late=sum_scratch(*late[1:]),
             whole_last=pltpu.VMEM(last, BF16),
             sum_last=pltpu.VMEM(last, BF16),
             got_last=pltpu.VMEM(last, BF16),
@@ -1305,6 +1332,9 @@
             if paired_cells:
                 given.update(whole=line.run(add_low, *pending))
                 riding = 1 if end else 2
+                if end:
+                    near_late = line.run(add_low, kept_late, got_late)
+                    given.update(near_late=near_late)
         if not end:
             below = saved[layer - 1]
             given.update(
@@ -1333,6 +1363,9 @@
                 early = found.summed
                 got_early = swap(early, CELL, 1)
                 late = line.run(add_low, *late)
+                bit = seq_index % 2
+                kept_late = jnp.where(bit == 0, late[0], late[1])
+                got_late = swap(jnp.where(bit == 0, late[1], late[0]), SEQ, 1)
             sums = line.run(attention_sums, wide_mid, above.mixed, above.wide_one, found.grads)
             if paired_cells:
                 kept, sent = line.run(functools.partial(pick, cell), sums[:2], sums[2:])
@@ -1381,7 +1414,8 @@
             got_feed=got_feed,
             kept_last=kept,
             sent_last=sent,
-            whole_late=late,
+            near_late=near_late,
+            far_late=found.far_late,
             near_prior=found.near_sum,
             far_prior=found.got_far,
         )
@@ -1420,14 +1454,18 @@
 
     gain_grad = jnp.stack([rows_of(attention_rows, 0), rows_of(feed_rows, 3)], axis=1)
     shift_grad = jnp.stack([rows_of(attention_rows, 1), rows_of(feed_rows, 4)], axis=1)
-    qv_grad = rows_of(attention_rows, 7, 8)[:, :local_width]
+    second = totals.shape[2] // 256 * 128
+    qv_rows = rows_of(attention_rows, 7)
+    qv_grad = jnp.stack(
+        [qv_rows[:, :local_width], qv_rows[:, second : second + local_width]], axis=1
+    )
     return (
         jnp.swapaxes(block_out, 1, 2),
         jnp.swapaxes(closing.tokens_grad, 1, 2),
         jnp.swapaxes(
             final([jnp.stack([*member[0], member[1, 0]]) for member in attentions]), 2, 3
         ),
-        qv_grad.reshape(layer_count, 2, local_width),
+        qv_grad,
         final([member[1, 1] for member in attentions]),
         rows_of(feed_rows, 5),
         final([square(member[0]) for member in feeds]),

time: 896 us -> 801 us (0.89)
  Pallas kernels: 750 us -> 647 us
    pallas_call x7, Pallas kernels: 636 us -> 575 us  [call_kernel(): pl.pallas_call(kernel, out_shape=tuple(flat[2][0] + flat[3][0]), in_specs...]
    pallas_call x4, Pallas kernels: 56.4 us -> 30.8 us  [attend(): pl.pallas_call(functools.partial(attend_kernel, first_chunk, len(pairs),...]
    pallas_call x4, Pallas kernels: 57.2 us -> 41.6 us  [attend_back(): pl.pallas_call(functools.partial(attend_back_kernel, first_chunk, len(pai...]
    ppermute x11 -> x12, waiting for transfers between devices: 13.1 us -> 21.5 us  [swap(): return lax.ppermute(values, axis, [(i, i ^ bit) for i in range(size)])]
    unnamed x188 -> x187, local copies, waits for them, and re-layouts: 34.6 us -> 35.2 us
  transfers between devices with their start and end apart: 11 -> 12, of which waited for: 2 -> 3; matrix products, arithmetic and copies ran while one was open for 3% -> 5% of each run, Pallas kernels for 26% -> 25%
where the time goes in v3:
time: 801 us; the launch traced here: 793 us
  Pallas kernels  647 us (81%)
  local copies, waits for them, and re-layouts  48.8 us (6%)
  other arithmetic  36.5 us (5%)
  matrix products  24.4 us (3%)
  waiting for transfers between devices  21.5 us (3%)
  starting transfers between devices  10.6 us (1%)
    pallas_call x7, Pallas kernels, call_kernel(): pl.pallas_call(kernel, out_shape=tuple(flat[2][0] + flat[3][0]), in_specs...  575 us
    pallas_call x4, Pallas kernels, attend_back(): pl.pallas_call(functools.partial(attend_back_kernel, first_chunk, len(pai...  41.6 us
    unnamed x187, local copies, waits for them, and re-layouts  35.2 us
    pallas_call x4, Pallas kernels, attend(): pl.pallas_call(functools.partial(attend_kernel, first_chunk, len(pairs),...  30.8 us
    dot_general x24, matrix products, contract(): lax.dot_general(left, right, (((left_dim,), (right_dim,)), ((), ())), pre...  24.4 us
    ppermute x12, waiting for transfers between devices, swap(): return lax.ppermute(values, axis, [(i, i ^ bit) for i in range(size)])  21.5 us
  transfers between devices with their start and end apart: 12, of which 3 were waited for; matrix products, arithmetic and copies ran while one was open for 5% of the time, Pallas kernels for 25%

profile of v3, /device:TPU:0, one launch (start us, length us, event | category | flops | bytes accessed | tf_op | source)
XLA Modules:
  0.0 792.7 jit_solution(15830278809314455464)
XLA Ops:
  4.2 40.9 %shard_map.238 = (bf16[2,5,56,512]{3,2,1,0:T(8,128)(2,1)}, f32[256,1]{1,0:T(8,128)}, f32[256,1]{1,0:T(8,128)}, bf16[256,1120]{1,0:T(8,128)(2,1)}, bf16[256,1120]...) custom-call(f32[1,1120]{1,0:T(1,128)} %get-tuple-element.796.refs_0_, ...), custom_call_target="tpu_custom_call" | custom-call | flops 1048576 | bytes 1048576 | tf_op jit(solution)/shard_map/pallas_call | solution.py:390
  53.3 11.4 %shard_map.239 = (f32[5,1,512]{2,1,0:T(1,128)S(1)}, f32[5,1,512]{2,1,0:T(1,128)S(1)}, f32[5,56,512]{2,1,0:T(8,128)S(1)}, f32[5,1,512]{2,1,0:T(1,128)S(1)}, f32[5...) custom-call(s32[13]{0:T(128)S(1)} %pad_add_fusion.info, bf16[5,56,512]{2,1,0:T(8,128)(2,1)S(1)} %copy-done.4, ...), custom_call_target="tpu_custom_call" | custom-call | flops 1048576 | bytes 1048576 | tf_op jit(solution)/shard_map/pallas_call | solution.py:266
  65.3 4.0 shard_map.240
  70.7 72.9 %shard_map.241 = (bf16[2,5,56,512]{3,2,1,0:T(8,128)(2,1)}, bf16[512,1120]{1,0:T(8,128)(2,1)}, bf16[512,1120]{1,0:T(8,128)(2,1)}, f32[256,1]{1,0:T(8,128)}, f32[2...) custom-call(f32[256,1120]{1,0:T(8,128)} %get-tuple-element.382.refs_, ...), custom_call_target="tpu_custom_call" | custom-call | flops 1048576 | bytes 1048576 | tf_op jit(solution)/shard_map/pallas_call | solution.py:390
  151.6 11.4 %shard_map.242 = (f32[5,1,512]{2,1,0:T(1,128)S(1)}, f32[5,1,512]{2,1,0:T(1,128)S(1)}, f32[5,56,512]{2,1,0:T(8,128)S(1)}, f32[5,1,512]{2,1,0:T(1,128)S(1)}, f32[5...) custom-call(s32[13]{0:T(128)S(1)} %pad_add_fusion.info, bf16[5,56,512]{2,1,0:T(8,128)(2,1)S(1)} %copy-done.8, ...), custom_call_target="tpu_custom_call" | custom-call | flops 1048576 | bytes 1048576 | tf_op jit(solution)/shard_map/pallas_call | solution.py:266
  163.1 4.0 shard_map.243
  168.5 62.7 %shard_map.244 = (bf16[512,1120]{1,0:T(8,128)(2,1)}, bf16[512,1120]{1,0:T(8,128)(2,1)}, f32[256,1]{1,0:T(8,128)}, f32[256,1]{1,0:T(8,128)}, bf16[1120,256]{1,0:T...) custom-call(f32[256,1120]{1,0:T(8,128)} %get-tuple-element.424.refs_, ...), custom_call_target="tpu_custom_call" | custom-call | flops 1048576 | bytes 1048576 | tf_op jit(solution)/shard_map/pallas_call | solution.py:390
  231.2 46.3 %shard_map.245 = (f32[256,1120]{1,0:T(8,128)}, f32[256,1120]{1,0:T(8,128)}, bf16[5,56,512]{2,1,0:T(8,128)(2,1)}, bf16[5,56,512]{2,1,0:T(8,128)(2,1)}, bf16[512,1...) custom-call(bf16[1120,256]{1,0:T(8,128)(2,1)} %get-tuple-element.442, ...), custom_call_target="tpu_custom_call" | custom-call | flops 1048576 | bytes 1048576 | tf_op jit(solution)/shard_map/pallas_call | solution.py:390
  277.6 3.5 fusion.27
  281.1 1.8 fusion
  284.5 1.7 fusion.28
  286.2 1.8 fusion.1
  288.2 1.9 broadcast_select_fusion.2
  294.1 2.4 slice.382
  298.5 9.3 %shard_map.246 = (f32[5,56,512]{2,1,0:T(8,128)S(1)}, f32[5,56,512]{2,1,0:T(8,128)S(1)}, bf16[2,5,56,512]{3,2,1,0:T(8,128)(2,1)S(1)}, bf16[2,5,56,512]{3,2,1,0:T(8,128)(2,1)S(1)}) custom-call(s32[13]{0:T(128)S(1)} %pad_add_fusion.info, bf16[5,56,512]{2,1,0:T(8,128)(2,1)S(1)} %copy-done.9, bf16[5,56,512]{2,1,0:T(8,128)(2,1)S(1)} %copy-done.36, ...), custom_call_target="tpu_custom_call" | custom-call | flops 1048576 | bytes 1048576 | tf_op jit(solution)/shard_map/pallas_call | solution.py:284
  309.9 11.6 %shard_map.247 = (f32[5,56,512]{2,1,0:T(8,128)S(1)}, f32[5,56,512]{2,1,0:T(8,128)S(1)}, f32[2,5,56,512]{3,2,1,0:T(8,128)S(1)}, f32[2,5,56,512]{3,2,1,0:T(8,128)S(1)}) custom-call(s32[13]{0:T(128)S(1)} %pad_add_fusion.info, bf16[5,56,512]{2,1,0:T(8,128)(2,1)S(1)} %copy-done.9, bf16[5,56,512]{2,1,0:T(8,128)(2,1)S(1)} %copy-done.36, ...), custom_call_target="tpu_custom_call" | custom-call | flops 1048576 | bytes 1048576 | tf_op jit(solution)/shard_map/pallas_call | solution.py:284
  322.4 3.0 add_convert_fusion.refs_19_
  325.4 9.8 %collective-permute-done.3.refs_12_ = bf16[2,5,56,512]{3,2,1,0:T(8,128)(2,1)S(1)} collective-permute-done((bf16[2,5,56,512]{3,2,1,0:T(8,128)(2,1)S(1)}, bf16[2,5,56,512]{3,2,1,0:T(8,128)(2,1)S(1)}, u32[]{:S(2)}, u32[]{:S(2)}) %collective-permute-start.3) | collective-permute-done | bytes 573472 | tf_op jit(solution)/shard_map/ppermute | solution.py:26
  336.1 72.1 %shard_map.248 = (f32[256,1120]{1,0:T(8,128)}, f32[256,1120]{1,0:T(8,128)}, bf16[3,5,56,512]{3,2,1,0:T(8,128)(2,1)}, bf16[3,5,56,512]{3,2,1,0:T(8,128)(2,1)}, bf...) custom-call(f32[2,1120]{1,0:T(2,128)} %pad_maximum_fusion.15.refs_0_, ...), custom_call_target="tpu_custom_call" | custom-call | flops 1048576 | bytes 1048576 | tf_op jit(solution)/shard_map/pallas_call | solution.py:390
  408.1 2.0 add_convert_fusion.2
  424.0 1.8 fusion.2
  429.1 1.8 fusion.3
  431.2 2.9 broadcast_select_fusion
  434.2 9.1 %shard_map.249 = (f32[5,56,512]{2,1,0:T(8,128)S(1)}, f32[5,56,512]{2,1,0:T(8,128)S(1)}, bf16[2,5,56,512]{3,2,1,0:T(8,128)(2,1)S(1)}, bf16[2,5,56,512]{3,2,1,0:T(8,128)(2,1)S(1)}) custom-call(s32[13]{0:T(128)S(1)} %pad_add_fusion.info, bf16[5,56,512]{2,1,0:T(8,128)(2,1)S(1)} %copy-done.5, bf16[5,56,512]{2,1,0:T(8,128)(2,1)S(1)} %copy-done.34, ...), custom_call_target="tpu_custom_call" | custom-call | flops 1048576 | bytes 1048576 | tf_op jit(solution)/shard_map/pallas_call | solution.py:284
  445.4 11.6 %shard_map.250 = (f32[5,56,512]{2,1,0:T(8,128)S(1)}, f32[5,56,512]{2,1,0:T(8,128)S(1)}, f32[2,5,56,512]{3,2,1,0:T(8,128)S(1)}, f32[2,5,56,512]{3,2,1,0:T(8,128)S(1)}) custom-call(s32[13]{0:T(128)S(1)} %pad_add_fusion.info, bf16[5,56,512]{2,1,0:T(8,128)(2,1)S(1)} %copy-done.5, bf16[5,56,512]{2,1,0:T(8,128)(2,1)S(1)} %copy-done.34, ...), custom_call_target="tpu_custom_call" | custom-call | flops 1048576 | bytes 1048576 | tf_op jit(solution)/shard_map/pallas_call | solution.py:284
  460.2 10.8 %collective-permute-done.9.refs_9_ = bf16[2,5,56,512]{3,2,1,0:T(8,128)(2,1)S(1)} collective-permute-done((bf16[2,5,56,512]{3,2,1,0:T(8,128)(2,1)S(1)}, bf16[2,5,56,512]{3,2,1,0:T(8,128)(2,1)S(1)}, u32[]{:S(2)}, u32[]{:S(2)}) %collective-permute-start.9) | collective-permute-done | bytes 573472 | tf_op jit(solution)/shard_map/ppermute | solution.py:26
  471.8 65.3 %shard_map.251 = (bf16[272,1120]{1,0:T(8,128)(2,1)}, bf16[280,1120]{1,0:T(8,128)(2,1)}, f32[256,1120]{1,0:T(8,128)}, f32[256,1120]{1,0:T(8,128)}, bf16[3,5,56,51...) custom-call(f32[2,1120]{1,0:T(2,128)} %get-tuple-element.632.refs_0_, ...), custom_call_target="tpu_custom_call" | custom-call | flops 1048576 | bytes 1048576 | tf_op jit(solution)/shard_map/pallas_call | solution.py:390
  546.8 1.9 broadcast_select_fusion.4
  548.7 214.8 %shard_map.252 = (f32[3,8,1120]{2,1,0:T(8,128)}, bf16[2,2,560,1120]{3,2,1,0:T(8,128)(2,1)}, bf16[2,2,280,1120]{3,2,1,0:T(8,128)(2,1)}, bf16[2,2,560,1120]{3,2,1,...) custom-call(bf16[272,1120]{1,0:T(8,128)(2,1)} %get-tuple-element.675.refs_0_, ...), custom_call_target="tpu_custom_call" | custom-call | flops 1048576 | bytes 1048576 | tf_op jit(solution)/shard_map/pallas_call | solution.py:390
  775.3 4.7 maximum_convert_fusion
  780.1 4.7 maximum_convert_fusion.1
  784.8 3.5 convert_bitcast_fusion
  (284 shorter events, 81.5 us)
Async XLA Ops:
  4.2 41.0 %copy-start.88 = (s32[6]{0:T(128)S(1)}, s32[6]{0:T(128)}, u32[]{:S(2)}) copy-start(s32[6]{0:T(128)} %constant.55.clone) | copy-start | bytes 76
  4.2 41.2 %copy-start.79 = (s32[2,8]{1,0:T(2,128)S(1)}, s32[2,8]{1,0:T(2,128)}, u32[]{:S(2)}) copy-start(s32[2,8]{1,0:T(2,128)} %param.17) | copy-start | bytes 196
  4.2 41.3 %copy-start.76 = (bf16[2,1120]{1,0:T(2,128)(2,1)S(1)}, bf16[2,1120]{1,0:T(2,128)(2,1)}, u32[]{:S(2)}) copy-start(bf16[2,1120]{1,0:T(2,128)(2,1)} %param.26) | copy-start | bytes 13444
  4.2 41.3 %copy-start.77 = (bf16[2,1120]{1,0:T(2,128)(2,1)S(1)}, bf16[2,1120]{1,0:T(2,128)(2,1)}, u32[]{:S(2)}) copy-start(bf16[2,1120]{1,0:T(2,128)(2,1)} %param.22) | copy-start | bytes 13444
  4.2 41.3 %copy-start.78 = (s32[2]{0:T(128)S(1)}, s32[2]{0:T(128)}, u32[]{:S(2)}) copy-start(s32[2]{0:T(128)} %param.18) | copy-start | bytes 28
  45.1 19.6 %copy-start.75 = (bf16[2,1120]{1,0:T(2,128)(2,1)S(1)}, bf16[2,1120]{1,0:T(2,128)(2,1)}, u32[]{:S(2)}) copy-start(bf16[2,1120]{1,0:T(2,128)(2,1)} %param.24) | copy-start | bytes 13444
  45.1 20.2 %collective-permute-start = (bf16[2,5,56,512]{3,2,1,0:T(8,128)(2,1)}, bf16[2,5,56,512]{3,2,1,0:T(8,128)(2,1)S(1)}, u32[]{:S(2)}, u32[]{:S(2)}) collective-permute-start(bf16[2,5,56,512]{3,2,1,0:T(8,128)(2,1)} %get-tuple-element.619.refs_3_.refs_11_), channel_id=1, source_target_pairs={{0,4},{4,0},{8,12},{12,8},{1,5},{5,1},{9,13},{13,9},{2,6},{6,2},{1... | collective-permute-start | bytes 1720328 | tf_op jit(solution)/shard_map/ppermute | solution.py:26
  53.3 12.1 %copy-start.5 = (bf16[5,56,512]{2,1,0:T(8,128)(2,1)S(1)}, bf16[5,56,512]{2,1,0:T(8,128)(2,1)}, u32[]{:S(2)}) copy-start(bf16[5,56,512]{2,1,0:T(8,128)(2,1)} %get-tuple-element.608.refs_0_) | copy-start | bytes 860164
  53.3 12.1 %copy-start.7 = (bf16[5,56,512]{2,1,0:T(8,128)(2,1)S(1)}, bf16[5,56,512]{2,1,0:T(8,128)(2,1)}, u32[]{:S(2)}) copy-start(bf16[5,56,512]{2,1,0:T(8,128)(2,1)} %get-tuple-element.613.refs_1_.refs_4_.refs_5_) | copy-start | bytes 860164
  65.3 4.0 copy-start.26
  70.7 74.5 %copy-start.71 = (f32[1,1120]{1,0:T(1,128)S(1)}, f32[1,1120]{1,0:T(1,128)}, u32[]{:S(2)}) copy-start(f32[1,1120]{1,0:T(1,128)} %get-tuple-element.796.refs_0_) | copy-start | bytes 13444
  143.7 19.4 %collective-permute-start.1 = (bf16[2,5,56,512]{3,2,1,0:T(8,128)(2,1)}, bf16[2,5,56,512]{3,2,1,0:T(8,128)(2,1)S(1)}, u32[]{:S(2)}, u32[]{:S(2)}) collective-permute-start(bf16[2,5,56,512]{3,2,1,0:T(8,128)(2,1)} %get-tuple-element.515.refs_3_.refs_11_), channel_id=1, source_target_pairs={{0,4},{4,0},{8,12},{12,8},{1,5},{5,1},{9,13},{13,9},{2,6},{6,2},{1... | collective-permute-start | bytes 1720328 | tf_op jit(solution)/shard_map/ppermute | solution.py:26
  151.6 11.5 %copy-start.9 = (bf16[5,56,512]{2,1,0:T(8,128)(2,1)S(1)}, bf16[5,56,512]{2,1,0:T(8,128)(2,1)}, u32[]{:S(2)}) copy-start(bf16[5,56,512]{2,1,0:T(8,128)(2,1)} %get-tuple-element.504.refs_0_) | copy-start | bytes 860164
  151.6 11.5 %copy-start.11 = (bf16[5,56,512]{2,1,0:T(8,128)(2,1)S(1)}, bf16[5,56,512]{2,1,0:T(8,128)(2,1)}, u32[]{:S(2)}) copy-start(bf16[5,56,512]{2,1,0:T(8,128)(2,1)} %get-tuple-element.509.refs_1_.refs_4_.refs_5_) | copy-start | bytes 860164
  163.0 4.0 copy-start.30
  290.3 32.2 %collective-permute-start.4 = (bf16[2,288,1120]{2,1,0:T(8,128)(2,1)S(1)}, bf16[2,288,1120]{2,1,0:T(8,128)(2,1)}, u32[]{:S(2)}, u32[]{:S(2)}) collective-permute-start(bf16[2,288,1120]{2,1,0:T(8,128)(2,1)S(1)} %slice.381), channel_id=1, source_target_pairs={{0,16},{16,0},{1,17},{17,1},{2,18},{18,2},{3,19},{19,3},{4,20},{20... | collective-permute-start | bytes 3870728 | tf_op jit(solution)/shard_map/ppermute | solution.py:26
  292.9 115.2 %collective-permute-start.5 = (bf16[2,272,1120]{2,1,0:T(8,128)(2,1)}, bf16[2,272,1120]{2,1,0:T(8,128)(2,1)}, u32[]{:S(2)}, u32[]{:S(2)}) collective-permute-start(bf16[2,272,1120]{2,1,0:T(8,128)(2,1)} %slice.383), channel_id=1, source_target_pairs={{0,16},{16,0},{1,17},{17,1},{2,18},{18,2},{3,19},{19,3},{4,20},{20... | collective-permute-start | bytes 3655688 | tf_op jit(solution)/shard_map/ppermute | solution.py:26
  298.5 11.4 %copy-start.21 = (bf16[2,5,56,512]{3,2,1,0:T(8,128)(2,1)S(1)}, bf16[2,5,56,512]{3,2,1,0:T(8,128)(2,1)}, u32[]{:S(2)}) copy-start(bf16[2,5,56,512]{3,2,1,0:T(8,128)(2,1)} %get-tuple-element.514.refs_2_.refs_10_) | copy-start | bytes 1720324
  298.5 11.4 %copy-start.23 = (bf16[2,5,56,512]{3,2,1,0:T(8,128)(2,1)S(1)}, bf16[2,5,56,512]{3,2,1,0:T(8,128)(2,1)}, u32[]{:S(2)}) copy-start(bf16[2,5,56,512]{3,2,1,0:T(8,128)(2,1)} %get-tuple-element.515.refs_3_.refs_11_) | copy-start | bytes 1720324
  307.8 17.6 %collective-permute-start.2 = (bf16[2,5,56,512]{3,2,1,0:T(8,128)(2,1)S(1)}, bf16[2,5,56,512]{3,2,1,0:T(8,128)(2,1)S(1)}, u32[]{:S(2)}, u32[]{:S(2)}) collective-permute-start(bf16[2,5,56,512]{3,2,1,0:T(8,128)(2,1)S(1)} %get-tuple-element.500), channel_id=1, source_target_pairs={{0,4},{4,0},{8,12},{12,8},{1,5},{5,1},{9,13},{13,9},{2,6},{6,2},{1... | collective-permute-start | bytes 1720328 | tf_op jit(solution)/shard_map/ppermute | solution.py:26
  308.8 26.4 %collective-permute-start.3 = (bf16[2,5,56,512]{3,2,1,0:T(8,128)(2,1)S(1)}, bf16[2,5,56,512]{3,2,1,0:T(8,128)(2,1)S(1)}, u32[]{:S(2)}, u32[]{:S(2)}) collective-permute-start(bf16[2,5,56,512]{3,2,1,0:T(8,128)(2,1)S(1)} %get-tuple-element.501), channel_id=1, source_target_pairs={{0,4},{4,0},{8,12},{12,8},{1,5},{5,1},{9,13},{13,9},{2,6},{6,2},{1... | collective-permute-start | bytes 1720328 | tf_op jit(solution)/shard_map/ppermute | solution.py:26
  321.5 3.9 copy-start.38
  325.4 9.8 %copy-start.66 = (bf16[2,5,56,512]{3,2,1,0:T(8,128)(2,1)}, bf16[2,5,56,512]{3,2,1,0:T(8,128)(2,1)S(1)}, u32[]{:S(2)}) copy-start(bf16[2,5,56,512]{3,2,1,0:T(8,128)(2,1)S(1)} %collective-permute-done.2.refs_11_) | copy-start | bytes 1720324
  414.4 44.8 %collective-permute-start.6 = (bf16[272,1120]{1,0:T(8,128)(2,1)S(1)}, bf16[272,1120]{1,0:T(8,128)(2,1)S(1)}, u32[]{:S(2)}, u32[]{:S(2)}) collective-permute-start(bf16[272,1120]{1,0:T(8,128)(2,1)S(1)} %get-tuple-element.742), channel_id=1, source_target_pairs={{0,4},{4,0},{8,12},{12,8},{1,5},{5,1},{9,13},{13,9},{2,6},{6,2},{1... | collective-permute-start | bytes 1827848 | tf_op jit(solution)/shard_map/ppermute | solution.py:26
  420.1 36.9 %collective-permute-start.7 = (bf16[2,280,1120]{2,1,0:T(8,128)(2,1)S(1)}, bf16[2,280,1120]{2,1,0:T(8,128)(2,1)S(1)}, u32[]{:S(2)}, u32[]{:S(2)}) collective-permute-start(bf16[2,280,1120]{2,1,0:T(8,128)(2,1)S(1)} %get-tuple-element.736), channel_id=1, source_target_pairs={{0,16},{16,0},{1,17},{17,1},{2,18},{18,2},{3,19},{19,3},{4,20},{20... | collective-permute-start | bytes 3763208 | tf_op jit(solution)/shard_map/ppermute | solution.py:26
  421.1 127.6 %collective-permute-start.11 = (bf16[2,288,1120]{2,1,0:T(8,128)(2,1)}, bf16[2,288,1120]{2,1,0:T(8,128)(2,1)}, u32[]{:S(2)}, u32[]{:S(2)}) collective-permute-start(bf16[2,288,1120]{2,1,0:T(8,128)(2,1)} %get-tuple-element.686.refs_11_), channel_id=1, source_target_pairs={{0,16},{16,0},{1,17},{17,1},{2,18},{18,2},{3,19},{19,3},{4,20},{20... | collective-permute-start | bytes 3870728 | tf_op jit(solution)/shard_map/ppermute | solution.py:26
  434.2 11.3 %copy-start.17 = (bf16[2,5,56,512]{3,2,1,0:T(8,128)(2,1)S(1)}, bf16[2,5,56,512]{3,2,1,0:T(8,128)(2,1)}, u32[]{:S(2)}) copy-start(bf16[2,5,56,512]{3,2,1,0:T(8,128)(2,1)} %get-tuple-element.618.refs_2_.refs_10_) | copy-start | bytes 1720324
  434.2 11.3 %copy-start.19 = (bf16[2,5,56,512]{3,2,1,0:T(8,128)(2,1)S(1)}, bf16[2,5,56,512]{3,2,1,0:T(8,128)(2,1)}, u32[]{:S(2)}) copy-start(bf16[2,5,56,512]{3,2,1,0:T(8,128)(2,1)} %get-tuple-element.619.refs_3_.refs_11_) | copy-start | bytes 1720324
  443.3 16.8 %collective-permute-start.8 = (bf16[2,5,56,512]{3,2,1,0:T(8,128)(2,1)S(1)}, bf16[2,5,56,512]{3,2,1,0:T(8,128)(2,1)S(1)}, u32[]{:S(2)}, u32[]{:S(2)}) collective-permute-start(bf16[2,5,56,512]{3,2,1,0:T(8,128)(2,1)S(1)} %get-tuple-element.627), channel_id=1, source_target_pairs={{0,4},{4,0},{8,12},{12,8},{1,5},{5,1},{9,13},{13,9},{2,6},{6,2},{1... | collective-permute-start | bytes 1720328 | tf_op jit(solution)/shard_map/ppermute | solution.py:26
  444.4 26.6 %collective-permute-start.9 = (bf16[2,5,56,512]{3,2,1,0:T(8,128)(2,1)S(1)}, bf16[2,5,56,512]{3,2,1,0:T(8,128)(2,1)S(1)}, u32[]{:S(2)}, u32[]{:S(2)}) collective-permute-start(bf16[2,5,56,512]{3,2,1,0:T(8,128)(2,1)S(1)} %get-tuple-element.628), channel_id=1, source_target_pairs={{0,4},{4,0},{8,12},{12,8},{1,5},{5,1},{9,13},{13,9},{2,6},{6,2},{1... | collective-permute-start | bytes 1720328 | tf_op jit(solution)/shard_map/ppermute | solution.py:26
  457.1 91.6 %collective-permute-start.10 = (bf16[2,560,1120]{2,1,0:T(8,128)(2,1)}, bf16[2,560,1120]{2,1,0:T(8,128)(2,1)}, u32[]{:S(2)}, u32[]{:S(2)}) collective-permute-start(bf16[2,560,1120]{2,1,0:T(8,128)(2,1)} %get-tuple-element.722), channel_id=1, source_target_pairs={{0,16},{16,0},{1,17},{17,1},{2,18},{18,2},{3,19},{19,3},{4,20},{20... | collective-permute-start | bytes 7526408 | tf_op jit(solution)/shard_map/ppermute | solution.py:26
  460.2 11.7 %copy-start.68 = (bf16[2,5,56,512]{3,2,1,0:T(8,128)(2,1)}, bf16[2,5,56,512]{3,2,1,0:T(8,128)(2,1)S(1)}, u32[]{:S(2)}) copy-start(bf16[2,5,56,512]{3,2,1,0:T(8,128)(2,1)S(1)} %collective-permute-done.8.refs_8_) | copy-start | bytes 1720324
  (71 other events, 129.0 us)

commit v4 on v3

--- a/solution.py
+++ b/solution.py
@@ -271,7 +271,7 @@
         in_specs=[pl.BlockSpec(memory_space=pltpu.SMEM)] + [vmem] * len(operands),
         out_specs=(vmem,) * (len(shapes) * len(queries)),
         scratch_shapes=[pltpu.VMEM(shape, F32) for shape in state] * len(queries) if last else [],
-        compiler_params=pltpu.CompilerParams(vmem_limit_bytes=24 << 20),
+        compiler_params=pltpu.CompilerParams(vmem_limit_bytes=62 << 20),
         cost_estimate=SMALL_COST,
     )(info, *operands)
     return [results[len(shapes) * i : len(shapes) * (i + 1)] for i in range(len(queries))]
@@ -293,7 +293,7 @@
             pltpu.VMEM((len(given), heads, 1, tokens), F32),
             pltpu.VMEM((2, heads, head_size, tokens), F32),
         ],
-        compiler_params=pltpu.CompilerParams(vmem_limit_bytes=32 << 20),
+        compiler_params=pltpu.CompilerParams(vmem_limit_bytes=62 << 20),
         cost_estimate=SMALL_COST,
     )(info, *operands)
     return results[: len(given)], results[len(given) :]
@@ -369,12 +369,14 @@
         return self.target
 
 
-def call_kernel(body, given, in_hbm, results, out_hbm, scratch, collective_id):
+def call_kernel(body, given, in_hbm, results, streamed, out_hbm, scratch, collective_id):
+    out_hbm = dict(out_hbm, out=streamed)
     scratch = dict(
         scratch,
+        **jax.tree.map(lambda member: pltpu.VMEM(member.shape, member.dtype), streamed),
         send=pltpu.SemaphoreType.DMA((COPIES,)),
         recv=pltpu.SemaphoreType.DMA((COPIES,)),
-        local=pltpu.SemaphoreType.DMA((12,)),
+        local=pltpu.SemaphoreType.DMA((40,)),
     )
     vmem, hbm = pl.BlockSpec(memory_space=pltpu.VMEM), pl.BlockSpec(memory_space=pl.ANY)
     trees = (given, in_hbm, results, out_hbm, scratch)
@@ -385,6 +387,7 @@
         for leaves, tree in flat:
             found.update(jax.tree.unflatten(tree, refs[at : at + len(leaves)]))
             at += len(leaves)
+        found.update(out=types.SimpleNamespace(**found[next(iter(dict(out=0)))]))
         body(types.SimpleNamespace(**found))
 
     outs = pl.pallas_call(
@@ -400,8 +403,22 @@
     )(*flat[0][0], *flat[1][0])
     count = len(flat[2][0])
     found = jax.tree.unflatten(flat[2][1], outs[:count])
-    found.update(jax.tree.unflatten(flat[3][1], outs[count:]))
+    others = jax.tree.unflatten(flat[3][1], outs[count:])
+    found.update(others.pop(next(iter(dict(out=0)))))
+    found.update(others)
     return found
+
+
+class Flush:
+    def __init__(self, r):
+        self.r, self.copies = r, []
+
+    def __call__(self, source, target):
+        self.copies.append(Local(self.r, 12 + len(self.copies), source, target))
+
+    def finish(self):
+        for copy in self.copies:
+            copy.get()
 
 
 def shape_of(shape, dtype):
@@ -486,6 +503,26 @@
 
     def total(self, rows):
         return self.sent[1, rows].astype(F32) + self.got[1, rows].astype(F32)
+
+
+def add_into(target, left, right):
+    def work(columns):
+        target[:, columns] = (
+            left[:, columns].astype(F32) + right[:, columns].astype(F32)
+        ).astype(BF16)
+
+    by_columns(target.shape[1], work)
+
+
+def weight_grads(r):
+    for j in range(3):
+        total = None
+        for grads, wide in zip(r.grads, r.wide_one):
+            heads = [grads[j, head].astype(F32) for head in range(grads.shape[1])]
+            product = mm(jnp.concatenate(heads, axis=0).astype(BF16), wide[...])
+            total = product if total is None else total + product
+        r.pieces[j // 2, j % 2] = total.astype(BF16)
+    r.pieces[1, 1] = r.out_piece[...]
 
 
 class Sum:
@@ -500,26 +537,18 @@
             self.copy.wait_recv()
             self.copy = None
 
-    def add(self, target, left, right):
-        def work(columns):
-            target[:, columns] = (
-                left[:, columns].astype(F32) + right[:, columns].astype(F32)
-            ).astype(BF16)
-
-        by_columns(target.shape[1], work)
-
     def one(self):
         self.copy = self.wires.start(self.whole.at[1 - self.bit], self.got, pair)
 
     def two(self):
         self.wait()
-        self.add(self.near_sum, self.whole.at[self.bit], self.got)
+        add_into(self.near_sum, self.whole.at[self.bit], self.got)
         self.copy = self.wires.start(self.near_sum, self.got_far, pair_far)
 
     def three(self):
         self.wait()
         mine = self.out.at[self.bit]
-        self.add(mine, self.near_sum, self.got_far)
+        add_into(mine, self.near_sum, self.got_far)
         self.copy = self.wires.start(mine, mine, pair)
 
     def five(self, everything, rows):
@@ -575,6 +604,7 @@
     own = Local(r, 0, r.tokens.at[side], r.own_tokens)
     weight = Local(r, 1, r.qkv_w.at[0], r.own_qkv)
     wires = Wires(r, (near, pair, pair_far))
+    flush = Flush(r)
     arriving = wires.start(
         r.tokens.at[1 - side, :, core_columns(half, core)], r.got_tokens, pair_far
     )
@@ -599,13 +629,29 @@
         norm(0, part, tokens[:, core_columns(half, lax.rem(core + part, 2))])
     project(r, 0, None, weight.get())
     paired = wires.start(r.pair[0], r.got_pair, pair)
+    flush_next(r, flush, 0)
     arriving.wait_recv()
     norm(1, 0, r.got_tokens[...])
     wide = r.wide_one[1]
     to_near = wires.start(wide.at[pl.ds(0, half)], wide.at[pl.ds(half, half)], near)
     project(r, 1, to_near, weight.get())
+    flush_next(r, flush, 1)
     paired.wait_recv()
+    flush(r.got_pair, r.out.got_pair)
+    flush.finish()
     wires.finish()
+
+
+def flush_next(r, flush, i):
+    for own, out in (
+        (r.stream, r.out.stream),
+        (r.wide_one, r.out.wide_one),
+        (r.normed_one, r.out.normed_one),
+        (r.inverse_one, r.out.inverse_one),
+        (r.queries, r.out.queries),
+        (r.pair, r.out.pair),
+    ):
+        flush(own[i], out[i])
 
 
 def next_shapes(half, width, head_shape):
@@ -627,6 +673,7 @@
         start_kernel,
         dict(qkv_b=qkv_b, gain=gain, shift=shift),
         dict(tokens=tokens, qkv_w=qkv_w),
+        {},
         next_shapes(half, width, head_shape),
         {},
         dict(
@@ -649,6 +696,7 @@
     if not last:
         qkv_w = Local(r, 3, r.qkv_w.at[layer + 1], r.own_qkv)
     wires = Wires(r, (near, far) + (() if last else (pair, pair_far)))
+    flush = Flush(r)
     first, second = exchanges_of(r, wires, 2)
     to_near = {}
 
@@ -693,6 +741,14 @@
         for part in (1, 0):
             values = mm(r.hidden[i][halves[part]], down_w.get()[...])
             (second[i].give if part else second[i].keep)(values)
+        for own, out in (
+            (r.wide_two, r.out.wide_two),
+            (r.normed_two, r.out.normed_two),
+            (r.inverse_two, r.out.inverse_two),
+            (r.hidden, r.out.hidden),
+            (r.slope, r.out.slope),
+        ):
+            flush(own[i], out[i])
 
     def leave(i):
         if last:
@@ -708,6 +764,7 @@
                 r.wide_one[i],
             )
             project(r, i, to_near[i], qkv_w.get())
+            flush_next(r, flush, i)
 
     for i in (0, 1):
         attended(i)
@@ -734,6 +791,8 @@
     if not last:
         given.wait_recv()
         paired.wait_recv()
+        flush(r.got_pair, r.out.got_pair)
+    flush.finish()
     wires.finish()
 
 
@@ -742,7 +801,8 @@
     hidden_width = in_hbm["up_w"].shape[2]
     head_shape = given["mixed"][0].shape
     wide_hidden = shape_of((2 * half, hidden_width), BF16)
-    results = dict(
+    results = {}
+    streamed = dict(
         wide_two=twice(shape_of((2 * half, width), BF16)),
         normed_two=twice(shape_of((half, width), BF16)),
         inverse_two=twice(shape_of((half, 1), F32)),
@@ -761,7 +821,7 @@
     if last:
         results.update(low=twice(shape_of((width, half), BF16)))
     else:
-        results.update(next_shapes(half, width, head_shape))
+        streamed.update(next_shapes(half, width, head_shape))
         out_hbm.update(got_grad=shape_of((width, half), BF16))
         scratch.update(own_qkv=pltpu.VMEM(in_hbm["qkv_w"].shape[1:], BF16))
     return call_kernel(
@@ -769,6 +829,7 @@
         given,
         in_hbm,
         results,
+        streamed,
         out_hbm,
         scratch,
         collective_id,
@@ -793,10 +854,14 @@
         partners.append(pair_far)
     if riding:
         partners.append(pair)
+    if riding == 2:
+        partners.append(across)
     wires = Wires(r, partners)
     exchanges = exchanges_of(r, wires, int(not begin) + int(not end))
     to_near = {}
+    flush = Flush(r)
     r.sums[...] = jnp.zeros_like(r.sums)
+    cell = lax.axis_index(CELL)
     if riding:
         rider = Sum(wires, r.whole, r.summed if riding == 2 else None, r.near_sum, r.got_sum, r.got_far)
 
@@ -827,6 +892,7 @@
                 product = mm(rows.astype(BF16), qkv_w.get()[j])
                 values = product if values is None else values + product
             (exchange.give if part else exchange.keep)(values)
+        flush(r.grads[i], r.out.grads[i])
 
     def norm(i, exchange, base, normed_of, inverse_of, gain, at, wide):
         def work(rows):
@@ -864,6 +930,12 @@
                 to_near[i].wait_recv()
             values = contract(out_w.get()[...], r.wide_mid[i][halves[part]], 1, 1)
             put_heads(r.mixed_grad[i], halves[part], values)
+        for own, out in (
+            (r.wide_mid, r.out.wide_mid),
+            (r.mixed_grad, r.out.mixed_grad),
+            (r.grad_out, r.out.grad_out),
+        ):
+            flush(own[i], out[i])
 
     def first_rows(i):
         if i == 0:
@@ -898,20 +970,31 @@
         for part in (1, 0):
             values = contract(r.pre[i][halves[part]], up_w.get()[...], 1, 1)
             (exchange.give if part else exchange.keep)(values)
+        flush(r.pre[i], r.out.pre[i])
+        flush(r.wide[i], r.out.wide[i])
 
     def ride(step):
-        if riding and step == 0:
+        if riding == 1 and step == 0:
             rider.one()
-            if riding == 1:
-                r.late = wires.start(r.near_late, r.far_late, pair_far)
-        elif riding and step == 1:
+            r.late = wires.start(r.near_late, r.far_late, pair_far)
+        elif riding == 1 and step == 1:
             rider.two()
-        elif riding and step == 5:
+        elif riding == 1 and step == 5:
             rider.wait()
-            if riding == 1:
-                r.late.wait_recv()
+            r.late.wait_recv()
+        elif riding == 2 and step == 0:
+            rider.one()
+        elif riding == 2 and step == 1:
+            rider.two()
+            weight_grads(r)
+            r.crossing = wires.start(r.pieces.at[1 - cell], r.got_pieces, across)
         elif riding == 2 and step == 3:
             rider.three()
+            r.crossing.wait_recv()
+            for k in (0, 1):
+                add_into(r.whole_next.at[k], r.pieces.at[cell, k], r.got_pieces.at[k])
+        elif riding == 2 and step == 5:
+            rider.wait()
 
     ride(0)
     if begin:
@@ -953,6 +1036,7 @@
             after[b].wait()
             second_norm(b)
     ride(5)
+    flush.finish()
     wires.finish()
 
 
@@ -983,7 +1067,9 @@
     some = given["block_low"][0] if begin else given["grad"][0]
     width = given["gains"].shape[1]
     half = some.shape[1] if begin else some.shape[0]
-    results = dict(sums=shape_of((8, width), F32), grad_out=twice(shape_of((half, width), F32)))
+    results = dict(sums=shape_of((8, width), F32))
+    streamed = dict()
+    grad_out = twice(shape_of((half, width), F32))
     wide = twice(shape_of((2 * half, width), BF16))
     out_hbm = {}
     scratch = exchange_scratch(half, width, int(not begin) + int(not end))
@@ -992,14 +1078,15 @@
         scratch.update(own_grad=pltpu.VMEM((width, 2 * half), BF16))
     else:
         head_shape = given["query_sum"][0].shape
-        results.update(grads=twice(shape_of((3,) + head_shape, BF16)))
+        streamed.update(grads=twice(shape_of((3,) + head_shape, BF16)))
         scratch.update(own_qkv=pltpu.VMEM(in_hbm["qkv_w"].shape[1:], BF16))
     if end:
-        results.update(low=twice(shape_of((width, half), BF16)))
+        results.update(low=twice(shape_of((width, half), BF16)), grad_out=grad_out)
     else:
         hidden_width = in_hbm["up_w"].shape[2]
         head_count = in_hbm["out_w"].shape[1] // HEAD
-        results.update(
+        streamed.update(
+            grad_out=grad_out,
             wide=wide,
             wide_mid=wide,
             pre=twice(shape_of((2 * half, hidden_width), BF16)),
@@ -1015,8 +1102,17 @@
         whole = given["whole"]
         one = pltpu.VMEM(whole.shape[1:], BF16)
         if riding == 2:
-            results.update(summed=shape_of(whole.shape, BF16))
-            scratch.update(near_sum=one, got_far=one)
+            piece = given["out_piece"].shape
+            results.update(
+                summed=shape_of(whole.shape, BF16),
+                whole_next=shape_of((2,) + piece, BF16),
+            )
+            scratch.update(
+                near_sum=one,
+                got_far=one,
+                pieces=pltpu.VMEM((2, 2) + piece, BF16),
+                got_pieces=pltpu.VMEM((2,) + piece, BF16),
+            )
         else:
             part = shape_of(whole.shape[1:], BF16)
             results.update(near_sum=part, got_far=part)
@@ -1027,6 +1123,7 @@
         given,
         in_hbm,
         results,
+        streamed,
         out_hbm,
         scratch,
         collective_id,
@@ -1054,7 +1151,6 @@
         span = r.sum_feed[0].shape[1]
         spans = [pl.ds(0, span), pl.ds(span, r.all_feed.shape[2] - span)]
         whole = pl.ds(0, r.all_last.shape[2])
-        arriving = wires.start(r.sent_last, r.got_last, across)
         feed = [
             Sum(wires, r.whole_feed[k], r.sum_feed[k], *r.riding_feed[k]) for k in (0, 1)
         ]
@@ -1075,15 +1171,18 @@
             own, target = member.five(everything, rows)
             local.append(Local(r, len(local), own, target))
 
-        late.three()
         fold(r.whole_feed[0], r.kept_feed, r.got_feed, spans[0])
         feed[0].one()
+        late.three()
+        weight_grads(r)
+        arriving = wires.start(r.pieces.at[1 - cell], r.got_last, across)
         local.append(Local(r, 0, r.early, r.all_late.at[cell, :, spans[0]]))
         local.append(Local(r, 1, r.got_early, r.all_late.at[1 - cell, :, spans[0]]))
         add = vectors(0, near, 6)
         feed[0].two()
         arriving.wait_recv()
-        fold(r.whole_last, r.kept_last, r.got_last, whole)
+        for k in (0, 1):
+            add_into(r.whole_last.at[k], r.pieces.at[cell, k], r.got_last.at[k])
         last.one()
         prior.three()
         five(late, r.all_late, spans[1])
@@ -1129,7 +1228,7 @@
     out_hbm = dict(tokens_grad=shape_of((2, width, 2 * half), BF16))
     scratch = dict(total=pltpu.VMEM(vectors, F32), around=pltpu.VMEM((4,) + vectors, F32))
     if sums_too:
-        feed, last = given["kept_feed"].shape, given["kept_last"].shape
+        feed, last = given["kept_feed"].shape, (2,) + given["out_piece"].shape
         late = (2,) + given["near_late"].shape
         early = (feed[0], feed[1] - late[1]) + feed[2:]
         spans = [pltpu.VMEM(early, BF16), pltpu.VMEM(late, BF16)]
@@ -1147,6 +1246,7 @@
             whole_last=pltpu.VMEM(last, BF16),
             sum_last=pltpu.VMEM(last, BF16),
             got_last=pltpu.VMEM(last, BF16),
+            pieces=pltpu.VMEM((2,) + last, BF16),
             riding_last=sum_scratch(*last[1:]),
             sum_prior=pltpu.VMEM(last, BF16),
         )
@@ -1155,6 +1255,7 @@
         given,
         in_hbm,
         results,
+        {},
         out_hbm,
         scratch,
         collective_id,
@@ -1330,11 +1431,16 @@
             in_hbm.update(qkv_w=qkv_weight)
             gain_rows[0] = gains[layer, 0]
             if paired_cells:
-                given.update(whole=line.run(add_low, *pending))
                 riding = 1 if end else 2
                 if end:
                     near_late = line.run(add_low, kept_late, got_late)
-                    given.update(near_late=near_late)
+                    given.update(near_late=near_late, whole=next_whole)
+                else:
+                    given.update(
+                        whole=line.run(add_low, *pending),
+                        wide_one=above.wide_one,
+                        out_piece=out_piece,
+                    )
         if not end:
             below = saved[layer - 1]
             given.update(
@@ -1362,35 +1468,56 @@
             if riding == 2:
                 early = found.summed
                 got_early = swap(early, CELL, 1)
+                next_whole = found.whole_next
                 late = line.run(add_low, *late)
                 bit = seq_index % 2
                 kept_late = jnp.where(bit == 0, late[0], late[1])
                 got_late = swap(jnp.where(bit == 0, late[1], late[0]), SEQ, 1)
-            sums = line.run(attention_sums, wide_mid, above.mixed, above.wide_one, found.grads)
-            if paired_cells:
-                kept, sent = line.run(functools.partial(pick, cell), sums[:2], sums[2:])
-                if not end:
-                    pending = [kept, swap(sent, CELL, 1)]
-            else:
-                halves[layer, 1] = sums
+            elif not paired_cells:
+                halves[layer, 1] = line.run(
+                    attention_sums, wide_mid, above.mixed, above.wide_one, found.grads
+                )
         if end:
             break
         wide_mid = found.wide_mid
-        sums = line.run(feed_sums, below.hidden, found.wide, below.wide_two, found.pre)
-        if paired_cells:
-            kept_feed, sent_feed = line.run(functools.partial(pick, cell), sums[:2], sums[2:])
-            if begin:
-                cut = kept_feed.shape[1] // 32 * 16 + 16
-                pending = [kept_feed[:, :cut], swap(sent_feed[:, :cut], CELL, 1)]
-                late = [kept_feed[:, cut:], swap(sent_feed[:, cut:], CELL, 1)]
-            else:
-                got_feed = swap(sent_feed, CELL, 1)
-        else:
-            halves[layer - 1, 0] = sums
         streams = [
             list(members)
             for members in zip(below.queries, found.mixed_grad, below.mixed, below.log_total)
         ]
+
+        def feed_totals():
+            return line.run(feed_sums, below.hidden, found.wide, below.wide_two, found.pre)
+
+        if paired_cells:
+            sums = feed_totals()
+            if begin:
+                cut = sums[0].shape[0] // 32 * 16 + 16
+                spans = [slice(0, cut), slice(cut, None)]
+
+                def pick_spans(low, high):
+                    return [
+                        pick(cell, [m[span] for m in low], [m[span] for m in high])
+                        for span in spans
+                    ]
+
+                pending, late = (
+                    [kept, swap(sent, CELL, 1)]
+                    for kept, sent in line.run(pick_spans, sums[:2], sums[2:])
+                )
+            else:
+                kept_feed, sent_feed = line.run(
+                    functools.partial(pick, cell), sums[:2], sums[2:]
+                )
+                got_feed = swap(sent_feed, CELL, 1)
+            out_piece = line.run(
+                lambda mixed, wide: two_sum(
+                    lambda left, right: mm(left.reshape(local_width, row_count), right), mixed, wide
+                ),
+                below.mixed,
+                wide_mid,
+            )
+        else:
+            halves[layer - 1, 0] = feed_totals()
         query_sums, far_sums = line.run(
             lambda given, pairs: attend_back(info, given, pairs, 2, False, BF16),
             streams,
@@ -1412,8 +1539,9 @@
         given.update(
             kept_feed=kept_feed,
             got_feed=got_feed,
-            kept_last=kept,
-            sent_last=sent,
+            grads=found.grads,
+            wide_one=above.wide_one,
+            out_piece=out_piece,
             near_late=near_late,
             far_late=found.far_late,
             near_prior=found.near_sum,
@@ -1441,6 +1569,9 @@
 
     def final(pieces):
         return jnp.stack([piece.astype(F32) for piece in pieces])
+
+    def quarters(member):
+        return member.reshape((4,) + member.shape[2:])
 
     def square(member):
         return member.reshape(member.shape[0] * member.shape[1], member.shape[2])
@@ -1463,10 +1594,10 @@
         jnp.swapaxes(block_out, 1, 2),
         jnp.swapaxes(closing.tokens_grad, 1, 2),
         jnp.swapaxes(
-            final([jnp.stack([*member[0], member[1, 0]]) for member in attentions]), 2, 3
+            final([quarters(member)[:3] for member in attentions]), 2, 3
         ),
         qv_grad,
-        final([member[1, 1] for member in attentions]),
+        final([quarters(member)[3] for member in attentions]),
         rows_of(feed_rows, 5),
         final([square(member[0]) for member in feeds]),
         rows_of(feed_rows, 6),

time: 801 us -> 767 us (0.958)
  local copies, waits for them, and re-layouts: 48.8 us -> 21.8 us
  Pallas kernels: 647 us -> 637 us
    unnamed x187 -> x91, local copies, waits for them, and re-layouts: 35.2 us -> 13.2 us
    pallas_call x7, Pallas kernels: 575 us -> 554 us  [call_kernel(): pl.pallas_call(kernel, out_shape=tuple(flat[2][0] + flat[3][0]), in_specs...]
    dot_general x24 -> x12, matrix products: 24.4 us -> 20.6 us  [contract(): lax.dot_general(left, right, (((left_dim,), (right_dim,)), ((), ())), pre...]
    ppermute x12 -> x11, waiting for transfers between devices: 21.5 us -> 23.2 us  [swap(): return lax.ppermute(values, axis, [(i, i ^ bit) for i in range(size)])]
  transfers between devices with their start and end apart: 12 -> 11, of which waited for: 3 -> 4; matrix products, arithmetic and copies ran while one was open for 5% -> 2% of each run, Pallas kernels for 25% -> 27%
where the time goes in v4:
time: 767 us; the launch traced here: 756 us
  Pallas kernels  637 us (83%)
  other arithmetic  36.6 us (5%)
  waiting for transfers between devices  23.2 us (3%)
  local copies, waits for them, and re-layouts  21.8 us (3%)
  matrix products  20.6 us (3%)
  starting transfers between devices  13.6 us (2%)
    pallas_call x7, Pallas kernels, call_kernel(): pl.pallas_call(kernel, out_shape=tuple(flat[2][0] + flat[3][0]), in_specs...  554 us
    pallas_call x4, Pallas kernels, attend_back(): pl.pallas_call(functools.partial(attend_back_kernel, first_chunk, len(pai...  47.7 us
    pallas_call x4, Pallas kernels, attend(): pl.pallas_call(functools.partial(attend_kernel, first_chunk, len(pairs),...  34.5 us
    ppermute x11, waiting for transfers between devices, swap(): return lax.ppermute(values, axis, [(i, i ^ bit) for i in range(size)])  23.2 us
    dot_general x12, matrix products, contract(): lax.dot_general(left, right, (((left_dim,), (right_dim,)), ((), ())), pre...  20.6 us
  transfers between devices with their start and end apart: 11, of which 4 were waited for; matrix products, arithmetic and copies ran while one was open for 2% of the time, Pallas kernels for 27%

profile of v4, /device:TPU:0, one launch (start us, length us, event | category | flops | bytes accessed | tf_op | source)
XLA Modules:
  0.0 755.6 jit_solution(9548547370840449802)
XLA Ops:
  4.2 38.6 %shard_map.238 = (bf16[2,5,56,512]{3,2,1,0:T(8,128)(2,1)}, f32[256,1]{1,0:T(8,128)}, f32[256,1]{1,0:T(8,128)}, bf16[256,1120]{1,0:T(8,128)(2,1)}, bf16[256,1120]...) custom-call(f32[1,1120]{1,0:T(1,128)} %get-tuple-element.752.refs_0_, ...), custom_call_target="tpu_custom_call" | custom-call | flops 1048576 | bytes 1048576 | tf_op jit(solution)/shard_map/pallas_call | solution.py:393
  46.4 11.4 %shard_map.239 = (f32[5,1,512]{2,1,0:T(1,128)}, f32[5,1,512]{2,1,0:T(1,128)}, f32[5,56,512]{2,1,0:T(8,128)}, f32[5,1,512]{2,1,0:T(1,128)}, f32[5,1,512]{2,1,0:T(1,128)}, /*index=5*/f32[5,56,512]{2,1,0:T(8,128)}) custom-call(s32[13]{0:T(128)} %pad_add_fusion.info, bf16[5,56,512]{2,1,0:T(8,128)(2,1)} %get-tuple-element.594.refs_0_, ...), custom_call_target="tpu_custom_call" | custom-call | flops 1048576 | bytes 1048576 | tf_op jit(solution)/shard_map/pallas_call | solution.py:266
  59.2 5.9 shard_map.240
  65.1 68.1 %shard_map.241 = (bf16[1120,256]{1,0:T(8,128)(2,1)}, bf16[2,5,56,512]{3,2,1,0:T(8,128)(2,1)}, bf16[512,1120]{1,0:T(8,128)(2,1)}, bf16[512,1120]{1,0:T(8,128)(2,1...) custom-call(f32[256,1120]{1,0:T(8,128)} %get-tuple-element.369.refs_, ...), custom_call_target="tpu_custom_call" | custom-call | flops 1048576 | bytes 1048576 | tf_op jit(solution)/shard_map/pallas_call | solution.py:393
  136.5 11.4 %shard_map.242 = (f32[5,1,512]{2,1,0:T(1,128)}, f32[5,1,512]{2,1,0:T(1,128)}, f32[5,56,512]{2,1,0:T(8,128)}, f32[5,1,512]{2,1,0:T(1,128)}, f32[5,1,512]{2,1,0:T(1,128)}, /*index=5*/f32[5,56,512]{2,1,0:T(8,128)}) custom-call(s32[13]{0:T(128)} %pad_add_fusion.info, bf16[5,56,512]{2,1,0:T(8,128)(2,1)} %get-tuple-element.497.refs_0_, ...), custom_call_target="tpu_custom_call" | custom-call | flops 1048576 | bytes 1048576 | tf_op jit(solution)/shard_map/pallas_call | solution.py:266
  149.2 5.8 shard_map.243
  155.0 60.4 %shard_map.244 = (bf16[1120,256]{1,0:T(8,128)(2,1)}, bf16[1120,256]{1,0:T(8,128)(2,1)}, bf16[512,1120]{1,0:T(8,128)(2,1)}, bf16[512,1120]{1,0:T(8,128)(2,1)}, f3...) custom-call(f32[256,1120]{1,0:T(8,128)} %get-tuple-element.411.refs_, ...), custom_call_target="tpu_custom_call" | custom-call | flops 1048576 | bytes 1048576 | tf_op jit(solution)/shard_map/pallas_call | solution.py:393
  215.4 45.3 %shard_map.245 = (f32[8,1120]{1,0:T(8,128)}, bf16[2,1120,512]{2,1,0:T(8,128)(2,1)}, f32[256,1120]{1,0:T(8,128)}, f32[256,1120]{1,0:T(8,128)}, bf16[5,56,512]{2,1...) custom-call(bf16[1120,256]{1,0:T(8,128)(2,1)} %get-tuple-element.429, ...), custom_call_target="tpu_custom_call" | custom-call | flops 1048576 | bytes 1048576 | tf_op jit(solution)/shard_map/pallas_call | solution.py:393
  260.8 3.1 fusion.17
  269.0 1.8 fusion.1
  273.0 4.7 collective-permute-start.4
  277.7 1.9 broadcast_select_fusion.4
  282.3 12.1 %shard_map.246 = (f32[5,56,512]{2,1,0:T(8,128)}, f32[5,56,512]{2,1,0:T(8,128)}, bf16[2,5,56,512]{3,2,1,0:T(8,128)(2,1)}, bf16[2,5,56,512]{3,2,1,0:T(8,128)(2,1)}) custom-call(s32[13]{0:T(128)} %pad_add_fusion.info, bf16[5,56,512]{2,1,0:T(8,128)(2,1)} %get-tuple-element.497.refs_0_, bf16[5,56,512]{2,1,0:T(8,128)(2,1)} %get-tuple-element.498.refs_1_, ...), custom_call_target="tpu_custom_call" | custom-call | flops 1048576 | bytes 1048576 | tf_op jit(solution)/shard_map/pallas_call | solution.py:284
  294.4 2.0 collective-permute-start.3
  296.4 11.8 %shard_map.247 = (f32[5,56,512]{2,1,0:T(8,128)}, f32[5,56,512]{2,1,0:T(8,128)}, f32[2,5,56,512]{3,2,1,0:T(8,128)}, f32[2,5,56,512]{3,2,1,0:T(8,128)}) custom-call(s32[13]{0:T(128)} %pad_add_fusion.info, bf16[5,56,512]{2,1,0:T(8,128)(2,1)} %get-tuple-element.497.refs_0_, bf16[5,56,512]{2,1,0:T(8,128)(2,1)} %get-tuple-element.498.refs_1_, ...), custom_call_target="tpu_custom_call" | custom-call | flops 1048576 | bytes 1048576 | tf_op jit(solution)/shard_map/pallas_call | solution.py:284
  308.3 2.7 add_convert_fusion.refs_20_
  311.0 11.3 %collective-permute-done.3.refs_13_ = bf16[2,5,56,512]{3,2,1,0:T(8,128)(2,1)} collective-permute-done((bf16[2,5,56,512]{3,2,1,0:T(8,128)(2,1)}, bf16[2,5,56,512]{3,2,1,0:T(8,128)(2,1)}, u32[]{:S(2)}, u32[]{:S(2)}) %collective-permute-start.3) | collective-permute-done | bytes 573472 | tf_op jit(solution)/shard_map/ppermute | solution.py:26
  322.3 70.4 %shard_map.248 = (bf16[2,288,1120]{2,1,0:T(8,128)(2,1)}, f32[8,1120]{1,0:T(8,128)}, bf16[2,280,1120]{2,1,0:T(8,128)(2,1)}, f32[256,1120]{1,0:T(8,128)}, f32[256,...) custom-call(f32[2,1120]{1,0:T(2,128)} %pad_maximum_fusion.13.refs_0_, ...), custom_call_target="tpu_custom_call" | custom-call | flops 1048576 | bytes 1048576 | tf_op jit(solution)/shard_map/pallas_call | solution.py:393
  403.6 2.9 broadcast_select_fusion
  406.6 1.9 collective-permute-start.9
  410.9 1.9 fusion.22
  414.2 11.9 %shard_map.249 = (f32[5,56,512]{2,1,0:T(8,128)}, f32[5,56,512]{2,1,0:T(8,128)}, bf16[2,5,56,512]{3,2,1,0:T(8,128)(2,1)}, bf16[2,5,56,512]{3,2,1,0:T(8,128)(2,1)}) custom-call(s32[13]{0:T(128)} %pad_add_fusion.info, bf16[5,56,512]{2,1,0:T(8,128)(2,1)} %get-tuple-element.594.refs_0_, bf16[5,56,512]{2,1,0:T(8,128)(2,1)} %get-tuple-element.595.refs_1_, ...), custom_call_target="tpu_custom_call" | custom-call | flops 1048576 | bytes 1048576 | tf_op jit(solution)/shard_map/pallas_call | solution.py:284
  426.2 2.0 collective-permute-start.8
  428.2 11.8 %shard_map.250 = (f32[5,56,512]{2,1,0:T(8,128)}, f32[5,56,512]{2,1,0:T(8,128)}, f32[2,5,56,512]{3,2,1,0:T(8,128)}, f32[2,5,56,512]{3,2,1,0:T(8,128)}) custom-call(s32[13]{0:T(128)} %pad_add_fusion.info, bf16[5,56,512]{2,1,0:T(8,128)(2,1)} %get-tuple-element.594.refs_0_, bf16[5,56,512]{2,1,0:T(8,128)(2,1)} %get-tuple-element.595.refs_1_, ...), custom_call_target="tpu_custom_call" | custom-call | flops 1048576 | bytes 1048576 | tf_op jit(solution)/shard_map/pallas_call | solution.py:284
  440.0 2.1 add_convert_fusion.2.refs_5_.refs_8_
  442.4 11.2 %collective-permute-done.8.refs_9_ = bf16[2,5,56,512]{3,2,1,0:T(8,128)(2,1)} collective-permute-done((bf16[2,5,56,512]{3,2,1,0:T(8,128)(2,1)}, bf16[2,5,56,512]{3,2,1,0:T(8,128)(2,1)}, u32[]{:S(2)}, u32[]{:S(2)}) %collective-permute-start.8) | collective-permute-done | bytes 573472 | tf_op jit(solution)/shard_map/ppermute | solution.py:26
  453.5 64.7 %shard_map.251 = (bf16[272,1120]{1,0:T(8,128)(2,1)}, bf16[280,1120]{1,0:T(8,128)(2,1)}, f32[256,1120]{1,0:T(8,128)}, f32[256,1120]{1,0:T(8,128)}, bf16[1120,256]...) custom-call(f32[2,1120]{1,0:T(2,128)} %get-tuple-element.617.refs_0_, ...), custom_call_target="tpu_custom_call" | custom-call | flops 1048576 | bytes 1048576 | tf_op jit(solution)/shard_map/pallas_call | solution.py:393
  519.7 207.0 %shard_map.252 = (f32[3,8,1120]{2,1,0:T(8,128)}, bf16[2,2,560,1120]{3,2,1,0:T(8,128)(2,1)}, bf16[2,2,280,1120]{3,2,1,0:T(8,128)(2,1)}, bf16[2,2,560,1120]{3,2,1,...) custom-call(bf16[272,1120]{1,0:T(8,128)(2,1)} %get-tuple-element.646.refs_0_, ...), custom_call_target="tpu_custom_call" | custom-call | flops 1048576 | bytes 1048576 | tf_op jit(solution)/shard_map/pallas_call | solution.py:393
  727.8 1.8 slice_bitcast_fusion.1
  738.1 3.7 convert_bitcast_fusion
  741.8 4.7 maximum_convert_fusion
  746.6 4.7 maximum_convert_fusion.1
  (172 shorter events, 51.4 us)
Async XLA Ops:
  4.2 38.7 %copy-start.40 = (s32[6]{0:T(128)S(1)}, s32[6]{0:T(128)}, u32[]{:S(2)}) copy-start(s32[6]{0:T(128)} %constant.55.clone) | copy-start | bytes 76
  4.2 38.9 %copy-start.31 = (s32[2,8]{1,0:T(2,128)S(1)}, s32[2,8]{1,0:T(2,128)}, u32[]{:S(2)}) copy-start(s32[2,8]{1,0:T(2,128)} %param.17) | copy-start | bytes 196
  4.2 39.0 %copy-start.28 = (bf16[2,1120]{1,0:T(2,128)(2,1)S(1)}, bf16[2,1120]{1,0:T(2,128)(2,1)}, u32[]{:S(2)}) copy-start(bf16[2,1120]{1,0:T(2,128)(2,1)} %param.26) | copy-start | bytes 13444
  4.2 39.0 %copy-start.29 = (bf16[2,1120]{1,0:T(2,128)(2,1)S(1)}, bf16[2,1120]{1,0:T(2,128)(2,1)}, u32[]{:S(2)}) copy-start(bf16[2,1120]{1,0:T(2,128)(2,1)} %param.22) | copy-start | bytes 13444
  4.2 39.0 %copy-start.30 = (s32[2]{0:T(128)S(1)}, s32[2]{0:T(128)}, u32[]{:S(2)}) copy-start(s32[2]{0:T(128)} %param.18) | copy-start | bytes 28
  42.8 15.0 %copy-start.27 = (bf16[2,1120]{1,0:T(2,128)(2,1)S(1)}, bf16[2,1120]{1,0:T(2,128)(2,1)}, u32[]{:S(2)}) copy-start(bf16[2,1120]{1,0:T(2,128)(2,1)} %param.24) | copy-start | bytes 13444
  42.8 15.6 %collective-permute-start = (bf16[2,5,56,512]{3,2,1,0:T(8,128)(2,1)}, bf16[2,5,56,512]{3,2,1,0:T(8,128)(2,1)S(1)}, u32[]{:S(2)}, u32[]{:S(2)}) collective-permute-start(bf16[2,5,56,512]{3,2,1,0:T(8,128)(2,1)} %get-tuple-element.605.refs_3_.refs_11_), channel_id=1, source_target_pairs={{0,4},{4,0},{8,12},{12,8},{1,5},{5,1},{9,13},{13,9},{2,6},{6,2},{1... | collective-permute-start | bytes 1720328 | tf_op jit(solution)/shard_map/ppermute | solution.py:26
  65.1 70.1 %copy-start.24 = (f32[1,1120]{1,0:T(1,128)S(1)}, f32[1,1120]{1,0:T(1,128)}, u32[]{:S(2)}) copy-start(f32[1,1120]{1,0:T(1,128)} %get-tuple-element.752.refs_0_) | copy-start | bytes 13444
  133.2 15.2 %collective-permute-start.1 = (bf16[2,5,56,512]{3,2,1,0:T(8,128)(2,1)}, bf16[2,5,56,512]{3,2,1,0:T(8,128)(2,1)S(1)}, u32[]{:S(2)}, u32[]{:S(2)}) collective-permute-start(bf16[2,5,56,512]{3,2,1,0:T(8,128)(2,1)} %get-tuple-element.508.refs_3_.refs_11_), channel_id=1, source_target_pairs={{0,4},{4,0},{8,12},{12,8},{1,5},{5,1},{9,13},{13,9},{2,6},{6,2},{1... | collective-permute-start | bytes 1720328 | tf_op jit(solution)/shard_map/ppermute | solution.py:26
  215.4 45.3 %copy-start.14 = (bf16[512,1120]{1,0:T(8,128)(2,1)S(1)}, bf16[512,1120]{1,0:T(8,128)(2,1)}, u32[]{:S(2)}) copy-start(bf16[512,1120]{1,0:T(8,128)(2,1)} %get-tuple-element.463) | copy-start | bytes 3440644
  260.7 3.1 copy-start.38
  260.7 3.1 copy-start.39
  273.0 35.3 %collective-permute-start.4 = (bf16[2,288,1120]{2,1,0:T(8,128)(2,1)}, bf16[2,288,1120]{2,1,0:T(8,128)(2,1)}, u32[]{:S(2)}, u32[]{:S(2)}) collective-permute-start(bf16[2,288,1120]{2,1,0:T(8,128)(2,1)} %get-tuple-element.698), channel_id=1, source_target_pairs={{0,16},{16,0},{1,17},{17,1},{2,18},{18,2},{3,19},{19,3},{4,20},{20... | collective-permute-start | bytes 3870728 | tf_op jit(solution)/shard_map/ppermute | solution.py:26
  279.6 113.2 %collective-permute-start.5 = (bf16[2,272,1120]{2,1,0:T(8,128)(2,1)}, bf16[2,272,1120]{2,1,0:T(8,128)(2,1)}, u32[]{:S(2)}, u32[]{:S(2)}) collective-permute-start(bf16[2,272,1120]{2,1,0:T(8,128)(2,1)} %get-tuple-element.708), channel_id=1, source_target_pairs={{0,16},{16,0},{1,17},{17,1},{2,18},{18,2},{3,19},{19,3},{4,20},{20... | collective-permute-start | bytes 3655688 | tf_op jit(solution)/shard_map/ppermute | solution.py:26
  294.4 16.6 %collective-permute-start.2 = (bf16[2,5,56,512]{3,2,1,0:T(8,128)(2,1)}, bf16[2,5,56,512]{3,2,1,0:T(8,128)(2,1)S(1)}, u32[]{:S(2)}, u32[]{:S(2)}) collective-permute-start(bf16[2,5,56,512]{3,2,1,0:T(8,128)(2,1)} %get-tuple-element.493), channel_id=1, source_target_pairs={{0,4},{4,0},{8,12},{12,8},{1,5},{5,1},{9,13},{13,9},{2,6},{6,2},{1... | collective-permute-start | bytes 1720328 | tf_op jit(solution)/shard_map/ppermute | solution.py:26
  294.4 27.9 %collective-permute-start.3 = (bf16[2,5,56,512]{3,2,1,0:T(8,128)(2,1)}, bf16[2,5,56,512]{3,2,1,0:T(8,128)(2,1)}, u32[]{:S(2)}, u32[]{:S(2)}) collective-permute-start(bf16[2,5,56,512]{3,2,1,0:T(8,128)(2,1)} %get-tuple-element.494), channel_id=1, source_target_pairs={{0,4},{4,0},{8,12},{12,8},{1,5},{5,1},{9,13},{13,9},{2,6},{6,2},{1... | collective-permute-start | bytes 1720328 | tf_op jit(solution)/shard_map/ppermute | solution.py:26
  311.0 11.3 %copy-start.22 = (bf16[2,5,56,512]{3,2,1,0:T(8,128)(2,1)}, bf16[2,5,56,512]{3,2,1,0:T(8,128)(2,1)S(1)}, u32[]{:S(2)}) copy-start(bf16[2,5,56,512]{3,2,1,0:T(8,128)(2,1)S(1)} %collective-permute-done.2.refs_12_) | copy-start | bytes 1720324
  322.3 70.5 %copy-start.1 = (bf16[2,272,1120]{2,1,0:T(8,128)(2,1)S(1)}, bf16[2,272,1120]{2,1,0:T(8,128)(2,1)}, u32[]{:S(2)}) copy-start(bf16[2,272,1120]{2,1,0:T(8,128)(2,1)} %get-tuple-element.550) | copy-start | bytes 3655684
  406.6 3.8 copy-start.15
  406.6 4.3 copy-start.3
  406.6 113.1 %collective-permute-start.9 = (bf16[2,560,1120]{2,1,0:T(8,128)(2,1)}, bf16[2,560,1120]{2,1,0:T(8,128)(2,1)}, u32[]{:S(2)}, u32[]{:S(2)}) collective-permute-start(bf16[2,560,1120]{2,1,0:T(8,128)(2,1)} %get-tuple-element.696), channel_id=1, source_target_pairs={{0,16},{16,0},{1,17},{17,1},{2,18},{18,2},{3,19},{19,3},{4,20},{20... | collective-permute-start | bytes 7526408 | tf_op jit(solution)/shard_map/ppermute | solution.py:26
  409.4 30.7 %collective-permute-start.6 = (bf16[272,1120]{1,0:T(8,128)(2,1)}, bf16[272,1120]{1,0:T(8,128)(2,1)}, u32[]{:S(2)}, u32[]{:S(2)}) collective-permute-start(bf16[272,1120]{1,0:T(8,128)(2,1)} %get-tuple-element.710), channel_id=1, source_target_pairs={{0,4},{4,0},{8,12},{12,8},{1,5},{5,1},{9,13},{13,9},{2,6},{6,2},{1... | collective-permute-start | bytes 1827848 | tf_op jit(solution)/shard_map/ppermute | solution.py:26
  410.4 109.3 %collective-permute-start.10 = (bf16[2,288,1120]{2,1,0:T(8,128)(2,1)S(1)}, bf16[2,288,1120]{2,1,0:T(8,128)(2,1)}, u32[]{:S(2)}, u32[]{:S(2)}) collective-permute-start(bf16[2,288,1120]{2,1,0:T(8,128)(2,1)S(1)} %copy-done.15), channel_id=1, source_target_pairs={{0,16},{16,0},{1,17},{17,1},{2,18},{18,2},{3,19},{19,3},{4,20},{20... | collective-permute-start | bytes 3870728 | tf_op jit(solution)/shard_map/ppermute | solution.py:26
  426.2 16.2 %collective-permute-start.7 = (bf16[2,5,56,512]{3,2,1,0:T(8,128)(2,1)}, bf16[2,5,56,512]{3,2,1,0:T(8,128)(2,1)}, u32[]{:S(2)}, u32[]{:S(2)}) collective-permute-start(bf16[2,5,56,512]{3,2,1,0:T(8,128)(2,1)} %get-tuple-element.611), channel_id=1, source_target_pairs={{0,4},{4,0},{8,12},{12,8},{1,5},{5,1},{9,13},{13,9},{2,6},{6,2},{1... | collective-permute-start | bytes 1720328 | tf_op jit(solution)/shard_map/ppermute | solution.py:26
  426.2 27.4 %collective-permute-start.8 = (bf16[2,5,56,512]{3,2,1,0:T(8,128)(2,1)}, bf16[2,5,56,512]{3,2,1,0:T(8,128)(2,1)}, u32[]{:S(2)}, u32[]{:S(2)}) collective-permute-start(bf16[2,5,56,512]{3,2,1,0:T(8,128)(2,1)} %get-tuple-element.612), channel_id=1, source_target_pairs={{0,4},{4,0},{8,12},{12,8},{1,5},{5,1},{9,13},{13,9},{2,6},{6,2},{1... | collective-permute-start | bytes 1720328 | tf_op jit(solution)/shard_map/ppermute | solution.py:26
  453.5 64.7 %copy-start.25 = (f32[8,1120]{1,0:T(8,128)S(1)}, f32[8,1120]{1,0:T(8,128)}, u32[]{:S(2)}) copy-start(f32[8,1120]{1,0:T(8,128)} %get-tuple-element.640) | copy-start | bytes 107524
  453.5 64.7 %copy-start.26 = (f32[8,1120]{1,0:T(8,128)S(1)}, f32[8,1120]{1,0:T(8,128)}, u32[]{:S(2)}) copy-start(f32[8,1120]{1,0:T(8,128)} %get-tuple-element.641) | copy-start | bytes 107524
  727.8 2.5 copy-start.23
  730.1 2.5 copy-start
  731.1 3.1 slice-start
  746.6 4.7 copy-start.9
  751.3 2.5 copy-start.10
  (22 other events, 35.3 us)

commit v5 on v4

--- a/solution.py
+++ b/solution.py
@@ -976,12 +976,10 @@
     def ride(step):
         if riding == 1 and step == 0:
             rider.one()
-            r.late = wires.start(r.near_late, r.far_late, pair_far)
         elif riding == 1 and step == 1:
             rider.two()
         elif riding == 1 and step == 5:
             rider.wait()
-            r.late.wait_recv()
         elif riding == 2 and step == 0:
             rider.one()
         elif riding == 2 and step == 1:
@@ -1116,7 +1114,6 @@
         else:
             part = shape_of(whole.shape[1:], BF16)
             results.update(near_sum=part, got_far=part)
-            results.update(far_late=shape_of(given["near_late"].shape, BF16))
         scratch.update(got_sum=one)
     return call_kernel(
         functools.partial(backward_kernel, attention, feed, riding),
@@ -1434,7 +1431,8 @@
                 riding = 1 if end else 2
                 if end:
                     near_late = line.run(add_low, kept_late, got_late)
-                    given.update(near_late=near_late, whole=next_whole)
+                    far_late = swap(near_late, SEQ, 2)
+                    given.update(whole=next_whole)
                 else:
                     given.update(
                         whole=line.run(add_low, *pending),
@@ -1543,7 +1541,7 @@
             wide_one=above.wide_one,
             out_piece=out_piece,
             near_late=near_late,
-            far_late=found.far_late,
+            far_late=far_late,
             near_prior=found.near_sum,
             far_prior=found.got_far,
         )

time: 767 us -> 773 us (level)
  Pallas kernels: 637 us -> 649 us
    ppermute x11 -> x12, waiting for transfers between devices: 23.2 us -> 22.5 us  [swap(): return lax.ppermute(values, axis, [(i, i ^ bit) for i in range(size)])]
  transfers between devices with their start and end apart: 11 -> 12, of which waited for: 4 -> 2; matrix products, arithmetic and copies ran while one was open for 2% -> 2% of each run, Pallas kernels for 27% -> 28%
where the time goes in v5:
time: 773 us; the launch traced here: 763 us
  Pallas kernels  649 us (84%)
  other arithmetic  35.8 us (5%)
  local copies, waits for them, and re-layouts  23.4 us (3%)
  waiting for transfers between devices  22.5 us (3%)
  matrix products  19.2 us (2%)
  starting transfers between devices  10.4 us (1%)
    pallas_call x7, Pallas kernels, call_kernel(): pl.pallas_call(kernel, out_shape=tuple(flat[2][0] + flat[3][0]), in_specs...  556 us
    pallas_call x4, Pallas kernels, attend_back(): pl.pallas_call(functools.partial(attend_back_kernel, first_chunk, len(pai...  53.7 us
    pallas_call x4, Pallas kernels, attend(): pl.pallas_call(functools.partial(attend_kernel, first_chunk, len(pairs),...  38.7 us
    ppermute x12, waiting for transfers between devices, swap(): return lax.ppermute(values, axis, [(i, i ^ bit) for i in range(size)])  22.5 us
    dot_general x12, matrix products, contract(): lax.dot_general(left, right, (((left_dim,), (right_dim,)), ((), ())), pre...  19.2 us
  transfers between devices with their start and end apart: 12, of which 2 were waited for; matrix products, arithmetic and copies ran while one was open for 2% of the time, Pallas kernels for 28%

profile of v5, /device:TPU:0, one launch (start us, length us, event | category | flops | bytes accessed | tf_op | source)
XLA Modules:
  0.0 762.9 jit_solution(10685840621321453044)
XLA Ops:
  4.2 38.6 %shard_map.238 = (bf16[2,5,56,512]{3,2,1,0:T(8,128)(2,1)}, f32[256,1]{1,0:T(8,128)}, f32[256,1]{1,0:T(8,128)}, bf16[256,1120]{1,0:T(8,128)(2,1)}, bf16[256,1120]...) custom-call(f32[1,1120]{1,0:T(1,128)} %get-tuple-element.748.refs_0_, ...), custom_call_target="tpu_custom_call" | custom-call | flops 1048576 | bytes 1048576 | tf_op jit(solution)/shard_map/pallas_call | solution.py:393
  46.4 13.5 %shard_map.239 = (f32[5,1,512]{2,1,0:T(1,128)}, f32[5,1,512]{2,1,0:T(1,128)}, f32[5,56,512]{2,1,0:T(8,128)}, f32[5,1,512]{2,1,0:T(1,128)}, f32[5,1,512]{2,1,0:T(1,128)}, /*index=5*/f32[5,56,512]{2,1,0:T(8,128)}) custom-call(s32[13]{0:T(128)} %pad_add_fusion.info, bf16[5,56,512]{2,1,0:T(8,128)(2,1)} %get-tuple-element.589.refs_0_, ...), custom_call_target="tpu_custom_call" | custom-call | flops 1048576 | bytes 1048576 | tf_op jit(solution)/shard_map/pallas_call | solution.py:266
  61.3 5.9 shard_map.240
  67.2 68.1 %shard_map.241 = (bf16[1120,256]{1,0:T(8,128)(2,1)}, bf16[2,5,56,512]{3,2,1,0:T(8,128)(2,1)}, bf16[512,1120]{1,0:T(8,128)(2,1)}, bf16[512,1120]{1,0:T(8,128)(2,1...) custom-call(f32[256,1120]{1,0:T(8,128)} %get-tuple-element.367.refs_, ...), custom_call_target="tpu_custom_call" | custom-call | flops 1048576 | bytes 1048576 | tf_op jit(solution)/shard_map/pallas_call | solution.py:393
  138.4 13.5 %shard_map.242 = (f32[5,1,512]{2,1,0:T(1,128)}, f32[5,1,512]{2,1,0:T(1,128)}, f32[5,56,512]{2,1,0:T(8,128)}, f32[5,1,512]{2,1,0:T(1,128)}, f32[5,1,512]{2,1,0:T(1,128)}, /*index=5*/f32[5,56,512]{2,1,0:T(8,128)}) custom-call(s32[13]{0:T(128)} %pad_add_fusion.info, bf16[5,56,512]{2,1,0:T(8,128)(2,1)} %get-tuple-element.495.refs_0_, ...), custom_call_target="tpu_custom_call" | custom-call | flops 1048576 | bytes 1048576 | tf_op jit(solution)/shard_map/pallas_call | solution.py:266
  152.7 5.8 shard_map.243
  158.5 60.3 %shard_map.244 = (bf16[1120,256]{1,0:T(8,128)(2,1)}, bf16[1120,256]{1,0:T(8,128)(2,1)}, bf16[512,1120]{1,0:T(8,128)(2,1)}, bf16[512,1120]{1,0:T(8,128)(2,1)}, f3...) custom-call(f32[256,1120]{1,0:T(8,128)} %get-tuple-element.409.refs_, ...), custom_call_target="tpu_custom_call" | custom-call | flops 1048576 | bytes 1048576 | tf_op jit(solution)/shard_map/pallas_call | solution.py:393
  218.9 44.6 %shard_map.245 = (f32[8,1120]{1,0:T(8,128)}, bf16[2,1120,512]{2,1,0:T(8,128)(2,1)}, f32[256,1120]{1,0:T(8,128)}, f32[256,1120]{1,0:T(8,128)}, bf16[5,56,512]{2,1...) custom-call(bf16[1120,256]{1,0:T(8,128)(2,1)} %get-tuple-element.427, ...), custom_call_target="tpu_custom_call" | custom-call | flops 1048576 | bytes 1048576 | tf_op jit(solution)/shard_map/pallas_call | solution.py:393
  263.5 3.1 fusion.17
  266.7 1.8 fusion
  270.1 1.7 fusion.18
  271.8 1.8 fusion.1
  277.4 1.9 broadcast_select_fusion.4
  282.5 12.0 %shard_map.246 = (f32[5,56,512]{2,1,0:T(8,128)}, f32[5,56,512]{2,1,0:T(8,128)}, bf16[2,5,56,512]{3,2,1,0:T(8,128)(2,1)}, bf16[2,5,56,512]{3,2,1,0:T(8,128)(2,1)}) custom-call(s32[13]{0:T(128)} %pad_add_fusion.info, bf16[5,56,512]{2,1,0:T(8,128)(2,1)} %get-tuple-element.495.refs_0_, bf16[5,56,512]{2,1,0:T(8,128)(2,1)} %get-tuple-element.496.refs_1_, ...), custom_call_target="tpu_custom_call" | custom-call | flops 1048576 | bytes 1048576 | tf_op jit(solution)/shard_map/pallas_call | solution.py:284
  296.5 14.9 %shard_map.247 = (f32[5,56,512]{2,1,0:T(8,128)}, f32[5,56,512]{2,1,0:T(8,128)}, f32[2,5,56,512]{3,2,1,0:T(8,128)}, f32[2,5,56,512]{3,2,1,0:T(8,128)}) custom-call(s32[13]{0:T(128)} %pad_add_fusion.info, bf16[5,56,512]{2,1,0:T(8,128)(2,1)} %get-tuple-element.495.refs_0_, bf16[5,56,512]{2,1,0:T(8,128)(2,1)} %get-tuple-element.496.refs_1_, ...), custom_call_target="tpu_custom_call" | custom-call | flops 1048576 | bytes 1048576 | tf_op jit(solution)/shard_map/pallas_call | solution.py:284
  311.4 2.7 add_convert_fusion.refs_20_
  314.1 7.9 %collective-permute-done.4.refs_13_ = bf16[2,5,56,512]{3,2,1,0:T(8,128)(2,1)} collective-permute-done((bf16[2,5,56,512]{3,2,1,0:T(8,128)(2,1)}, bf16[2,5,56,512]{3,2,1,0:T(8,128)(2,1)}, u32[]{:S(2)}, u32[]{:S(2)}) %collective-permute-start.4) | collective-permute-done | bytes 573472 | tf_op jit(solution)/shard_map/ppermute | solution.py:26
  322.0 70.7 %shard_map.248 = (bf16[2,288,1120]{2,1,0:T(8,128)(2,1)}, f32[8,1120]{1,0:T(8,128)}, bf16[2,280,1120]{2,1,0:T(8,128)(2,1)}, f32[256,1120]{1,0:T(8,128)}, f32[256,...) custom-call(f32[2,1120]{1,0:T(2,128)} %pad_maximum_fusion.13.refs_0_, ...), custom_call_target="tpu_custom_call" | custom-call | flops 1048576 | bytes 1048576 | tf_op jit(solution)/shard_map/pallas_call | solution.py:393
  392.8 1.7 add_convert_fusion.1
  396.5 1.8 fusion.2
  399.9 1.7 fusion.21
  401.6 1.8 fusion.3
  403.7 2.9 broadcast_select_fusion
  413.3 12.0 %shard_map.249 = (f32[5,56,512]{2,1,0:T(8,128)}, f32[5,56,512]{2,1,0:T(8,128)}, bf16[2,5,56,512]{3,2,1,0:T(8,128)(2,1)}, bf16[2,5,56,512]{3,2,1,0:T(8,128)(2,1)}) custom-call(s32[13]{0:T(128)} %pad_add_fusion.info, bf16[5,56,512]{2,1,0:T(8,128)(2,1)} %get-tuple-element.589.refs_0_, bf16[5,56,512]{2,1,0:T(8,128)(2,1)} %get-tuple-element.590.refs_1_, ...), custom_call_target="tpu_custom_call" | custom-call | flops 1048576 | bytes 1048576 | tf_op jit(solution)/shard_map/pallas_call | solution.py:284
  427.2 14.9 %shard_map.250 = (f32[5,56,512]{2,1,0:T(8,128)}, f32[5,56,512]{2,1,0:T(8,128)}, f32[2,5,56,512]{3,2,1,0:T(8,128)}, f32[2,5,56,512]{3,2,1,0:T(8,128)}) custom-call(s32[13]{0:T(128)} %pad_add_fusion.info, bf16[5,56,512]{2,1,0:T(8,128)(2,1)} %get-tuple-element.589.refs_0_, bf16[5,56,512]{2,1,0:T(8,128)(2,1)} %get-tuple-element.590.refs_1_, ...), custom_call_target="tpu_custom_call" | custom-call | flops 1048576 | bytes 1048576 | tf_op jit(solution)/shard_map/pallas_call | solution.py:284
  443.5 14.6 %collective-permute-done.9.refs_8_ = bf16[2,5,56,512]{3,2,1,0:T(8,128)(2,1)} collective-permute-done((bf16[2,5,56,512]{3,2,1,0:T(8,128)(2,1)}, bf16[2,5,56,512]{3,2,1,0:T(8,128)(2,1)}, u32[]{:S(2)}, u32[]{:S(2)}) %collective-permute-start.9) | collective-permute-done | bytes 573472 | tf_op jit(solution)/shard_map/ppermute | solution.py:26
  458.1 60.2 %shard_map.251 = (bf16[280,1120]{1,0:T(8,128)(2,1)}, f32[256,1120]{1,0:T(8,128)}, f32[256,1120]{1,0:T(8,128)}, bf16[1120,256]{1,0:T(8,128)(2,1)}, bf16[1120,256]...) custom-call(f32[2,1120]{1,0:T(2,128)} %get-tuple-element.615.refs_0_, ...), custom_call_target="tpu_custom_call" | custom-call | flops 1048576 | bytes 1048576 | tf_op jit(solution)/shard_map/pallas_call | solution.py:393
  520.6 213.4 %shard_map.252 = (f32[3,8,1120]{2,1,0:T(8,128)}, bf16[2,2,560,1120]{3,2,1,0:T(8,128)(2,1)}, bf16[2,2,280,1120]{3,2,1,0:T(8,128)(2,1)}, bf16[2,2,560,1120]{3,2,1,...) custom-call(bf16[272,1120]{1,0:T(8,128)(2,1)} %copy-done.23, ...), custom_call_target="tpu_custom_call" | custom-call | flops 1048576 | bytes 1048576 | tf_op jit(solution)/shard_map/pallas_call | solution.py:393
  735.2 1.8 slice_bitcast_fusion.1
  745.4 3.7 convert_bitcast_fusion
  749.1 4.7 maximum_convert_fusion
  753.9 4.7 maximum_convert_fusion.1
  (180 shorter events, 50.9 us)
Async XLA Ops:
  4.2 38.7 %copy-start.43 = (s32[6]{0:T(128)S(1)}, s32[6]{0:T(128)}, u32[]{:S(2)}) copy-start(s32[6]{0:T(128)} %constant.55.clone) | copy-start | bytes 76
  4.2 38.9 %copy-start.34 = (s32[2,8]{1,0:T(2,128)S(1)}, s32[2,8]{1,0:T(2,128)}, u32[]{:S(2)}) copy-start(s32[2,8]{1,0:T(2,128)} %param.17) | copy-start | bytes 196
  4.2 39.0 %copy-start.31 = (bf16[2,1120]{1,0:T(2,128)(2,1)S(1)}, bf16[2,1120]{1,0:T(2,128)(2,1)}, u32[]{:S(2)}) copy-start(bf16[2,1120]{1,0:T(2,128)(2,1)} %param.26) | copy-start | bytes 13444
  4.2 39.0 %copy-start.32 = (bf16[2,1120]{1,0:T(2,128)(2,1)S(1)}, bf16[2,1120]{1,0:T(2,128)(2,1)}, u32[]{:S(2)}) copy-start(bf16[2,1120]{1,0:T(2,128)(2,1)} %param.22) | copy-start | bytes 13444
  4.2 39.0 %copy-start.33 = (s32[2]{0:T(128)S(1)}, s32[2]{0:T(128)}, u32[]{:S(2)}) copy-start(s32[2]{0:T(128)} %param.18) | copy-start | bytes 28
  42.8 17.1 %copy-start.30 = (bf16[2,1120]{1,0:T(2,128)(2,1)S(1)}, bf16[2,1120]{1,0:T(2,128)(2,1)}, u32[]{:S(2)}) copy-start(bf16[2,1120]{1,0:T(2,128)(2,1)} %param.24) | copy-start | bytes 13444
  42.8 17.7 %collective-permute-start = (bf16[2,5,56,512]{3,2,1,0:T(8,128)(2,1)}, bf16[2,5,56,512]{3,2,1,0:T(8,128)(2,1)S(1)}, u32[]{:S(2)}, u32[]{:S(2)}) collective-permute-start(bf16[2,5,56,512]{3,2,1,0:T(8,128)(2,1)} %get-tuple-element.600.refs_3_.refs_11_), channel_id=1, source_target_pairs={{0,4},{4,0},{8,12},{12,8},{1,5},{5,1},{9,13},{13,9},{2,6},{6,2},{1... | collective-permute-start | bytes 1720328 | tf_op jit(solution)/shard_map/ppermute | solution.py:26
  67.2 69.9 %copy-start.27 = (f32[1,1120]{1,0:T(1,128)S(1)}, f32[1,1120]{1,0:T(1,128)}, u32[]{:S(2)}) copy-start(f32[1,1120]{1,0:T(1,128)} %get-tuple-element.748.refs_0_) | copy-start | bytes 13444
  135.3 16.5 %collective-permute-start.1 = (bf16[2,5,56,512]{3,2,1,0:T(8,128)(2,1)}, bf16[2,5,56,512]{3,2,1,0:T(8,128)(2,1)S(1)}, u32[]{:S(2)}, u32[]{:S(2)}) collective-permute-start(bf16[2,5,56,512]{3,2,1,0:T(8,128)(2,1)} %get-tuple-element.506.refs_3_.refs_11_), channel_id=1, source_target_pairs={{0,4},{4,0},{8,12},{12,8},{1,5},{5,1},{9,13},{13,9},{2,6},{6,2},{1... | collective-permute-start | bytes 1720328 | tf_op jit(solution)/shard_map/ppermute | solution.py:26
  218.9 44.7 %copy-start.15 = (bf16[512,1120]{1,0:T(8,128)(2,1)S(1)}, bf16[512,1120]{1,0:T(8,128)(2,1)}, u32[]{:S(2)}) copy-start(bf16[512,1120]{1,0:T(8,128)(2,1)} %get-tuple-element.449) | copy-start | bytes 3440644
  263.5 3.1 copy-start.41
  263.5 3.1 copy-start.42
  275.8 35.7 %collective-permute-start.5 = (bf16[2,288,1120]{2,1,0:T(8,128)(2,1)}, bf16[2,288,1120]{2,1,0:T(8,128)(2,1)}, u32[]{:S(2)}, u32[]{:S(2)}) collective-permute-start(bf16[2,288,1120]{2,1,0:T(8,128)(2,1)} %get-tuple-element.694), channel_id=1, source_target_pairs={{0,16},{16,0},{1,17},{17,1},{2,18},{18,2},{3,19},{19,3},{4,20},{20... | collective-permute-start | bytes 3870728 | tf_op jit(solution)/shard_map/ppermute | solution.py:26
  279.2 113.5 %collective-permute-start.2 = (bf16[2,272,1120]{2,1,0:T(8,128)(2,1)}, bf16[2,272,1120]{2,1,0:T(8,128)(2,1)}, u32[]{:S(2)}, u32[]{:S(2)}) collective-permute-start(bf16[2,272,1120]{2,1,0:T(8,128)(2,1)} %get-tuple-element.704), channel_id=1, source_target_pairs={{0,16},{16,0},{1,17},{17,1},{2,18},{18,2},{3,19},{19,3},{4,20},{20... | collective-permute-start | bytes 3655688 | tf_op jit(solution)/shard_map/ppermute | solution.py:26
  294.5 19.6 %collective-permute-start.3 = (bf16[2,5,56,512]{3,2,1,0:T(8,128)(2,1)}, bf16[2,5,56,512]{3,2,1,0:T(8,128)(2,1)S(1)}, u32[]{:S(2)}, u32[]{:S(2)}) collective-permute-start(bf16[2,5,56,512]{3,2,1,0:T(8,128)(2,1)} %get-tuple-element.491), channel_id=1, source_target_pairs={{0,4},{4,0},{8,12},{12,8},{1,5},{5,1},{9,13},{13,9},{2,6},{6,2},{1... | collective-permute-start | bytes 1720328 | tf_op jit(solution)/shard_map/ppermute | solution.py:26
  295.8 26.2 %collective-permute-start.4 = (bf16[2,5,56,512]{3,2,1,0:T(8,128)(2,1)}, bf16[2,5,56,512]{3,2,1,0:T(8,128)(2,1)}, u32[]{:S(2)}, u32[]{:S(2)}) collective-permute-start(bf16[2,5,56,512]{3,2,1,0:T(8,128)(2,1)} %get-tuple-element.492), channel_id=1, source_target_pairs={{0,4},{4,0},{8,12},{12,8},{1,5},{5,1},{9,13},{13,9},{2,6},{6,2},{1... | collective-permute-start | bytes 1720328 | tf_op jit(solution)/shard_map/ppermute | solution.py:26
  314.1 7.9 %copy-start.25 = (bf16[2,5,56,512]{3,2,1,0:T(8,128)(2,1)}, bf16[2,5,56,512]{3,2,1,0:T(8,128)(2,1)S(1)}, u32[]{:S(2)}) copy-start(bf16[2,5,56,512]{3,2,1,0:T(8,128)(2,1)S(1)} %collective-permute-done.3.refs_12_) | copy-start | bytes 1720324
  322.0 70.7 %copy-start.1 = (bf16[2,272,1120]{2,1,0:T(8,128)(2,1)S(1)}, bf16[2,272,1120]{2,1,0:T(8,128)(2,1)}, u32[]{:S(2)}) copy-start(bf16[2,272,1120]{2,1,0:T(8,128)(2,1)} %get-tuple-element.545) | copy-start | bytes 3655684
  406.6 3.9 copy-start.3
  406.6 3.9 copy-start.16
  406.6 113.2 %collective-permute-start.10 = (bf16[2,560,1120]{2,1,0:T(8,128)(2,1)}, bf16[2,560,1120]{2,1,0:T(8,128)(2,1)}, u32[]{:S(2)}, u32[]{:S(2)}) collective-permute-start(bf16[2,560,1120]{2,1,0:T(8,128)(2,1)} %get-tuple-element.692), channel_id=1, source_target_pairs={{0,16},{16,0},{1,17},{17,1},{2,18},{18,2},{3,19},{19,3},{4,20},{20... | collective-permute-start | bytes 7526408 | tf_op jit(solution)/shard_map/ppermute | solution.py:26
  409.2 32.9 %collective-permute-start.6 = (bf16[272,1120]{1,0:T(8,128)(2,1)}, bf16[272,1120]{1,0:T(8,128)(2,1)}, u32[]{:S(2)}, u32[]{:S(2)}) collective-permute-start(bf16[272,1120]{1,0:T(8,128)(2,1)} %get-tuple-element.706), channel_id=1, source_target_pairs={{0,4},{4,0},{8,12},{12,8},{1,5},{5,1},{9,13},{13,9},{2,6},{6,2},{1... | collective-permute-start | bytes 1827848 | tf_op jit(solution)/shard_map/ppermute | solution.py:26
  410.0 109.7 %collective-permute-start.11 = (bf16[2,288,1120]{2,1,0:T(8,128)(2,1)}, bf16[2,288,1120]{2,1,0:T(8,128)(2,1)}, u32[]{:S(2)}, u32[]{:S(2)}) collective-permute-start(bf16[2,288,1120]{2,1,0:T(8,128)(2,1)} %get-tuple-element.656.refs_14_), channel_id=1, source_target_pairs={{0,16},{16,0},{1,17},{17,1},{2,18},{18,2},{3,19},{19,3},{4,20},{20... | collective-permute-start | bytes 3870728 | tf_op jit(solution)/shard_map/ppermute | solution.py:26
  425.2 18.2 %collective-permute-start.8 = (bf16[2,5,56,512]{3,2,1,0:T(8,128)(2,1)}, bf16[2,5,56,512]{3,2,1,0:T(8,128)(2,1)S(1)}, u32[]{:S(2)}, u32[]{:S(2)}) collective-permute-start(bf16[2,5,56,512]{3,2,1,0:T(8,128)(2,1)} %get-tuple-element.609), channel_id=1, source_target_pairs={{0,4},{4,0},{8,12},{12,8},{1,5},{5,1},{9,13},{13,9},{2,6},{6,2},{1... | collective-permute-start | bytes 1720328 | tf_op jit(solution)/shard_map/ppermute | solution.py:26
  426.3 31.7 %collective-permute-start.9 = (bf16[2,5,56,512]{3,2,1,0:T(8,128)(2,1)}, bf16[2,5,56,512]{3,2,1,0:T(8,128)(2,1)}, u32[]{:S(2)}, u32[]{:S(2)}) collective-permute-start(bf16[2,5,56,512]{3,2,1,0:T(8,128)(2,1)} %get-tuple-element.610), channel_id=1, source_target_pairs={{0,4},{4,0},{8,12},{12,8},{1,5},{5,1},{9,13},{13,9},{2,6},{6,2},{1... | collective-permute-start | bytes 1720328 | tf_op jit(solution)/shard_map/ppermute | solution.py:26
  443.4 74.9 %copy-start.7 = (bf16[272,1120]{1,0:T(8,128)(2,1)}, bf16[272,1120]{1,0:T(8,128)(2,1)S(1)}, u32[]{:S(2)}) copy-start(bf16[272,1120]{1,0:T(8,128)(2,1)S(1)} %add_convert_fusion.2.refs_8_) | copy-start | bytes 1827844
  443.4 76.4 %collective-permute-start.7 = (bf16[272,1120]{1,0:T(8,128)(2,1)S(1)}, bf16[272,1120]{1,0:T(8,128)(2,1)S(1)}, u32[]{:S(2)}, u32[]{:S(2)}) collective-permute-start(bf16[272,1120]{1,0:T(8,128)(2,1)S(1)} %add_convert_fusion.2.refs_8_), channel_id=1, source_target_pairs={{0,8},{4,12},{8,0},{12,4},{1,9},{5,13},{9,1},{13,5},{2,10},{6,14},... | collective-permute-start | bytes 1827848 | tf_op jit(solution)/shard_map/ppermute | solution.py:26
  443.5 14.6 %copy-start.24 = (bf16[2,5,56,512]{3,2,1,0:T(8,128)(2,1)}, bf16[2,5,56,512]{3,2,1,0:T(8,128)(2,1)S(1)}, u32[]{:S(2)}) copy-start(bf16[2,5,56,512]{3,2,1,0:T(8,128)(2,1)S(1)} %collective-permute-done.8.refs_7_) | copy-start | bytes 1720324
  458.1 60.3 %copy-start.28 = (f32[8,1120]{1,0:T(8,128)S(1)}, f32[8,1120]{1,0:T(8,128)}, u32[]{:S(2)}) copy-start(f32[8,1120]{1,0:T(8,128)} %get-tuple-element.636) | copy-start | bytes 107524
  458.1 60.3 %copy-start.29 = (f32[8,1120]{1,0:T(8,128)S(1)}, f32[8,1120]{1,0:T(8,128)}, u32[]{:S(2)}) copy-start(f32[8,1120]{1,0:T(8,128)} %get-tuple-element.637) | copy-start | bytes 107524
  738.4 3.1 slice-start
  753.9 4.7 copy-start.10
  (26 other events, 43.1 us)
